TPU v7x, 32 devices: a whole 2x2x4 slice. The times are simulated.
32 devices in a mesh: dp: 8 (over z, y), band: 4 (over x, core).
Axes of the slice: x: 2, y: 2, z: 4, core: 2. Of those that a mesh axis runs over, the one named last changes fastest.
Arguments:
- kept_tokens: bfloat16 [32, 512, 1152], P('dp', 'band'), may hold values from -6 to 6
- kept_index: int32 [32, 512], P('dp', 'band'), may hold values from 0 to 1023, as said below
- resolution: int32 [32], P('dp'), may hold values from 0 to 1, as said below
- labels: int32 [32, 4], P('dp'), may hold values from 0 to 999
- timesteps: int32 [32, 4], P('dp'), may hold values from 0 to 999
- class_table: float32 [1000, 1152], replicated, may hold values from -6 to 6
- cotangent: bfloat16 [32, 1024, 1152], P('dp', 'band')
- mask_token: float32 [1152], replicated, may hold values from -0.6 to 0.6
- w_qkv: float32 [1152, 3456], P('band', 'dp'), may hold values from -0.1875 to 0.1875
- w_proj: float32 [1152, 1152], P('band', 'dp'), may hold values from -0.75 to 0.75
- w_fc1: float32 [1152, 4608], P('band', 'dp'), may hold values from -0.1875 to 0.1875
- w_fc2: float32 [4608, 1152], P('band', 'dp'), may hold values from -0.09375 to 0.09375
- w_ada: float32 [1152, 6912], P('band', 'dp'), may hold values from -0.1875 to 0.1875
- mask_first: float32 [1152], replicated, may hold values from -0.00012207031 to 0.00012207031
- first_qkv: float32 [1152, 3456], P('band', 'dp'), may hold values from -0.00012207031 to 0.00012207031
- first_proj: float32 [1152, 1152], P('band', 'dp'), may hold values from -0.00012207031 to 0.00012207031
- first_fc1: float32 [1152, 4608], P('band', 'dp'), may hold values from -0.00012207031 to 0.00012207031
- first_fc2: float32 [4608, 1152], P('band', 'dp'), may hold values from -0.00012207031 to 0.00012207031
- first_ada: float32 [1152, 6912], P('band', 'dp'), may hold values from -0.00012207031 to 0.00012207031
- mask_second: float32 [1152], replicated, may hold values from 2.0931124e-09 to 8.372449e-09
- second_qkv: float32 [1152, 3456], P('band', 'dp'), may hold values from 2.0931124e-09 to 8.372449e-09
- second_proj: float32 [1152, 1152], P('band', 'dp'), may hold values from 2.0931124e-09 to 8.372449e-09
- second_fc1: float32 [1152, 4608], P('band', 'dp'), may hold values from 2.5117347e-10 to 1.0046939e-09
- second_fc2: float32 [4608, 1152], P('band', 'dp'), may hold values from 2.0931124e-09 to 8.372449e-09
- second_ada: float32 [1152, 6912], P('band', 'dp'), may hold values from 2.0931124e-09 to 8.372449e-09
Outputs:
- block_out: bfloat16 [32, 1024, 1152], P('dp', 'band')
- kept_grad: float32 [32, 512, 1152], P('dp', 'band')
- grad_norm: float32 [], replicated
- new_mask: float32 [1152], replicated
- new_qkv: float32 [1152, 3456], P('band', 'dp')
- new_proj: float32 [1152, 1152], P('band', 'dp')
- new_fc1: float32 [1152, 4608], P('band', 'dp')
- new_fc2: float32 [4608, 1152], P('band', 'dp')
- new_ada: float32 [1152, 6912], P('band', 'dp')
- new_mask_first: float32 [1152], replicated
- new_first_qkv: float32 [1152, 3456], P('band', 'dp')
- new_first_proj: float32 [1152, 1152], P('band', 'dp')
- new_first_fc1: float32 [1152, 4608], P('band', 'dp')
- new_first_fc2: float32 [4608, 1152], P('band', 'dp')
- new_first_ada: float32 [1152, 6912], P('band', 'dp')
- new_mask_second: float32 [1152], replicated
- new_second_qkv: float32 [1152, 3456], P('band', 'dp')
- new_second_proj: float32 [1152, 1152], P('band', 'dp')
- new_second_fc1: float32 [1152, 4608], P('band', 'dp')
- new_second_fc2: float32 [4608, 1152], P('band', 'dp')
- new_second_ada: float32 [1152, 6912], P('band', 'dp')
Inputs may be any that keep to these rules, and one draw needn't show every extreme that they name: Each group of 4 consecutive slots holds at least one slot of resolution 0, which one drawn from the seed. `kept_index`: within a slot the entries are distinct positions; a slot of resolution 1 keeps exactly half of the positions of each of its four regions of 256 positions. `labels`: in a slot of resolution 0 only the first column is read. `timesteps`: in a slot of resolution 0 only the first column is read.
All inputs are finite; a program needn't handle non-finite values.
Results may differ from a plain program's by a relative error of at most 0.023.
Values may be sent and summed in bfloat16 or wider, within the bound.
A program may use at most 384 MiB of HBM per device.

v0:
```python
import math

import jax
import jax.numpy as jnp
from jax import lax
from jax.sharding import PartitionSpec as P

D = 1152
HEADS = 16
HEAD_DIM = 72
SIDE = 32
STEP = 10
REGION = 256


learn_rate = 0.1
beta_first = 0.9
beta_second = 0.95
adam_eps = 1e-08
decay_rate = 0.1
clip_level = 1.0


def time_embed(timestep):
    half_width = D // 2
    frequency = jnp.exp(-math.log(10000.0) * jnp.arange(half_width, dtype=jnp.float32) / half_width)
    angles = timestep.astype(jnp.float32)[..., None] * frequency
    return jnp.concatenate([jnp.cos(angles), jnp.sin(angles)], axis=-1)


def grid_embed(grid_rows, grid_cols):
    quarter = D // 4
    omegas = 1.0 / 10000.0 ** (jnp.arange(quarter, dtype=jnp.float32) / quarter)
    row_angle = grid_rows.astype(jnp.float32)[..., None] * omegas
    col_angle = grid_cols.astype(jnp.float32)[..., None] * omegas
    return jnp.concatenate(
        [jnp.sin(row_angle), jnp.cos(row_angle), jnp.sin(col_angle), jnp.cos(col_angle)], axis=-1
    )


def slot_layout(positions, slot_kinds):
    small_side = SIDE // 2
    region = positions // REGION
    inside = positions % REGION
    grid_rows = jnp.where(slot_kinds == 1, inside // small_side, positions // SIDE)
    grid_cols = jnp.where(slot_kinds == 1, inside % small_side, positions % SIDE)
    image_id = jnp.where(slot_kinds == 1, region, 0)
    return (grid_rows, grid_cols, image_id)


def modulate(values, shifts, scales):
    center = jnp.mean(values, axis=-1, keepdims=True)
    spread = jnp.mean((values - center) ** 2, axis=-1, keepdims=True)
    return (values - center) * lax.rsqrt(spread + 1e-06) * (1.0 + scales) + shifts


def gelu_tanh(values):
    return jax.nn.gelu(values, approximate=True)


def pick_rows(table_rows, picks):
    return table_rows[picks]


def allowed_pairs(query_pos, key_pos, slot_kinds):
    same_region = (query_pos // REGION)[None, :, None] == (key_pos // REGION)[None, None, :]
    return (slot_kinds[:, None, None] == 0) | same_region


def attend(queries, keys_in, values_in, allowed):

    def one_slot(pieces):
        query_s, key_s, value_s, allow_s = pieces
        scores = jnp.einsum(
            "qhd,khd->hqk", query_s, key_s, preferred_element_type=jnp.float32
        ) * HEAD_DIM ** (-0.5)
        scores = jnp.where(allow_s[None], scores, -1e30)
        row_peak = jnp.max(scores, axis=-1, keepdims=True)
        row_total = jnp.sum(jnp.exp(scores - row_peak), axis=-1, keepdims=True)
        log_total = row_peak + jnp.log(row_total)
        weights_soft = jnp.exp(scores - log_total).astype(jnp.bfloat16)
        result = jnp.einsum(
            "hqk,khd->qhd", weights_soft, value_s, preferred_element_type=jnp.float32
        )
        return (result.astype(jnp.bfloat16), log_total)

    return lax.map(one_slot, (queries, keys_in, values_in, allowed))


def attend_back(queries, keys_in, values_in, allowed, log_total, grad_attended):

    def one_slot(pieces):
        query_s, key_s, value_s, allow_s, total_s, grad_s = pieces
        scores = jnp.einsum(
            "qhd,khd->hqk", query_s, key_s, preferred_element_type=jnp.float32
        ) * HEAD_DIM ** (-0.5)
        scores = jnp.where(allow_s[None], scores, -1e30)
        weights_full = jnp.exp(scores - total_s)
        weights_soft = weights_full.astype(jnp.bfloat16)
        grad_weights = jnp.einsum(
            "qhd,khd->hqk", grad_s, value_s, preferred_element_type=jnp.float32
        )
        row_dot = jnp.sum(weights_full * grad_weights, axis=-1, keepdims=True)
        grad_scores = (weights_full * (grad_weights - row_dot) * HEAD_DIM ** (-0.5)).astype(
            jnp.bfloat16
        )
        grad_queries = jnp.einsum(
            "hqk,khd->qhd", grad_scores, key_s, preferred_element_type=jnp.float32
        )
        grad_keys = jnp.einsum(
            "hqk,qhd->khd", grad_scores, query_s, preferred_element_type=jnp.float32
        )
        grad_values = jnp.einsum(
            "hqk,qhd->khd", weights_soft, grad_s, preferred_element_type=jnp.float32
        )
        return (grad_queries, grad_keys, grad_values)

    return lax.map(one_slot, (queries, keys_in, values_in, allowed, log_total, grad_attended))


def adamw(weight, first, second, grad):
    first_new = beta_first * first + (1.0 - beta_first) * grad
    second_new = beta_second * second + (1.0 - beta_second) * grad * grad
    first_hat = first_new / (1.0 - beta_first**STEP)
    second_hat = second_new / (1.0 - beta_second**STEP)
    weight_new = weight - learn_rate * (
        first_hat / (jnp.sqrt(second_hat) + adam_eps) + decay_rate * weight
    )
    return (weight_new, first_new, second_new)


def per_device(
    kept_tokens,
    kept_index,
    resolution,
    labels,
    timesteps,
    class_table,
    cotangent,
    mask_token,
    w_qkv,
    w_proj,
    w_fc1,
    w_fc2,
    w_ada,
    mask_first,
    first_qkv,
    first_proj,
    first_fc1,
    first_fc2,
    first_ada,
    mask_second,
    second_qkv,
    second_proj,
    second_fc1,
    second_fc2,
    second_ada,
):
    highest = lax.Precision.HIGHEST
    band_index = lax.axis_index("band")
    slot_count = cotangent.shape[0]
    local_rows = cotangent.shape[1]
    qkv_low = w_qkv.astype(jnp.bfloat16)
    proj_low = w_proj.astype(jnp.bfloat16)
    fc1_low = w_fc1.astype(jnp.bfloat16)
    fc2_low = w_fc2.astype(jnp.bfloat16)
    ada_low = w_ada.astype(jnp.bfloat16)
    cols_qkv, cols_proj, cols_fc1, cols_fc2, cols_ada = (
        lax.all_gather(qkv_low, "dp", axis=1, tiled=True),
        lax.all_gather(proj_low, "dp", axis=1, tiled=True),
        lax.all_gather(fc1_low, "dp", axis=1, tiled=True),
        lax.all_gather(fc2_low, "dp", axis=1, tiled=True),
        lax.all_gather(ada_low, "dp", axis=1, tiled=True),
    )
    condition = jnp.take(class_table, labels, axis=0) + time_embed(timesteps)
    cond_low = jax.nn.silu(condition).astype(jnp.bfloat16)
    qkv_full, proj_full, fc1_full, fc2_full, ada_full = (
        lax.all_gather(cols_qkv, "band", axis=0, tiled=True),
        lax.all_gather(cols_proj, "band", axis=0, tiled=True),
        lax.all_gather(cols_fc1, "band", axis=0, tiled=True),
        lax.all_gather(cols_fc2, "band", axis=0, tiled=True),
        lax.all_gather(cols_ada, "band", axis=0, tiled=True),
    )
    modulation = jnp.einsum("sid,de->sie", cond_low, ada_full, preferred_element_type=jnp.float32)
    kept_all, index_all = (
        lax.all_gather(kept_tokens, "band", axis=1, tiled=True),
        lax.all_gather(kept_index, "band", axis=1, tiled=True),
    )
    positions = band_index * local_rows + jnp.arange(local_rows)
    select = index_all[:, None, :] == positions[None, :, None]
    placed = jnp.einsum(
        "spj,sjd->spd", select.astype(jnp.bfloat16), kept_all, preferred_element_type=jnp.float32
    )
    unfilled = 1.0 - jnp.sum(select.astype(jnp.float32), axis=2)
    grid_rows, grid_cols, image_id = slot_layout(positions[None, :], resolution[:, None])
    tokens = placed + unfilled[..., None] * mask_token + grid_embed(grid_rows, grid_cols)
    token_mod = jax.vmap(pick_rows)(modulation, image_id)
    shift_attn, scale_attn, gate_attn, shift_mlp, scale_mlp, gate_mlp = jnp.split(
        token_mod, 6, axis=-1
    )
    attn_value, attn_pull = jax.vjp(modulate, tokens, shift_attn, scale_attn)
    hidden = attn_value.astype(jnp.bfloat16)
    qkv = jnp.einsum("std,de->ste", hidden, qkv_full, preferred_element_type=jnp.float32).astype(
        jnp.bfloat16
    )
    queries = qkv[..., :D].reshape(slot_count, local_rows, HEADS, HEAD_DIM)
    keys_in = qkv[..., D : 2 * D].reshape(slot_count, local_rows, HEADS, HEAD_DIM)
    values_in = qkv[..., 2 * D :].reshape(slot_count, local_rows, HEADS, HEAD_DIM)
    keys_all, values_all = (
        lax.all_gather(keys_in, "band", axis=1, tiled=True),
        lax.all_gather(values_in, "band", axis=1, tiled=True),
    )
    allowed = allowed_pairs(positions, jnp.arange(keys_all.shape[1]), resolution)
    attended, log_total = attend(queries, keys_all, values_all, allowed)
    attended_flat = attended.reshape(slot_count, local_rows, D)
    branch = jnp.einsum("std,de->ste", attended_flat, proj_full, preferred_element_type=jnp.float32)
    middle = tokens + gate_attn * branch
    mlp_value, mlp_pull = jax.vjp(modulate, middle, shift_mlp, scale_mlp)
    hidden_mlp = mlp_value.astype(jnp.bfloat16)
    upward = jnp.einsum("std,df->stf", hidden_mlp, fc1_full, preferred_element_type=jnp.float32)
    active_value, gelu_pull = jax.vjp(gelu_tanh, upward)
    active = active_value.astype(jnp.bfloat16)
    output = jnp.einsum("stf,fd->std", active, fc2_full, preferred_element_type=jnp.float32)
    block_out = (middle + gate_mlp * output).astype(jnp.bfloat16)
    grad_out = cotangent.astype(jnp.float32)
    grad_gate_mlp = grad_out * output
    grad_output = (gate_mlp * grad_out).astype(jnp.bfloat16)
    grad_fc2 = jnp.einsum("stf,std->fd", active, grad_output, preferred_element_type=jnp.float32)
    grad_active = jnp.einsum(
        "std,fd->stf", grad_output, fc2_full, preferred_element_type=jnp.float32
    )
    grad_upward = gelu_pull(grad_active)[0].astype(jnp.bfloat16)
    grad_fc1 = jnp.einsum(
        "std,stf->df", hidden_mlp, grad_upward, preferred_element_type=jnp.float32
    )
    grad_hidden_mlp = jnp.einsum(
        "stf,df->std", grad_upward, fc1_full, preferred_element_type=jnp.float32
    )
    grad_mid_norm, grad_shift_mlp, grad_scale_mlp = mlp_pull(grad_hidden_mlp)
    grad_middle = grad_out + grad_mid_norm
    grad_gate_attn = grad_middle * branch
    grad_branch = (gate_attn * grad_middle).astype(jnp.bfloat16)
    grad_proj = jnp.einsum(
        "std,ste->de", attended_flat, grad_branch, preferred_element_type=jnp.float32
    )
    grad_attended = jnp.einsum(
        "ste,de->std", grad_branch, proj_full, preferred_element_type=jnp.float32
    ).astype(jnp.bfloat16)
    grad_attended = grad_attended.reshape(slot_count, local_rows, HEADS, HEAD_DIM)
    grad_queries, grad_keys_part, grad_values_part = attend_back(
        queries, keys_all, values_all, allowed, log_total, grad_attended
    )
    grad_keys, grad_values = (
        lax.psum_scatter(
            grad_keys_part.astype(jnp.bfloat16), "band", scatter_dimension=1, tiled=True
        ).astype(jnp.float32),
        lax.psum_scatter(
            grad_values_part.astype(jnp.bfloat16), "band", scatter_dimension=1, tiled=True
        ).astype(jnp.float32),
    )
    grad_qkv = jnp.concatenate(
        [
            grad_queries.reshape(slot_count, local_rows, D),
            grad_keys.reshape(slot_count, local_rows, D),
            grad_values.reshape(slot_count, local_rows, D),
        ],
        axis=-1,
    ).astype(jnp.bfloat16)
    grad_qkv_weight = jnp.einsum(
        "std,ste->de", hidden, grad_qkv, preferred_element_type=jnp.float32
    )
    grad_hidden = jnp.einsum("ste,de->std", grad_qkv, qkv_full, preferred_element_type=jnp.float32)
    grad_tok_norm, grad_shift_attn, grad_scale_attn = attn_pull(grad_hidden)
    grad_tokens = grad_middle + grad_tok_norm
    grad_mod_tok = jnp.concatenate(
        [
            grad_shift_attn,
            grad_scale_attn,
            grad_gate_attn,
            grad_shift_mlp,
            grad_scale_mlp,
            grad_gate_mlp,
        ],
        axis=-1,
    )
    image_onehot = (image_id[..., None] == jnp.arange(4)).astype(jnp.float32)
    grad_modulation = jnp.einsum("spi,spe->sie", image_onehot, grad_mod_tok, precision=highest)
    grad_mask_part = jnp.sum(unfilled[..., None] * grad_tokens, axis=(0, 1))
    grad_kept_all = jnp.einsum(
        "spj,spd->sjd", select.astype(jnp.float32), grad_tokens, precision=highest
    )
    kept_grad = lax.psum_scatter(
        grad_kept_all.astype(jnp.bfloat16), "band", scatter_dimension=1, tiled=True
    ).astype(jnp.float32)
    grad_ada = jnp.einsum(
        "sid,sie->de", cond_low.astype(jnp.float32), grad_modulation, precision=highest
    )
    row_grads = (
        lax.psum_scatter(
            grad_qkv_weight.astype(jnp.bfloat16), "band", scatter_dimension=0, tiled=True
        ).astype(jnp.float32),
        lax.psum_scatter(
            grad_proj.astype(jnp.bfloat16), "band", scatter_dimension=0, tiled=True
        ).astype(jnp.float32),
        lax.psum_scatter(
            grad_fc1.astype(jnp.bfloat16), "band", scatter_dimension=0, tiled=True
        ).astype(jnp.float32),
        lax.psum_scatter(
            grad_fc2.astype(jnp.bfloat16), "band", scatter_dimension=0, tiled=True
        ).astype(jnp.float32),
        lax.psum_scatter(
            grad_ada.astype(jnp.bfloat16), "band", scatter_dimension=0, tiled=True
        ).astype(jnp.float32),
    )
    red_qkv, red_proj, red_fc1, red_fc2, red_ada = (
        lax.psum_scatter(
            row_grads[0].astype(jnp.bfloat16), "dp", scatter_dimension=1, tiled=True
        ).astype(jnp.float32),
        lax.psum_scatter(
            row_grads[1].astype(jnp.bfloat16), "dp", scatter_dimension=1, tiled=True
        ).astype(jnp.float32),
        lax.psum_scatter(
            row_grads[2].astype(jnp.bfloat16), "dp", scatter_dimension=1, tiled=True
        ).astype(jnp.float32),
        lax.psum_scatter(
            row_grads[3].astype(jnp.bfloat16), "dp", scatter_dimension=1, tiled=True
        ).astype(jnp.float32),
        lax.psum_scatter(
            row_grads[4].astype(jnp.bfloat16), "dp", scatter_dimension=1, tiled=True
        ).astype(jnp.float32),
    )
    grad_mask = lax.psum(grad_mask_part, ("dp", "band"))
    reduced = (red_qkv, red_proj, red_fc1, red_fc2, red_ada)
    local_squares = sum((jnp.sum(grad * grad) for grad in reduced))
    total_squares = lax.psum(local_squares, ("dp", "band")) + jnp.sum(grad_mask * grad_mask)
    norm_value = jnp.sqrt(total_squares)
    factor = clip_level / jnp.maximum(norm_value, clip_level)
    mask_new = adamw(mask_token, mask_first, mask_second, grad_mask * factor)
    qkv_new = adamw(w_qkv, first_qkv, second_qkv, red_qkv * factor)
    proj_new = adamw(w_proj, first_proj, second_proj, red_proj * factor)
    fc1_new = adamw(w_fc1, first_fc1, second_fc1, red_fc1 * factor)
    fc2_new = adamw(w_fc2, first_fc2, second_fc2, red_fc2 * factor)
    ada_new = adamw(w_ada, first_ada, second_ada, red_ada * factor)
    return (
        block_out,
        kept_grad,
        norm_value,
        mask_new[0],
        qkv_new[0],
        proj_new[0],
        fc1_new[0],
        fc2_new[0],
        ada_new[0],
        mask_new[1],
        qkv_new[1],
        proj_new[1],
        fc1_new[1],
        fc2_new[1],
        ada_new[1],
        mask_new[2],
        qkv_new[2],
        proj_new[2],
        fc1_new[2],
        fc2_new[2],
        ada_new[2],
    )


def solution(mesh):
    in_specs = (
        P("dp", "band", None),
        P("dp", "band"),
        P("dp"),
        P("dp", None),
        P("dp", None),
        P(),
        P("dp", "band", None),
        P(),
        P("band", "dp"),
        P("band", "dp"),
        P("band", "dp"),
        P("band", "dp"),
        P("band", "dp"),
        P(),
        P("band", "dp"),
        P("band", "dp"),
        P("band", "dp"),
        P("band", "dp"),
        P("band", "dp"),
        P(),
        P("band", "dp"),
        P("band", "dp"),
        P("band", "dp"),
        P("band", "dp"),
        P("band", "dp"),
    )
    out_specs = (
        P("dp", "band", None),
        P("dp", "band", None),
        P(),
        P(),
        P("band", "dp"),
        P("band", "dp"),
        P("band", "dp"),
        P("band", "dp"),
        P("band", "dp"),
        P(),
        P("band", "dp"),
        P("band", "dp"),
        P("band", "dp"),
        P("band", "dp"),
        P("band", "dp"),
        P(),
        P("band", "dp"),
        P("band", "dp"),
        P("band", "dp"),
        P("band", "dp"),
        P("band", "dp"),
    )
    return jax.shard_map(
        per_device, mesh=mesh, in_specs=in_specs, out_specs=out_specs, check_vma=False
    )
```

profile of v0, /device:TPU:0, one launch (start us, length us, event | category | flops | bytes accessed | tf_op | source)
XLA Modules:
  0.0 2241.5 jit_solution(15069754811021875631)
XLA Ops:
  12.0 74.1 %all-gather.34.cloned.1.call-done = bf16[8,864,288]{1,2,0:T(8,128)(2,1)} async-done(((bf16[1,864,288]{1,2,0:T(8,128)(2,1)}), bf16[8,864,288]{1,2,0:T(8,128)(2,1)}) %all-gather.34.cloned.1.call-update) | async-done | bytes 3981328 | tf_op jit(solution)/shard_map/all_gather | solution.py:173
  99.5 39.7 %all-gather.36.cloned.1.call-done = bf16[8,432,288]{1,2,0:T(8,128)(2,1)} async-done(((bf16[1,432,288]{1,2,0:T(8,128)(2,1)}), bf16[8,432,288]{1,2,0:T(8,128)(2,1)}) %all-gather.36.cloned.1.call-update) | async-done | bytes 1990672 | tf_op jit(solution)/shard_map/all_gather | solution.py:169
  189.2 90.2 %all-gather.18.cloned.1.call-done = bf16[1152,6912]{1,0:T(8,128)(2,1)} async-done(((bf16[288,6912]{1,0:T(8,128)(2,1)}), bf16[1152,6912]{1,0:T(8,128)(2,1)}) %all-gather.18.cloned.1.call-update) | async-done | bytes 15925264 | tf_op jit(solution)/shard_map/all_gather | solution.py:182
  287.3 56.0 %gather_fusion.1 = f32[1024,6912]{1,0:T(8,128)} fusion(f32[4,4,6912]{2,1,0:T(4,128)S(1)} %fusion.82, s32[1024]{0:T(1024)S(1)} %bitcast.232), kind=kCustom, calls=%fused_computation.1 | custom fusion | bytes 56631296 | tf_op jit(solution)/shard_map/vmap()/gather | solution.py:62
  373.0 35.3 %all_gather.50 = bf16[288,1152]{0,1:T(8,128)(2,1)S(1)} all-gather(bf16[288,144]{0,1:T(8,128)(2,1)S(1)} %convert_element_type.151), channel_id=1, replica_groups=mesh['dp'=8,'band'=4] {'dp'}, dimensions={1}, use_global_device_ids=true | all-gather | bytes 746496 | tf_op jit(solution)/shard_map/all_gather | solution.py:170
  420.5 50.2 %all-gather.30.cloned.1.call-done = bf16[1152,1152]{0,1:T(8,128)(2,1)} async-done(((bf16[1152,144]{0,1:T(8,128)(2,1)}), bf16[1152,1152]{0,1:T(8,128)(2,1)}) %all-gather.30.cloned.1.call-update) | async-done | bytes 2654224 | tf_op jit(solution)/shard_map/all_gather | solution.py:172
  479.3 57.0 %all-gather.24.cloned.1.call-done = bf16[4,1024,16,72]{1,3,2,0:T(8,128)(2,1)} async-done(((bf16[4,256,16,72]{1,3,2,0:T(8,128)(2,1)}), bf16[4,1024,16,72]{1,3,2,0:T(8,128)(2,1)}) %all-gather.24.cloned.1.call-update) | async-done | bytes 9437200 | tf_op jit(solution)/shard_map/all_gather | solution.py:210
  536.4 67.1 %all-gather.22.cloned.1.call-done = bf16[4,1024,16,72]{1,3,2,0:T(8,128)(2,1)} async-done(((bf16[4,256,16,72]{1,3,2,0:T(8,128)(2,1)}), bf16[4,1024,16,72]{1,3,2,0:T(8,128)(2,1)}) %all-gather.22.cloned.1.call-update) | async-done | bytes 9437200 | tf_op jit(solution)/shard_map/all_gather | solution.py:211
  603.5 64.5 %while.26 = (s32[]{:T(128)}, bf16[4,256,16,72]{1,3,2,0:T(8,128)(2,1)}, f32[4,16,256,1]{2,1,3,0:T(8,128)S(1)}, bf16[4,1024,16,72]{1,3,2,0:T(8,128)(2,1)}, pred[4,...) while((s32[]{:T(128)}, ...), condition=%wide.region_6.7_spmd, body=%wide.region_3.6_spmd.sunk | while | flops 1254387712 | bytes 57673828 | solution.py:87
  722.8 53.4 %all-gather.32.cloned.1.call-done = bf16[4608,1152]{1,0:T(8,128)(2,1)} async-done(((bf16[1152,1152]{1,0:T(8,128)(2,1)}), bf16[4608,1152]{1,0:T(8,128)(2,1)}) %all-gather.32.cloned.1.call-update) | async-done | bytes 10616848 | tf_op jit(solution)/shard_map/all_gather | solution.py:181
  776.2 29.5 %fusion.81 = bf16[4,256,4608]{2,1,0:T(8,128)(2,1)} fusion(f32[4,256,4608]{2,1,0:T(8,128)} %fusion.93, bf16[4608,1152]{1,0:T(8,128)(2,1)} %all-gather.32.cloned.1.call-done, bf16[4,256,1152]{2,1,0:T(8,128)(2,1)} %param.35, f32[4,256,6912]{2,1,0:T(8,128)} %bitcast.224), kind=kOutput, calls=%fused_computation.77 | convolution fusion | flops 10969546752 | bytes 46006272 | tf_op jit(solution)/shard_map/std,fd->stf/dot_general | solution.py:229
  869.4 277.8 %while.27 = (s32[]{:T(128)}, bf16[4,256,16,72]{1,3,2,0:T(8,128)(2,1)}, bf16[4,1024,16,72]{1,3,2,0:T(8,128)(2,1)}, bf16[4,1024,16,72]{1,3,2,0:T(8,128)(2,1)}, bf1...) while((s32[]{:T(128)}, ...), condition=%wide.region_14.15_spmd, body=%wide.region_12.14_spmd.sunk | while | flops 3078629376 | bytes 272553120 | solution.py:118
  1230.3 76.5 %reduce-scatter.24.cloned.1.call-done = bf16[4,256,16,72]{1,3,2,0:T(8,128)(2,1)} async-done(((bf16[4,1024,16,72]{1,3,2,0:T(8,128)(2,1)}), bf16[4,256,16,72]{1,3,2,0:T(8,128)(2,1)}) %reduce-scatter.24.cloned.1.call-update) | async-done | bytes 2359312 | tf_op jit(solution)/shard_map/reduce_scatter | solution.py:254
  1400.6 32.3 %reduce-scatter.34.cloned.1.call-done = bf16[288,4608]{1,0:T(8,128)(2,1)} async-done(((bf16[1152,4608]{1,0:T(8,128)(2,1)}), bf16[288,4608]{1,0:T(8,128)(2,1)}) %reduce-scatter.34.cloned.1.call-update) | async-done | bytes 2654224 | tf_op jit(solution)/shard_map/reduce_scatter | solution.py:305
  1437.7 84.0 %reduce-scatter.36.cloned.1.call-done = bf16[1152,1152]{1,0:T(8,128)(2,1)} async-done(((bf16[4608,1152]{1,0:T(8,128)(2,1)}), bf16[1152,1152]{1,0:T(8,128)(2,1)}) %reduce-scatter.36.cloned.1.call-update) | async-done | bytes 2654224 | tf_op jit(solution)/shard_map/reduce_scatter | solution.py:308
  1543.2 50.4 %reduce-scatter.30.cloned.1.call-done = bf16[288,3456]{1,0:T(8,128)(2,1)} async-done(((bf16[1152,3456]{1,0:T(8,128)(2,1)}), bf16[288,3456]{1,0:T(8,128)(2,1)}) %reduce-scatter.30.cloned.1.call-update) | async-done | bytes 1990672 | tf_op jit(solution)/shard_map/reduce_scatter | solution.py:299
  1597.9 119.5 %reduce-scatter.38.cloned.1.call-done = bf16[288,6912]{1,0:T(8,128)(2,1)} async-done(((bf16[1152,6912]{1,0:T(8,128)(2,1)}), bf16[288,6912]{1,0:T(8,128)(2,1)}) %reduce-scatter.38.cloned.1.call-update) | async-done | bytes 3981328 | tf_op jit(solution)/shard_map/reduce_scatter | solution.py:311
  1725.4 57.1 %reduce-scatter.42.cloned.1.call-done = bf16[144,288]{1,0:T(8,128)(2,1)} async-done(((bf16[1152,288]{1,0:T(8,128)(2,1)}), bf16[144,288]{1,0:T(8,128)(2,1)}) %reduce-scatter.42.cloned.1.call-update) | async-done | bytes 82960
  1784.1 80.1 %reduce-scatter.44.cloned.1.call-done = bf16[576,288]{1,0:T(8,128)(2,1)} async-done(((bf16[4608,288]{1,0:T(8,128)(2,1)}), bf16[576,288]{1,0:T(8,128)(2,1)}) %reduce-scatter.44.cloned.1.call-update) | async-done | bytes 331792
  1865.5 72.7 %reduce-scatter.46.cloned.1.call-done = bf16[144,1152]{1,0:T(8,128)(2,1)} async-done(((bf16[1152,1152]{1,0:T(8,128)(2,1)}), bf16[144,1152]{1,0:T(8,128)(2,1)}) %reduce-scatter.46.cloned.1.call-update) | async-done | bytes 331792
  1940.7 47.1 %reduce-scatter.28.cloned.1.call-done = bf16[4,128,1152]{2,1,0:T(8,128)(2,1)} async-done(((bf16[4,512,1152]{2,1,0:T(8,128)(2,1)}), bf16[4,128,1152]{2,1,0:T(8,128)(2,1)}) %reduce-scatter.28.cloned.1.call-update) | async-done | bytes 1179664 | tf_op jit(solution)/shard_map/reduce_scatter | solution.py:292
  1990.7 71.6 %reduce-scatter.40.cloned.1.call-done = bf16[432,288]{1,0:T(8,128)(2,1)} async-done(((bf16[3456,288]{1,0:T(8,128)(2,1)}), bf16[432,288]{1,0:T(8,128)(2,1)}) %reduce-scatter.40.cloned.1.call-update) | async-done | bytes 248848
  2066.8 102.5 %reduce-scatter.48.cloned.1.call-done = bf16[864,288]{1,0:T(8,128)(2,1)} async-done(((bf16[6912,288]{1,0:T(8,128)(2,1)}), bf16[864,288]{1,0:T(8,128)(2,1)}) %reduce-scatter.48.cloned.1.call-update) | async-done | bytes 497680
  2172.2 40.6 %all-reduce = (f32[]{:T(128)}, f32[1152]{0:T(1024)}) all-reduce(f32[]{:T(128)S(6)} %add.356, f32[1152]{0:T(1024)S(1)} %get-tuple-element.279), channel_id=1, replica_groups=mesh['dp'=8,'band'=4] {'dp','band'}, use_global_device_ids=true, to_apply=%region_36.37 | all-reduce | flops 1153 | bytes 9224 | tf_op jit(solution)/shard_map/psum | solution.py:335
  (359 shorter events, 832.9 us)
Async XLA Ops:
  9.3 129.9 %all-gather.36.cloned.1.call-start = ((), (), s32[]{:S(2)}) async-start(), calls=%async_computation.31 | async-start | bytes 2654208 | tf_op jit(solution)/shard_map/all_gather | solution.py:169
  11.2 168.9 %all-gather.16.cloned.1.call-start = ((), (), s32[]{:S(2)}) async-start(), calls=%async_computation.13 | async-start | bytes 5898240 | tf_op jit(solution)/shard_map/all_gather | solution.py:186
  12.0 267.5 %all-gather.18.cloned.1.call-start = ((), (), s32[]{:S(2)}) async-start(), calls=%async_computation.14 | async-start | bytes 19906560 | tf_op jit(solution)/shard_map/all_gather | solution.py:182
  99.5 250.0 %all-gather.20.cloned.1.call-start = ((), (), s32[]{:S(2)}) async-start(), calls=%async_computation.15 | async-start | bytes 9953280 | tf_op jit(solution)/shard_map/all_gather | solution.py:178
  146.3 267.3 %all-gather.38.cloned.1.call-start = ((), (), s32[]{:S(2)}) async-start(), calls=%async_computation.32 | async-start | bytes 3317760 | tf_op jit(solution)/shard_map/all_gather | solution.py:171
  147.1 323.6 %all-gather.30.cloned.1.call-start = ((), (), s32[]{:S(2)}) async-start(), calls=%async_computation.20 | async-start | bytes 2985984 | tf_op jit(solution)/shard_map/all_gather | solution.py:172
  149.2 387.2 %all-gather.24.cloned.1.call-start = ((), (), s32[]{:S(2)}) async-start(), calls=%async_computation.17 | async-start | bytes 11796480 | tf_op jit(solution)/shard_map/all_gather | solution.py:210
  370.3 233.1 %all-gather.22.cloned.1.call-start = ((), (), s32[]{:S(2)}) async-start(), calls=%async_computation.16 | async-start | bytes 11796480 | tf_op jit(solution)/shard_map/all_gather | solution.py:211
  372.9 295.0 %all-gather.26.cloned.1.call-start = ((), (), s32[]{:S(2)}) async-start(), calls=%async_computation.18 | async-start | bytes 3317760 | tf_op jit(solution)/shard_map/all_gather | solution.py:179
  409.5 294.3 %all-gather.28.cloned.1.call-start = ((), (), s32[]{:S(2)}) async-start(), calls=%async_computation.19 | async-start | bytes 13271040 | tf_op jit(solution)/shard_map/all_gather | solution.py:180
  419.6 356.5 %all-gather.32.cloned.1.call-start = ((), (), s32[]{:S(2)}) async-start(), calls=%async_computation.21 | async-start | bytes 13271040 | tf_op jit(solution)/shard_map/all_gather | solution.py:181
  476.0 749.9 %reduce-scatter.26.cloned.1.call-start = ((), (), s32[]{:S(2)}) async-start(), calls=%async_computation.23 | async-start | bytes 11796480 | tf_op jit(solution)/shard_map/reduce_scatter | solution.py:257
  1147.3 159.5 %reduce-scatter.24.cloned.1.call-start = ((), (), s32[]{:S(2)}) async-start(), calls=%async_computation.22 | async-start | bytes 11796480 | tf_op jit(solution)/shard_map/reduce_scatter | solution.py:254
  1147.9 250.3 %reduce-scatter.32.cloned.1.call-start = ((), (), s32[]{:S(2)}) async-start(), calls=%async_computation.26 | async-start | bytes 3317760 | tf_op jit(solution)/shard_map/reduce_scatter | solution.py:302
  1155.2 277.7 %reduce-scatter.34.cloned.1.call-start = ((), (), s32[]{:S(2)}) async-start(), calls=%async_computation.27 | async-start | bytes 13271040 | tf_op jit(solution)/shard_map/reduce_scatter | solution.py:305
  1174.3 347.5 %reduce-scatter.36.cloned.1.call-start = ((), (), s32[]{:S(2)}) async-start(), calls=%async_computation.28 | async-start | bytes 13271040 | tf_op jit(solution)/shard_map/reduce_scatter | solution.py:308
  1199.2 394.3 %reduce-scatter.30.cloned.1.call-start = ((), (), s32[]{:S(2)}) async-start(), calls=%async_computation.25 | async-start | bytes 9953280 | tf_op jit(solution)/shard_map/reduce_scatter | solution.py:299
  1326.0 391.4 %reduce-scatter.38.cloned.1.call-start = ((), (), s32[]{:S(2)}) async-start(), calls=%async_computation.29 | async-start | bytes 19906560 | tf_op jit(solution)/shard_map/reduce_scatter | solution.py:311
  1398.1 384.4 %reduce-scatter.42.cloned.1.call-start = ((), (), s32[]{:S(2)}) async-start(), calls=%async_computation.34 | async-start | bytes 995328
  1400.5 463.7 %reduce-scatter.44.cloned.1.call-start = ((), (), s32[]{:S(2)}) async-start(), calls=%async_computation.35 | async-start | bytes 3981312
  1437.6 500.5 %reduce-scatter.46.cloned.1.call-start = ((), (), s32[]{:S(2)}) async-start(), calls=%async_computation.36 | async-start | bytes 2985984
  1527.0 460.9 %reduce-scatter.28.cloned.1.call-start = ((), (), s32[]{:S(2)}) async-start(), calls=%async_computation.24 | async-start | bytes 5898240 | tf_op jit(solution)/shard_map/reduce_scatter | solution.py:292
  1543.1 519.2 %reduce-scatter.40.cloned.1.call-start = ((), (), s32[]{:S(2)}) async-start(), calls=%async_computation.33 | async-start | bytes 2985984
  1597.8 571.5 %reduce-scatter.48.cloned.1.call-start = ((), (), s32[]{:S(2)}) async-start(), calls=%async_computation.37 | async-start | bytes 5971968
  (66 other events, 2280.0 us)
Sparse Core Ops, SparseCore 0:
  10.8 75.2 all-gather.33
  88.8 50.3 all-gather.35
  140.8 36.0 all-gather.15
  178.3 101.0 all-gather.17
  281.4 55.8 all-gather.19
  339.9 73.5 all-gather.37
  416.3 54.3 all-gather.29
  472.3 64.0 all-gather.23
  537.9 65.4 all-gather.21
  632.8 70.9 all-gather.27
  705.2 70.9 all-gather.31
  1147.4 78.4 reduce-scatter.25
  1228.3 78.4 reduce-scatter.23
  1309.2 34.8 reduce-scatter.31
  1346.7 86.1 reduce-scatter.33
  1435.5 86.1 reduce-scatter.35
  1524.4 69.1 reduce-scatter.29
  1596.3 121.0 reduce-scatter.37
  1721.2 61.1 reduce-scatter.41
  1786.1 78.0 reduce-scatter.43
  1867.9 70.2 reduce-scatter.45
  1940.9 46.9 reduce-scatter.27
  1991.4 70.9 reduce-scatter.39
  2066.3 102.9 reduce-scatter.47
  (1 shorter events, 25.7 us)
where the time goes:
time: 2250 us; the launch traced here: 2240 us
  waiting for transfers between devices  1270 us (56%)
  matrix products  572 us (25%)
  local copies, waits for them, and re-layouts  188 us (8%)
  other arithmetic  108 us (5%)
  blocking collectives  81.1 us (4%)
    unnamed x30, waiting for transfers between devices  386 us
    reduce_scatter x1, waiting for transfers between devices, per_device(): lax.psum_scatter(grad_ada.astype(jnp.bfloat16), 'band', scatter_dimension...  120 us
    dot_general x4, matrix products, one_slot(): jnp.einsum('hqk,qhd->khd', grad_scores, query_s, preferred_element_type=j...  93.3 us
    dot_general x4, matrix products, one_slot(): jnp.einsum('hqk,khd->qhd', grad_scores, key_s, preferred_element_type=jnp...  92.6 us
    all_gather x1, waiting for transfers between devices, per_device(): lax.all_gather(cols_ada, 'band', axis=0, tiled=True)  90.2 us
    reduce_scatter x1, waiting for transfers between devices, per_device(): lax.psum_scatter(grad_fc2.astype(jnp.bfloat16), 'band', scatter_dimension...  84 us
    reduce_scatter x1, waiting for transfers between devices, per_device(): lax.psum_scatter(grad_keys_part.astype(jnp.bfloat16), 'band', scatter_dim...  76.5 us
    all_gather x1, waiting for transfers between devices, per_device(): lax.all_gather(ada_low, 'dp', axis=1, tiled=True)  74.1 us
  transfers between devices with their start and end apart: 25, of which 21 were waited for; matrix products, arithmetic and copies ran while one was open for 21% of the time, Pallas kernels for 0%

commit v1 on v0

--- a/solution.py
+++ b/solution.py
@@ -3,6 +3,8 @@
 import jax
 import jax.numpy as jnp
 from jax import lax
+from jax.experimental import pallas as pl
+from jax.experimental.pallas import tpu as pltpu
 from jax.sharding import PartitionSpec as P
 
 D = 1152
@@ -129,7 +131,7 @@
     return (weight_new, first_new, second_new)
 
 
-def per_device(
+def general_device(
     kept_tokens,
     kept_index,
     resolution,
@@ -366,6 +368,433 @@
     )
 
 
+MASKED = -1e30
+SCORE_SCALE = HEAD_DIM ** (-0.5)
+LOG2E = math.log2(math.e)
+VMEM_LIMIT = 60 * 1024 * 1024
+
+
+def dot_nn(left, right):
+    return lax.dot_general(
+        left, right, (((1,), (0,)), ((), ())), preferred_element_type=jnp.float32
+    )
+
+
+def dot_nt(left, right):
+    return lax.dot_general(
+        left, right, (((1,), (1,)), ((), ())), preferred_element_type=jnp.float32
+    )
+
+
+def attn_kernel(kind_ref, q_ref, k_ref, v_ref, out_ref, lse_ref):
+    tokens = q_ref.shape[2]
+    regions = tokens // REGION
+    other = jnp.where(kind_ref[0] == 1, MASKED, 0.0)
+    keys = jnp.transpose(k_ref[0])
+    for block in range(regions):
+        cols = slice(block * REGION, (block + 1) * REGION)
+        raw = dot_nn(keys, q_ref[0, :, cols])
+        parts = [
+            raw[r * REGION : (r + 1) * REGION] + (0.0 if r == block else other)
+            for r in range(regions)
+        ]
+        scores = jnp.concatenate(parts, axis=0)
+        peak = jnp.max(scores, axis=0, keepdims=True)
+        weights = jnp.exp2((scores - peak) * (SCORE_SCALE * LOG2E))
+        total = jnp.sum(weights, axis=0, keepdims=True)
+        mixed = dot_nn(v_ref[0], weights.astype(jnp.bfloat16))
+        out_ref[0, :, cols] = (mixed / total).astype(jnp.bfloat16)
+        lse_ref[0, :, cols] = peak * (SCORE_SCALE * LOG2E) + jnp.log2(total)
+
+
+def attn_forward(kind, qkv_heads):
+    tokens = qkv_heads.shape[2]
+    head = lambda part: pl.BlockSpec(
+        (1, HEAD_DIM, tokens), lambda h: (h + part * HEADS, 0, 0)
+    )
+    return pl.pallas_call(
+        attn_kernel,
+        grid=(HEADS,),
+        in_specs=[pl.BlockSpec(memory_space=pltpu.SMEM), head(0), head(1), head(2)],
+        out_specs=[head(0), pl.BlockSpec((1, 1, tokens), lambda h: (h, 0, 0))],
+        out_shape=[
+            jax.ShapeDtypeStruct((HEADS, HEAD_DIM, tokens), jnp.bfloat16),
+            jax.ShapeDtypeStruct((HEADS, 1, tokens), jnp.float32),
+        ],
+        compiler_params=pltpu.CompilerParams(vmem_limit_bytes=VMEM_LIMIT),
+        name="attn_forward",
+    )(kind, qkv_heads, qkv_heads, qkv_heads)
+
+
+def attn_back_kernel(kind_ref, q_ref, k_ref, v_ref, out_ref, grad_ref, lse_ref, grads_ref):
+    tokens = q_ref.shape[2]
+    regions = tokens // REGION
+    other = jnp.where(kind_ref[0] == 1, MASKED, 0.0)
+    keys_t = k_ref[0]
+    keys = jnp.transpose(keys_t)
+    values = jnp.transpose(v_ref[0])
+    grad_keys = jnp.zeros((HEAD_DIM, tokens), jnp.float32)
+    grad_values = jnp.zeros((HEAD_DIM, tokens), jnp.float32)
+    for block in range(regions):
+        cols = slice(block * REGION, (block + 1) * REGION)
+        queries = q_ref[0, :, cols]
+        grad = grad_ref[0, :, cols]
+        row_dot = jnp.sum(
+            out_ref[0, :, cols].astype(jnp.float32) * grad.astype(jnp.float32),
+            axis=0,
+            keepdims=True,
+        )
+        raw = dot_nn(keys, queries)
+        parts = [
+            raw[r * REGION : (r + 1) * REGION] + (0.0 if r == block else other)
+            for r in range(regions)
+        ]
+        scores = jnp.concatenate(parts, axis=0)
+        weights = jnp.exp2(scores * (SCORE_SCALE * LOG2E) - lse_ref[0, :, cols])
+        grad_weights = dot_nn(values, grad)
+        grad_scores = (weights * (grad_weights - row_dot)).astype(jnp.bfloat16)
+        grad_values += dot_nt(grad, weights.astype(jnp.bfloat16))
+        grad_keys += dot_nt(queries, grad_scores)
+        grads_ref[0, 0, :, cols] = (dot_nn(keys_t, grad_scores) * SCORE_SCALE).astype(
+            jnp.bfloat16
+        )
+    grads_ref[1, 0] = (grad_keys * SCORE_SCALE).astype(jnp.bfloat16)
+    grads_ref[2, 0] = grad_values.astype(jnp.bfloat16)
+
+
+def attn_backward(kind, qkv_heads, attended, grad_attended, lse):
+    tokens = qkv_heads.shape[2]
+    head = lambda part: pl.BlockSpec(
+        (1, HEAD_DIM, tokens), lambda h: (h + part * HEADS, 0, 0)
+    )
+    return pl.pallas_call(
+        attn_back_kernel,
+        grid=(HEADS,),
+        in_specs=[
+            pl.BlockSpec(memory_space=pltpu.SMEM),
+            head(0),
+            head(1),
+            head(2),
+            head(0),
+            head(0),
+            pl.BlockSpec((1, 1, tokens), lambda h: (h, 0, 0)),
+        ],
+        out_specs=pl.BlockSpec((3, 1, HEAD_DIM, tokens), lambda h: (0, h, 0, 0)),
+        out_shape=jax.ShapeDtypeStruct((3, HEADS, HEAD_DIM, tokens), jnp.bfloat16),
+        compiler_params=pltpu.CompilerParams(vmem_limit_bytes=VMEM_LIMIT),
+        name="attn_backward",
+    )(kind, qkv_heads, qkv_heads, qkv_heads, attended, grad_attended, lse)
+
+
+GELU_A = math.sqrt(2.0 / math.pi)
+GELU_B = 0.044715
+
+
+def mlp_kernel(h_ref, ht_ref, g_ref, gt_ref, up_ref, down_ref, out_ref, grad_ref, gup_ref, gdown_ref):
+    step = pl.program_id(0)
+
+    @pl.when(step == 0)
+    def _():
+        out_ref[...] = jnp.zeros_like(out_ref)
+        grad_ref[...] = jnp.zeros_like(grad_ref)
+
+    up = up_ref[...]
+    down = down_ref[...]
+    upward = dot_nn(h_ref[...], up)
+    square = upward * upward
+    curve = jnp.tanh(GELU_A * upward * (1.0 + GELU_B * square))
+    half = 0.5 * (1.0 + curve)
+    active = (upward * half).astype(jnp.bfloat16)
+    slope = half + 0.5 * upward * (1.0 - curve * curve) * GELU_A * (
+        1.0 + 3.0 * GELU_B * square
+    )
+    grad_upward = (dot_nn(g_ref[...], down) * slope).astype(jnp.bfloat16)
+    out_ref[...] += dot_nt(active, down)
+    grad_ref[...] += dot_nt(grad_upward, up)
+    gup_ref[...] = dot_nn(ht_ref[...], grad_upward).astype(jnp.bfloat16)
+    gdown_ref[...] = dot_nn(gt_ref[...], active).astype(jnp.bfloat16)
+
+
+def mlp_both(hidden, hidden_t, grad, grad_t, up, down_t, tile):
+    tokens, width = hidden.shape
+    wide = up.shape[1]
+    whole = lambda shape: pl.BlockSpec(shape, lambda f: (0, 0))
+    part = pl.BlockSpec((width, tile), lambda f: (0, f))
+    return pl.pallas_call(
+        mlp_kernel,
+        grid=(wide // tile,),
+        in_specs=[
+            whole((tokens, width)),
+            whole((width, tokens)),
+            whole((tokens, width)),
+            whole((width, tokens)),
+            part,
+            part,
+        ],
+        out_specs=[whole((tokens, width)), whole((tokens, width)), part, part],
+        out_shape=[
+            jax.ShapeDtypeStruct((tokens, width), jnp.float32),
+            jax.ShapeDtypeStruct((tokens, width), jnp.float32),
+            jax.ShapeDtypeStruct((width, wide), jnp.bfloat16),
+            jax.ShapeDtypeStruct((width, wide), jnp.bfloat16),
+        ],
+        compiler_params=pltpu.CompilerParams(vmem_limit_bytes=VMEM_LIMIT),
+        name="mlp_both",
+    )(hidden, hidden_t, grad, grad_t, up, down_t)
+
+
+def gather_weight(shard, row_axis="band", column_axis="dp"):
+    columns = lax.all_gather(shard, column_axis, axis=1, tiled=True)
+    return lax.all_gather(columns, row_axis, axis=0, tiled=True)
+
+
+def scatter_grad(grad, row_axis="band", column_axis="dp"):
+    rows = lax.psum_scatter(grad, row_axis, scatter_dimension=0, tiled=True)
+    return lax.psum_scatter(rows, column_axis, scatter_dimension=1, tiled=True).astype(jnp.float32)
+
+
+def swap_slots(values):
+    moved = lax.all_to_all(values, "band", split_axis=0, concat_axis=0, tiled=True)
+    return moved.reshape((-1,) + values.shape[2:])
+
+
+def norm_parts(values):
+    center = jnp.mean(values, axis=-1, keepdims=True)
+    spread = jnp.mean((values - center) ** 2, axis=-1, keepdims=True)
+    root = lax.rsqrt(spread + 1e-06)
+    return ((values - center) * root, root)
+
+
+def norm_back(grad, normal, root, scales):
+    inner = grad * (1.0 + scales)
+    return root * (
+        inner
+        - jnp.mean(inner, axis=-1, keepdims=True)
+        - normal * jnp.mean(inner * normal, axis=-1, keepdims=True)
+    )
+
+
+def embed_tables(count):
+    quarter = D // 4
+    omegas = 1.0 / 10000.0 ** (jnp.arange(quarter, dtype=jnp.float32) / quarter)
+    angles = jnp.arange(count, dtype=jnp.float32)[:, None] * omegas
+    return jnp.concatenate([jnp.sin(angles), jnp.cos(angles)], axis=-1)
+
+
+def grid_embed_slot(kind, tokens):
+    table = embed_tables(SIDE)
+    half = D // 2
+    side = SIDE
+    wide = jnp.concatenate(
+        [
+            jnp.broadcast_to(table[:, None, :], (side, side, half)),
+            jnp.broadcast_to(table[None, :, :], (side, side, half)),
+        ],
+        axis=-1,
+    ).reshape(tokens, D)
+    small = side // 2
+    table_small = table[:small]
+    narrow = jnp.concatenate(
+        [
+            jnp.broadcast_to(table_small[None, :, None, :], (tokens // REGION, small, small, half)),
+            jnp.broadcast_to(table_small[None, None, :, :], (tokens // REGION, small, small, half)),
+        ],
+        axis=-1,
+    ).reshape(tokens, D)
+    return jnp.where(kind == 1, narrow, wide)
+
+
+def slot_device(
+    kept_tokens,
+    kept_index,
+    resolution,
+    labels,
+    timesteps,
+    class_table,
+    cotangent,
+    mask_token,
+    w_qkv,
+    w_proj,
+    w_fc1,
+    w_fc2,
+    w_ada,
+    mask_first,
+    first_qkv,
+    first_proj,
+    first_fc1,
+    first_fc2,
+    first_ada,
+    mask_second,
+    second_qkv,
+    second_proj,
+    second_fc1,
+    second_fc2,
+    second_ada,
+):
+    highest = lax.Precision.HIGHEST
+    bf16 = jnp.bfloat16
+    bands = lax.axis_size("band")
+    groups = lax.axis_size("dp")
+    band = lax.axis_index("band")
+    slots, local_rows, _ = cotangent.shape
+    tokens_count = bands * local_rows
+    regions = tokens_count // REGION
+    images = labels.shape[1]
+
+    picks = lax.all_gather(jnp.concatenate([labels, timesteps], axis=1), "dp", axis=0, tiled=True)
+    rows_ada, cols_ada = w_ada.shape
+    count = picks.shape[0] * images
+    all_labels = picks[:, :images].reshape(count)
+    all_times = picks[:, images:].reshape(count)
+    table_part = lax.dynamic_slice_in_dim(class_table, band * rows_ada, rows_ada, axis=1)
+    chosen = (all_labels[:, None] == jnp.arange(class_table.shape[0])[None, :]).astype(jnp.float32)
+    features = band * rows_ada + jnp.arange(rows_ada)
+    half_width = D // 2
+    frequency = jnp.exp(
+        -math.log(10000.0) * (features % half_width).astype(jnp.float32) / half_width
+    )
+    angles = all_times.astype(jnp.float32)[:, None] * frequency
+    waves = jnp.where(features < half_width, jnp.cos(angles), jnp.sin(angles))
+    condition = jnp.matmul(chosen, table_part, precision=highest) + waves
+    cond_low = jax.nn.silu(condition).astype(bf16)
+    partial = jnp.matmul(cond_low, w_ada.astype(bf16), preferred_element_type=jnp.float32)
+    partial = partial.reshape(groups, slots, images, cols_ada).transpose(1, 0, 2, 3)
+    own_rows = lax.psum_scatter(partial, "band", scatter_dimension=0, tiled=True)[0]
+    modulation = lax.all_to_all(own_rows, "dp", split_axis=0, concat_axis=0, tiled=True)
+    modulation = modulation.transpose(1, 0, 2).reshape(images, groups * cols_ada)
+
+    kind = lax.dynamic_slice_in_dim(resolution, band, 1)
+    kept = swap_slots(kept_tokens)
+    index = swap_slots(kept_index)
+    grad_out = swap_slots(cotangent).reshape(regions, REGION, D)
+
+    mod = jnp.where(kind[0] == 1, modulation, modulation[:1])
+    shift_attn, scale_attn, gate_attn, shift_mlp, scale_mlp, gate_mlp = [
+        piece[:, None, :] for piece in jnp.split(mod, 6, axis=-1)
+    ]
+    select = jnp.arange(tokens_count)[:, None] == index[None, :]
+    select_low = select.astype(bf16)
+    unfilled = 1.0 - jnp.sum(select.astype(jnp.float32), axis=1, keepdims=True)
+    placed = jnp.matmul(select_low, kept, preferred_element_type=jnp.float32)
+    tokens = placed + unfilled * mask_token + grid_embed_slot(kind[0], tokens_count)
+    tokens = tokens.reshape(regions, REGION, D)
+
+    qkv_full = gather_weight(w_qkv.astype(bf16))
+    proj_full = gather_weight(w_proj.astype(bf16))
+    fc1_full = gather_weight(w_fc1.astype(bf16))
+    fc2_full = gather_weight(w_fc2.astype(bf16).T, "dp", "band")
+
+    normal_attn, root_attn = norm_parts(tokens)
+    hidden = (normal_attn * (1.0 + scale_attn) + shift_attn).astype(bf16).reshape(tokens_count, D)
+    qkv = lax.dot_general(
+        qkv_full, hidden, (((0,), (1,)), ((), ())), preferred_element_type=jnp.float32
+    ).astype(bf16)
+    qkv_heads = qkv.reshape(3 * HEADS, HEAD_DIM, tokens_count)
+    attended, lse = attn_forward(kind, qkv_heads)
+    attended_t = attended.reshape(D, tokens_count)
+    branch = lax.dot_general(
+        attended_t, proj_full, (((0,), (0,)), ((), ())), preferred_element_type=jnp.float32
+    ).reshape(regions, REGION, D)
+    middle = tokens + gate_attn * branch
+    normal_mlp, root_mlp = norm_parts(middle)
+    hidden_mlp = (normal_mlp * (1.0 + scale_mlp) + shift_mlp).astype(bf16).reshape(tokens_count, D)
+    grad_full = grad_out.astype(jnp.float32)
+    grad_output = (gate_mlp * grad_full).astype(bf16).reshape(tokens_count, D)
+
+    output, grad_hidden_mlp, grad_fc1, grad_fc2 = mlp_both(
+        hidden_mlp, hidden_mlp.T, grad_output, grad_output.T, fc1_full, fc2_full, 512
+    )
+    output = output.reshape(regions, REGION, D)
+    grad_hidden_mlp = grad_hidden_mlp.reshape(regions, REGION, D)
+    block_slot = (middle + gate_mlp * output).astype(bf16)
+    block_out = lax.all_to_all(
+        block_slot.reshape(bands, local_rows, D), "band", split_axis=0, concat_axis=0, tiled=True
+    )
+    grad_gate_mlp = jnp.sum(grad_full * output, axis=1)
+    grad_shift_mlp = jnp.sum(grad_hidden_mlp, axis=1)
+    grad_scale_mlp = jnp.sum(grad_hidden_mlp * normal_mlp, axis=1)
+    grad_middle = grad_full + norm_back(grad_hidden_mlp, normal_mlp, root_mlp, scale_mlp)
+    grad_gate_attn = jnp.sum(grad_middle * branch, axis=1)
+    grad_branch = (gate_attn * grad_middle).astype(bf16).reshape(tokens_count, D)
+    grad_proj = dot_nn(attended_t, grad_branch).astype(bf16)
+    grad_attended = dot_nt(proj_full, grad_branch).astype(bf16)
+    grad_heads = grad_attended.reshape(HEADS, HEAD_DIM, tokens_count)
+    grad_qkv = attn_backward(kind, qkv_heads, attended, grad_heads, lse)
+    grad_qkv = grad_qkv.reshape(3 * D, tokens_count)
+    grad_qkv_weight = lax.dot_general(
+        hidden, grad_qkv, (((0,), (1,)), ((), ())), preferred_element_type=jnp.float32
+    ).astype(bf16)
+    grad_hidden = lax.dot_general(
+        grad_qkv, qkv_full, (((0,), (1,)), ((), ())), preferred_element_type=jnp.float32
+    ).reshape(regions, REGION, D)
+    grad_shift_attn = jnp.sum(grad_hidden, axis=1)
+    grad_scale_attn = jnp.sum(grad_hidden * normal_attn, axis=1)
+    grad_tokens = grad_middle + norm_back(grad_hidden, normal_attn, root_attn, scale_attn)
+    grad_tokens = grad_tokens.reshape(tokens_count, D)
+
+    grad_mod = jnp.concatenate(
+        [
+            grad_shift_attn,
+            grad_scale_attn,
+            grad_gate_attn,
+            grad_shift_mlp,
+            grad_scale_mlp,
+            grad_gate_mlp,
+        ],
+        axis=-1,
+    )
+    first_only = (jnp.arange(images) == 0).astype(jnp.float32)[:, None]
+    grad_mod = jnp.where(
+        kind[0] == 1, grad_mod, first_only * jnp.sum(grad_mod, axis=0, keepdims=True)
+    )
+    grad_mod = grad_mod.reshape(images, groups, cols_ada).transpose(1, 0, 2)
+    grad_mod = lax.all_to_all(grad_mod, "dp", split_axis=0, concat_axis=0, tiled=True)
+    grad_mod = lax.all_gather(grad_mod, "band", axis=1, tiled=True)
+    red_ada = lax.dot_general(
+        cond_low.astype(jnp.float32),
+        grad_mod.reshape(count, cols_ada),
+        (((0,), (0,)), ((), ())),
+        precision=highest,
+        preferred_element_type=jnp.float32,
+    )
+
+    grad_kept = lax.dot_general(
+        select_low, grad_tokens.astype(bf16), (((0,), (0,)), ((), ())),
+        preferred_element_type=jnp.float32,
+    ).astype(bf16)
+    kept_grad = lax.all_to_all(
+        grad_kept.reshape(bands, -1, D), "band", split_axis=0, concat_axis=0, tiled=True
+    ).astype(jnp.float32)
+    grad_mask_part = jnp.sum(unfilled * grad_tokens, axis=0)
+
+    red_qkv = scatter_grad(grad_qkv_weight)
+    red_proj = scatter_grad(grad_proj)
+    red_fc1 = scatter_grad(grad_fc1)
+    red_fc2 = scatter_grad(grad_fc2, "dp", "band").T
+
+    grad_mask = lax.psum(grad_mask_part, ("dp", "band"))
+    reduced = (red_qkv, red_proj, red_fc1, red_fc2, red_ada)
+    local_squares = sum((jnp.sum(grad * grad) for grad in reduced))
+    total_squares = lax.psum(local_squares, ("dp", "band")) + jnp.sum(grad_mask * grad_mask)
+    norm_value = jnp.sqrt(total_squares)
+    factor = clip_level / jnp.maximum(norm_value, clip_level)
+    mask_new = adamw(mask_token, mask_first, mask_second, grad_mask * factor)
+    qkv_new = adamw(w_qkv, first_qkv, second_qkv, red_qkv * factor)
+    proj_new = adamw(w_proj, first_proj, second_proj, red_proj * factor)
+    fc1_new = adamw(w_fc1, first_fc1, second_fc1, red_fc1 * factor)
+    fc2_new = adamw(w_fc2, first_fc2, second_fc2, red_fc2 * factor)
+    ada_new = adamw(w_ada, first_ada, second_ada, red_ada * factor)
+    moved = tuple(zip(mask_new, qkv_new, proj_new, fc1_new, fc2_new, ada_new))
+    return (block_out, kept_grad, norm_value) + moved[0] + moved[1] + moved[2]
+
+
+def per_device(*arguments):
+    cotangent = arguments[6]
+    if cotangent.shape[0] == lax.axis_size("band"):
+        return slot_device(*arguments)
+    return general_device(*arguments)
+
+
 def solution(mesh):
     in_specs = (
         P("dp", "band", None),

time: 2250 us -> 1370 us (0.61)
  waiting for transfers between devices: 1270 us -> 736 us
  matrix products: 572 us -> 85.6 us
  Pallas kernels: 0 us -> 173 us
  local copies, waits for them, and re-layouts: 188 us -> 96.4 us
  blocking collectives: 81.1 us -> 146 us
  other arithmetic: 108 us -> 71.1 us
  starting transfers between devices: 1.03 us -> 26 us
    dot_general x45 -> x11, matrix products: 572 us -> 85.6 us  [the longest x1 20.6 us: slot_device(): lax.dot_general(grad_qkv, qkv_full, (((0,), (1,)), ((), ())), preferred_e...]
    all_gather x12 -> x7, waiting for transfers between devices: 453 us -> 204 us  [the longest x4 148 us: gather_weight(): return lax.all_gather(columns, row_axis, axis=0, tiled=True)]
    unnamed x30 -> x20, waiting for transfers between devices: 386 us -> 174 us
    pallas_call x0 -> x3, Pallas kernels: none -> 173 us  [the longest x1 79.1 us: mlp_both(): pl.pallas_call(mlp_kernel, grid=(wide // tile,), in_specs=[whole((tokens,...]
    reduce_scatter x8 -> x5, waiting for transfers between devices: 432 us -> 300 us  [the longest x4 298 us: scatter_grad(): rows = lax.psum_scatter(grad, row_axis, scatter_dimension=0, tiled=True)]
    gather x3 -> x0, local copies, waits for them, and re-layouts: 59 us -> none  [the longest x1 56 us: pick_rows(): return table_rows[picks]]
    all_to_all x0 -> x6, waiting for transfers between devices: none -> 58.2 us  [the longest x3 58.1 us: swap_slots(): lax.all_to_all(values, 'band', split_axis=0, concat_axis=0, tiled=True)]
    all_gather x2 -> x3, blocking collectives: 40.5 us -> 86.7 us  [the longest x1 33.3 us: gather_weight(): columns = lax.all_gather(shard, column_axis, axis=1, tiled=True)]
  transfers between devices with their start and end apart: 25 -> 22, of which waited for: 21 -> 14; matrix products, arithmetic and copies ran while one was open for 21% -> 15% of each run, Pallas kernels for 0% -> 7%
where the time goes in v1:
time: 1370 us; the launch traced here: 1360 us
  waiting for transfers between devices  736 us (54%)
  Pallas kernels  173 us (13%)
  blocking collectives  146 us (11%)
  local copies, waits for them, and re-layouts  96.4 us (7%)
  matrix products  85.6 us (6%)
  other arithmetic  71.1 us (5%)
  starting transfers between devices  26 us (2%)
  between operations  21.5 us (2%)
    reduce_scatter x4, waiting for transfers between devices, scatter_grad(): rows = lax.psum_scatter(grad, row_axis, scatter_dimension=0, tiled=True)  298 us
    unnamed x20, waiting for transfers between devices  174 us
    all_gather x4, waiting for transfers between devices, gather_weight(): return lax.all_gather(columns, row_axis, axis=0, tiled=True)  148 us
    pallas_call x1, Pallas kernels, mlp_both(): pl.pallas_call(mlp_kernel, grid=(wide // tile,), in_specs=[whole((tokens,...  79.1 us
    all_to_all x3, waiting for transfers between devices, swap_slots(): lax.all_to_all(values, 'band', split_axis=0, concat_axis=0, tiled=True)  58.1 us
    all_gather x3, waiting for transfers between devices, gather_weight(): columns = lax.all_gather(shard, column_axis, axis=1, tiled=True)  56 us
    pallas_call x1, Pallas kernels, attn_backward(): pl.pallas_call(attn_back_kernel, grid=(HEADS,), in_specs=[pl.BlockSpec(me...  48.5 us
    unnamed x72, local copies, waits for them, and re-layouts  47.2 us
  transfers between devices with their start and end apart: 22, of which 14 were waited for; matrix products, arithmetic and copies ran while one was open for 15% of the time, Pallas kernels for 7%

profile of v1, /device:TPU:0, one launch (start us, length us, event | category | flops | bytes accessed | tf_op | source)
XLA Modules:
  0.0 1355.3 jit_solution(4849949287491856693)
XLA Ops:
  13.9 27.9 %all-gather = s32[8,4,8]{2,1,0:T(4,128)S(1)} all-gather(s32[1,4,8]{2,1,0:T(4,128)S(1)} %add_bitcast_fusion), channel_id=1, replica_groups=mesh['dp'=8,'band'=4] {'dp'}, dimensions={0}, use_global_device_ids=true | all-gather | bytes 1152 | tf_op jit(solution)/shard_map/all_gather | solution.py:644
  48.1 17.6 %all-gather.21.cloned.1.call-done = bf16[8,432,288]{1,2,0:T(8,128)(2,1)} async-done(((bf16[1,432,288]{1,2,0:T(8,128)(2,1)}), bf16[8,432,288]{1,2,0:T(8,128)(2,1)}) %all-gather.21.cloned.1.call-update) | async-done | bytes 1990672 | tf_op jit(solution)/shard_map/all_gather | solution.py:547
  72.7 33.3 %all_gather.33 = bf16[288,1152]{0,1:T(8,128)(2,1)S(1)} all-gather(bf16[288,144]{0,1:T(8,128)(2,1)S(1)} %convert_element_type.119), channel_id=1, replica_groups=mesh['dp'=8,'band'=4] {'dp'}, dimensions={1}, use_global_device_ids=true | all-gather | bytes 746496 | tf_op jit(solution)/shard_map/all_gather | solution.py:547
  108.0 38.4 %all-gather.23.cloned.1.call-done = bf16[8,576,288]{1,2,0:T(8,128)(2,1)} async-done(((bf16[1,576,288]{1,2,0:T(8,128)(2,1)}), bf16[8,576,288]{1,2,0:T(8,128)(2,1)}) %all-gather.23.cloned.1.call-update) | async-done | bytes 2654224 | tf_op jit(solution)/shard_map/all_gather | solution.py:547
  203.6 48.8 %all-to-all-done.3 = bf16[4,256,1152]{2,1,0:T(8,128)(2,1)S(1)} async-done(((bf16[4,256,1152]{2,1,0:T(8,128)(2,1)}), bf16[4,256,1152]{2,1,0:T(8,128)(2,1)S(1)}, u32[]{:S(2)}, u32[]{:S(2)}) %all-to-all-start.3) | async-done | bytes 2359328 | tf_op jit(solution)/shard_map/all_to_all | solution.py:557
  258.6 15.2 %fusion.2 = bf16[3456,1024]{0,1:T(8,128)(2,1)} fusion(bf16[1024,1152]{1,0:T(8,128)(2,1)} %fusion.6, bf16[1152,3456]{1,0:T(8,128)(2,1)} %all-gather.11.cloned.1.call-done), kind=kOutput, calls=%fused_computation.8 | convolution fusion | flops 8157265920 | bytes 17399808 | tf_op jit(solution)/shard_map/dot_general | solution.py:689
  273.8 10.3 copy.158
  284.1 45.4 %attn_forward.1 = (bf16[16,72,1024]{2,1,0:T(8,128)(2,1)}, f32[16,1,1024]{2,1,0:T(1,128)}) custom-call(s32[1]{0:T(128)} %dynamic_slice.6.kind_ref, bf16[48,72,1024]{2,1,0:T(8,128)(2,1)} %bitcast.128, bf16[48,72,1024]{2,1,0:T(8,128)(2,1)} %bitcast.129, bf16[48,72,1024]{2,1,0:T(8,128)(2,1)} %bitcast.130), custom_call_target="tpu_custom_call" | custom-call | tf_op jit(solution)/shard_map/attn_forward/pallas_call | solution.py:415
  333.9 10.9 multiply_add_fusion.1
  360.0 77.2 %all-gather.19.cloned.1.call-done.down_ref = bf16[1152,4608]{1,0:T(8,128)(2,1)} async-done(((bf16[144,4608]{1,0:T(8,128)(2,1)}), bf16[1152,4608]{1,0:T(8,128)(2,1)}) %all-gather.19.cloned.1.call-update) | async-done | bytes 10616848 | tf_op jit(solution)/shard_map/all_gather | solution.py:548
  437.2 70.7 %all-gather.15.cloned.1.call-done.up_ref = bf16[1152,4608]{1,0:T(8,128)(2,1)} async-done(((bf16[288,4608]{1,0:T(8,128)(2,1)}), bf16[1152,4608]{1,0:T(8,128)(2,1)}) %all-gather.15.cloned.1.call-update) | async-done | bytes 10616848 | tf_op jit(solution)/shard_map/all_gather | solution.py:548
  507.9 79.1 %mlp_both.1 = (f32[1024,1152]{1,0:T(8,128)}, f32[1024,1152]{1,0:T(8,128)}, bf16[1152,4608]{1,0:T(8,128)(2,1)}, bf16[1152,4608]{1,0:T(8,128)(2,1)}) custom-call(bf16[1024,1152]{1,0:T(8,128)(2,1)} %bitcast.141, bf16[1152,1024]{1,0:T(8,128)(2,1)} %bitcast.150, bf16[1024,1152]{1,0:T(8,128)(2,1)} %bitcast.139, bf16[1152,1024]{1,0:T(8,128)(2,1)} %bitcast.149, ...), custom_call_target="tpu_custom_call" | custom-call | tf_op jit(solution)/shard_map/mlp_both/pallas_call | solution.py:523
  621.0 48.5 %attn_backward.1 = bf16[3,16,72,1024]{3,2,1,0:T(8,128)(2,1)} custom-call(s32[1]{0:T(128)} %dynamic_slice.6.kind_ref, bf16[48,72,1024]{2,1,0:T(8,128)(2,1)} %bitcast.131, bf16[48,72,1024]{2,1,0:T(8,128)(2,1)} %bitcast.132, bf16[48,72,1024]{2,1,0:T(8,128)(2,1)} %bitcast.133, bf16[16,72,1024]{2,1,0:T(8,128)(2,1)} %get-tuple-element.27.out_ref, ...), custom_call_target="tpu_custom_call" | custom-call | tf_op jit(solution)/shard_map/attn_backward/pallas_call | solution.py:470
  669.5 13.8 %convolution_convert_fusion = bf16[1152,3456]{1,0:T(8,128)(2,1)} fusion(bf16[1024,1152]{1,0:T(8,128)(2,1)S(1)} %copy-done.9, bf16[3456,1024]{1,0:T(8,128)(2,1)} %bitcast.136), kind=kOutput, calls=%fused_computation | convolution fusion | flops 8157708288 | bytes 17399808 | tf_op jit(solution)/shard_map/dot_general | solution.py:724
  687.1 65.8 %reduce-scatter.20.cloned.1.call-done = bf16[288,3456]{1,0:T(8,128)(2,1)} async-done(((bf16[1152,3456]{1,0:T(8,128)(2,1)}), bf16[288,3456]{1,0:T(8,128)(2,1)}) %reduce-scatter.20.cloned.1.call-update) | async-done | bytes 1990672 | tf_op jit(solution)/shard_map/reduce_scatter | solution.py:552
  767.3 169.6 %reduce-scatter.26.cloned.1.call-done = bf16[144,4608]{1,0:T(8,128)(2,1)} async-done(((bf16[1152,4608]{1,0:T(8,128)(2,1)}), bf16[144,4608]{1,0:T(8,128)(2,1)}) %reduce-scatter.26.cloned.1.call-update) | async-done | bytes 1327120 | tf_op jit(solution)/shard_map/reduce_scatter | solution.py:552
  940.9 20.6 %multiply_reduce_fusion.7 = (f32[4,256]{1,0:T(4,128)S(1)}, f32[4,256]{1,0:T(4,128)S(1)}, f32[4,1152]{1,0:T(4,128)S(1)}, f32[4,1152]{1,0:T(4,128)S(1)}, f32[4,256,1152]{2,1,0:T(8,128)}) fusion(f32[4,1152]{1,0:T(4,128)S(1)} %get-tuple-element.196, f32[4,256]{1,0:T(4,128)S(1)} %rsqrt.22, f32[4,256,1152]{2,1,0:T(8,128)} %bitcast.134, f32[4,256]{1,0:T(4,128)S(1)} %div.154, ...), kind=kOutput, calls=%fused_computation.38 | convolution fusion | flops 8166691840 | bytes 29267968 | tf_op jit(solution)/shard_map/dot_general | solution.py:727
  961.6 63.0 %reduce-scatter.24.cloned.1.call-done = bf16[288,4608]{1,0:T(8,128)(2,1)} async-done(((bf16[1152,4608]{1,0:T(8,128)(2,1)}), bf16[288,4608]{1,0:T(8,128)(2,1)}) %reduce-scatter.24.cloned.1.call-update) | async-done | bytes 2654224 | tf_op jit(solution)/shard_map/reduce_scatter | solution.py:552
  1043.8 18.3 %all_to_all.39 = bf16[4,128,1152]{2,1,0:T(8,128)(2,1)S(1)} all-to-all(bf16[4,128,1152]{2,1,0:T(8,128)(2,1)S(1)} %bitcast.161), channel_id=1, replica_groups=mesh['dp'=8,'band'=4] {'band'}, dimensions={0} | all-to-all | bytes 2359296 | tf_op jit(solution)/shard_map/all_to_all | solution.py:765
  1072.0 25.5 %all_gather.39 = f32[8,16,864]{2,0,1:T(8,128)S(1)} all-gather(f32[8,4,864]{2,0,1:T(8,128)S(1)} %copy.169), channel_id=1, replica_groups=mesh['dp'=8,'band'=4] {'band'}, dimensions={1}, use_global_device_ids=true | all-gather | bytes 552960 | tf_op jit(solution)/shard_map/all_gather | solution.py:752
  1103.9 59.3 %reduce-scatter.28.cloned.1.call-done = bf16[432,288]{1,0:T(8,128)(2,1)} async-done(((bf16[3456,288]{1,0:T(8,128)(2,1)}), bf16[432,288]{1,0:T(8,128)(2,1)}) %reduce-scatter.28.cloned.1.call-update) | async-done | bytes 248848
  1166.3 31.8 %reduce-scatter.34.cloned.1.call-done = bf16[1152,144]{1,0:T(8,128)(2,1)} async-done(((bf16[4608,144]{1,0:T(8,128)(2,1)}), bf16[1152,144]{1,0:T(8,128)(2,1)}) %reduce-scatter.34.cloned.1.call-update) | async-done | bytes 331792
  1200.2 80.4 %reduce-scatter.32.cloned.1.call-done = bf16[576,288]{1,0:T(8,128)(2,1)} async-done(((bf16[4608,288]{1,0:T(8,128)(2,1)}), bf16[576,288]{1,0:T(8,128)(2,1)}) %reduce-scatter.32.cloned.1.call-update) | async-done | bytes 331792
  1284.6 40.7 %all-reduce = (f32[]{:T(128)}, f32[1152]{0:T(1024)S(1)}) all-reduce(f32[]{:T(128)S(6)} %add.250, f32[1152]{0:T(1024)S(1)} %get-tuple-element.186), channel_id=1, replica_groups=mesh['dp'=8,'band'=4] {'dp','band'}, use_global_device_ids=true, to_apply=%region_30.31 | all-reduce | flops 1153 | bytes 9224 | tf_op jit(solution)/shard_map/psum | solution.py:778
  (211 shorter events, 221.7 us)
Async XLA Ops:
  7.2 58.5 %all-gather.21.cloned.1.call-start = ((), (), s32[]{:S(2)}) async-start(), calls=%async_computation.26 | async-start | bytes 2654208 | tf_op jit(solution)/shard_map/all_gather | solution.py:547
  9.2 98.1 %all-gather.17.cloned.1.call-start = ((), (), s32[]{:S(2)}) async-start(), calls=%async_computation.20 | async-start | bytes 1658880 | tf_op jit(solution)/shard_map/all_gather | solution.py:547
  11.1 135.3 %all-gather.23.cloned.1.call-start = ((), (), s32[]{:S(2)}) async-start(), calls=%async_computation.27 | async-start | bytes 3317760 | tf_op jit(solution)/shard_map/all_gather | solution.py:547
  13.1 157.1 %reduce-scatter.18.cloned.1.call-start = ((), (), s32[]{:S(2)}) async-start(), calls=%async_computation.16 | async-start | bytes 573440 | tf_op jit(solution)/shard_map/reduce_scatter | solution.py:662
  48.0 210.6 %all-gather.11.cloned.1.call-start = ((), (), s32[]{:S(2)}) async-start(), calls=%async_computation.17 | async-start | bytes 9953280 | tf_op jit(solution)/shard_map/all_gather | solution.py:548
  72.6 261.3 %all-gather.13.cloned.1.call-start = ((), (), s32[]{:S(2)}) async-start(), calls=%async_computation.18 | async-start | bytes 3317760 | tf_op jit(solution)/shard_map/all_gather | solution.py:548
  107.2 330.0 %all-gather.19.cloned.1.call-start = ((), (), s32[]{:S(2)}) async-start(), calls=%async_computation.21 | async-start | bytes 11943936 | tf_op jit(solution)/shard_map/all_gather | solution.py:548
  108.0 400.0 %all-gather.15.cloned.1.call-start = ((), (), s32[]{:S(2)}) async-start(), calls=%async_computation.19 | async-start | bytes 13271040 | tf_op jit(solution)/shard_map/all_gather | solution.py:548
  152.5 8.3 all-to-all-start
  160.8 20.2 %all-to-all-start.1 = ((bf16[4,128,1152]{2,1,0:T(8,128)(2,1)}), bf16[4,128,1152]{2,1,0:T(8,128)(2,1)S(1)}, u32[]{:S(2)}, u32[]{:S(2)}) async-start(bf16[4,128,1152]{2,1,0:T(8,128)(2,1)} %param.25), calls=%async_computation.1 | async-start | bytes 2359296 | tf_op jit(solution)/shard_map/all_to_all | solution.py:557
  181.0 13.8 %all-to-all-start.2 = ((f32[8,4,864]{2,1,0:T(4,128)}), f32[8,4,864]{2,1,0:T(4,128)S(1)}, u32[]{:S(2)}, u32[]{:S(2)}) async-start(f32[8,4,864]{2,1,0:T(4,128)} %copy.155), calls=%async_computation.3 | async-start | bytes 229376 | tf_op jit(solution)/shard_map/all_to_all | solution.py:663
  194.7 57.7 %all-to-all-start.3 = ((bf16[4,256,1152]{2,1,0:T(8,128)(2,1)}), bf16[4,256,1152]{2,1,0:T(8,128)(2,1)S(1)}, u32[]{:S(2)}, u32[]{:S(2)}) async-start(bf16[4,256,1152]{2,1,0:T(8,128)(2,1)} %param.31), calls=%async_computation.4 | async-start | bytes 4718592 | tf_op jit(solution)/shard_map/all_to_all | solution.py:557
  198.4 486.3 %reduce-scatter.22.cloned.1.call-start = ((), (), s32[]{:S(2)}) async-start(), calls=%async_computation.23 | async-start | bytes 3317760 | tf_op jit(solution)/shard_map/reduce_scatter | solution.py:552
  612.2 140.7 %reduce-scatter.20.cloned.1.call-start = ((), (), s32[]{:S(2)}) async-start(), calls=%async_computation.22 | async-start | bytes 9953280 | tf_op jit(solution)/shard_map/reduce_scatter | solution.py:552
  683.3 253.5 %reduce-scatter.26.cloned.1.call-start = ((), (), s32[]{:S(2)}) async-start(), calls=%async_computation.25 | async-start | bytes 11943936 | tf_op jit(solution)/shard_map/reduce_scatter | solution.py:552
  684.1 340.5 %reduce-scatter.24.cloned.1.call-start = ((), (), s32[]{:S(2)}) async-start(), calls=%async_computation.24 | async-start | bytes 13271040 | tf_op jit(solution)/shard_map/reduce_scatter | solution.py:552
  684.7 417.5 %reduce-scatter.30.cloned.1.call-start = ((), (), s32[]{:S(2)}) async-start(), calls=%async_computation.29 | async-start | bytes 995328
  687.1 476.1 %reduce-scatter.28.cloned.1.call-start = ((), (), s32[]{:S(2)}) async-start(), calls=%async_computation.28 | async-start | bytes 2985984
  757.1 441.0 %reduce-scatter.34.cloned.1.call-start = ((), (), s32[]{:S(2)}) async-start(), calls=%async_computation.31 | async-start | bytes 2949120
  940.6 340.0 %reduce-scatter.32.cloned.1.call-start = ((), (), s32[]{:S(2)}) async-start(), calls=%async_computation.30 | async-start | bytes 3981312
  1030.4 13.4 all-to-all-start.6
  1062.0 40.1 %all-to-all-start.4 = ((bf16[4,256,1152]{2,1,0:T(8,128)(2,1)}), bf16[4,256,1152]{2,1,0:T(8,128)(2,1)S(1)}, u32[]{:S(2)}, u32[]{:S(2)}) async-start(bf16[4,256,1152]{2,1,0:T(8,128)(2,1)} %get-tuple-element.190), calls=%async_computation.5 | async-start | bytes 4718592 | tf_op jit(solution)/shard_map/all_to_all | solution.py:710
  1100.6 234.2 %copy-start.19 = (f32[1152]{0:T(1024)S(1)}, f32[1152]{0:T(1024)}, u32[]{:S(2)}) copy-start(f32[1152]{0:T(1024)} %param.32) | copy-start | bytes 13828
  1102.2 232.7 %copy-start.23 = (f32[1152]{0:T(1024)S(1)}, f32[1152]{0:T(1024)}, u32[]{:S(2)}) copy-start(f32[1152]{0:T(1024)} %param.44) | copy-start | bytes 13828
  (23 other events, 479.5 us)
Sparse Core Ops, SparseCore 0:
  10.8 54.8 all-gather.20
  67.8 16.7 all-gather.16
  87.4 58.9 all-gather.22
  149.4 20.7 reduce-scatter.17
  172.1 82.6 all-gather.10
  256.8 25.7 all-gather.12
  284.7 152.4 all-gather.18
  438.8 69.1 all-gather.14
  612.3 34.8 reduce-scatter.21
  683.5 69.3 reduce-scatter.19
  756.9 179.8 reduce-scatter.25
  939.3 85.2 reduce-scatter.23
  1028.5 61.2 reduce-scatter.29
  1093.4 69.7 reduce-scatter.27
  1166.3 31.8 reduce-scatter.33
  1201.6 78.9 reduce-scatter.31

commit v2 on v1

--- a/solution.py
+++ b/solution.py
@@ -1,3 +1,4 @@
+import functools
 import math
 
 import jax
@@ -543,14 +544,463 @@
     )(hidden, hidden_t, grad, grad_t, up, down_t)
 
 
-def gather_weight(shard, row_axis="band", column_axis="dp"):
-    columns = lax.all_gather(shard, column_axis, axis=1, tiled=True)
-    return lax.all_gather(columns, row_axis, axis=0, tiled=True)
-
-
-def scatter_grad(grad, row_axis="band", column_axis="dp"):
-    rows = lax.psum_scatter(grad, row_axis, scatter_dimension=0, tiled=True)
-    return lax.psum_scatter(rows, column_axis, scatter_dimension=1, tiled=True).astype(jnp.float32)
+BLOCK_ROWS = 144
+BLOCK_COLS = 1152
+VIA_X = (0, 3)
+
+
+def flip(index):
+    return index + 1 - 2 * (index % 2)
+
+
+def along_z(z, step):
+    return (z, flip(z), (z + 2) % 4, 3 - z)[step]
+
+
+class Place:
+    def __init__(self):
+        dp = lax.axis_index("dp")
+        band = lax.axis_index("band")
+        self.z, self.y, self.x, self.core = dp // 2, dp % 2, band // 2, band % 2
+
+    def chip(self, i, a, b):
+        return (along_z(self.z, i), flip(self.y) if a else self.y, flip(self.x) if b else self.x)
+
+    def device(self, i=0, a=0, b=0, core=0):
+        z, y, x = self.chip(i, a, b)
+        return (z * 2 + y, x * 2 + (flip(self.core) if core else self.core))
+
+    def partners(self):
+        return [
+            self.device(core=1),
+            self.device(b=1),
+            self.device(a=1),
+            self.device(i=1),
+            self.device(i=2),
+            self.device(i=3),
+        ]
+
+    def block(self, by_rows, i, a, b, core=0):
+        z, y, x = self.chip(i, a, b)
+        c = flip(self.core) if core else self.core
+        if by_rows:
+            row, col = z * 2 + y, x * 2 + c
+        else:
+            row, col = (x * 2 + c) * 2 + y, z
+        return (
+            pl.ds(pl.multiple_of(row * BLOCK_ROWS, 16), BLOCK_ROWS),
+            pl.ds(pl.multiple_of(col * BLOCK_COLS, 128), BLOCK_COLS),
+        )
+
+
+def greet(place):
+    barrier = pltpu.get_barrier_semaphore()
+    partners = place.partners()
+    for partner in partners:
+        pl.semaphore_signal(
+            barrier, inc=1, device_id=partner, device_id_type=pl.DeviceIdType.MESH
+        )
+    pl.semaphore_wait(barrier, len(partners))
+
+
+def send(source, target, send_sem, recv_sem, device):
+    return pltpu.make_async_remote_copy(
+        src_ref=source,
+        dst_ref=target,
+        send_sem=send_sem,
+        recv_sem=recv_sem,
+        device_id=device,
+        device_id_type=pl.DeviceIdType.MESH,
+    )
+
+
+GATHER_SENDS = 16 + 6 + 6 + 3
+
+
+def gather_actions(place, by_rows, own_refs, full_refs, local_sems, send_sems, link_sems, core_sems):
+    weights = range(len(own_refs))
+    counts = [0] * len(own_refs)
+
+    def forward(w, source, piece, i=0, a=0, b=0, core=0):
+        pi, pa, pb = piece
+        name = (pi if i == 0 else i) * 4 + (pa ^ a) * 2 + (pb ^ b)
+        target = full_refs[w].at[place.block(by_rows[w], pi, pa, pb)]
+        sems = core_sems if core else link_sems
+        copy = send(
+            source,
+            target,
+            send_sems.at[w, counts[w]],
+            sems.at[w, name],
+            place.device(i, a, b, core),
+        )
+        counts[w] += 1
+        copy.start()
+
+    def arrive(w, piece, core=0):
+        i, a, b = piece
+        target = full_refs[w].at[place.block(by_rows[w], i, a, b, core)]
+        sems = core_sems if core else link_sems
+        name = i * 4 + a * 2 + b
+        send(
+            target, target, send_sems.at[w, 0], sems.at[w, name], place.device(core=1)
+        ).wait_recv()
+        return target
+
+    def begin():
+        greet(place)
+        for w in weights:
+            local = pltpu.make_async_copy(
+                own_refs[w], full_refs[w].at[place.block(by_rows[w], 0, 0, 0)], local_sems.at[w]
+            )
+            local.start()
+            own = (0, 0, 0)
+            for step in (1, 3, 2):
+                forward(w, own_refs[w], own, i=step)
+            forward(w, own_refs[w], own, b=1)
+            forward(w, own_refs[w], own, a=1)
+            forward(w, own_refs[w], own, core=1)
+
+    def pass_on(w, i, a, b):
+        def step():
+            piece = (i, a, b)
+            source = arrive(w, piece)
+            if not a and not b:
+                forward(w, source, piece, b=1)
+                forward(w, source, piece, a=1)
+            elif a and not b and i in VIA_X:
+                forward(w, source, piece, b=1)
+            elif b and not a and i not in VIA_X:
+                forward(w, source, piece, a=1)
+            forward(w, source, piece, core=1)
+
+        return step
+
+    steps = [begin]
+    for w in weights:
+        order = [(1, 0, 0), (0, 1, 0), (0, 0, 1), (3, 0, 0), (1, 0, 1), (1, 1, 0), (2, 0, 0)]
+        order += [(3, 1, 0), (3, 0, 1), (2, 0, 1), (2, 1, 0), (0, 1, 1), (1, 1, 1), (3, 1, 1), (2, 1, 1)]
+        steps += [pass_on(w, *piece) for piece in order]
+
+    def finish():
+        for w in weights:
+            for i in range(4):
+                for a in range(2):
+                    for b in range(2):
+                        arrive(w, (i, a, b), core=1)
+            pltpu.make_async_copy(
+                own_refs[w], full_refs[w].at[place.block(by_rows[w], 0, 0, 0)], local_sems.at[w]
+            ).wait()
+            for n in range(counts[w]):
+                send(
+                    own_refs[w], own_refs[w], send_sems.at[w, n], link_sems.at[w, 0],
+                    place.device(core=1),
+                ).wait_send()
+
+    return steps + [finish]
+
+
+def gather_kernel(by_rows, *refs):
+    count = len(by_rows)
+    own_refs, full_refs = refs[:count], refs[count : 2 * count]
+    place = Place()
+    for step in gather_actions(place, by_rows, own_refs, full_refs, *refs[2 * count :]):
+        step()
+
+
+def gather_scratch(count):
+    return [
+        pltpu.SemaphoreType.DMA((count,)),
+        pltpu.SemaphoreType.DMA((count, GATHER_SENDS)),
+        pltpu.SemaphoreType.DMA((count, 16)),
+        pltpu.SemaphoreType.DMA((count, 16)),
+    ]
+
+
+def gather_blocks(blocks, by_rows, collective_id):
+    count = len(blocks)
+    whole = jax.ShapeDtypeStruct((8 * BLOCK_ROWS, 4 * BLOCK_COLS), jnp.bfloat16)
+    return pl.pallas_call(
+        functools.partial(gather_kernel, by_rows),
+        in_specs=[pl.BlockSpec(memory_space=pltpu.VMEM)] * count,
+        out_specs=[pl.BlockSpec(memory_space=pl.ANY)] * count,
+        out_shape=[whole] * count,
+        scratch_shapes=gather_scratch(count),
+        compiler_params=pltpu.CompilerParams(
+            collective_id=collective_id, has_side_effects=True, vmem_limit_bytes=VMEM_LIMIT
+        ),
+        name="gather_blocks",
+    )(*blocks)
+
+
+SCATTER_SENDS = 16 + 6 + 6 + 3
+
+
+def scatter_actions(
+    place,
+    by_rows,
+    grad_refs,
+    out_refs,
+    held_refs,
+    over_x,
+    over_y,
+    over_z,
+    stage,
+    stage_sems,
+    send_sems,
+    held_sems,
+    x_sems,
+    y_sems,
+    z_sems,
+):
+    weights = range(len(grad_refs))
+    counts = [0] * len(grad_refs)
+    chips = [(i, a, b) for i in (1, 3, 2, 0) for a, b in ((1, 1), (0, 1), (1, 0), (0, 0))]
+    slot = lambda i, a, b: i * 4 + a * 2 + b
+
+    def ship(w, source, target, recv_sem, device):
+        copy = send(source, target, send_sems.at[w, counts[w]], recv_sem, device)
+        counts[w] += 1
+        copy.start()
+
+    def landed(target, recv_sem):
+        send(target, target, send_sems.at[0, 0], recv_sem, place.device(core=1)).wait_recv()
+
+    def begin():
+        greet(place)
+        for w in weights:
+            for i, a, b in chips:
+                source = grad_refs[w].at[place.block(by_rows[w], i, a, b, core=1)]
+                s = slot(i, a, b)
+                ship(w, source, held_refs.at[w, s], held_sems.at[w, s], place.device(core=1))
+
+    order = [(w, chip) for w in weights for chip in chips]
+
+    def load(n):
+        w, (i, a, b) = order[n]
+        return pltpu.make_async_copy(
+            grad_refs[w].at[place.block(by_rows[w], i, a, b)], stage.at[n % 4], stage_sems.at[n % 4]
+        )
+
+    def fold(n):
+        def step():
+            if n == 0:
+                for ahead in range(3):
+                    load(ahead).start()
+            if n + 3 < len(order):
+                load(n + 3).start()
+            w, (i, a, b) = order[n]
+            s = slot(i, a, b)
+            load(n).wait()
+            landed(held_refs.at[w, s], held_sems.at[w, s])
+            held = held_refs.at[w, s]
+            held[...] = held[...] + stage[n % 4]
+            via_x = i in VIA_X
+            if a and b:
+                if via_x:
+                    ship(w, held, over_x.at[w, 4 + VIA_X.index(i)], x_sems.at[w, 4 + VIA_X.index(i)], place.device(b=1))
+                else:
+                    k = 4 + (i - 1)
+                    ship(w, held, over_y.at[w, k], y_sems.at[w, k], place.device(a=1))
+            elif b and via_x:
+                ship(w, held, over_x.at[w, i], x_sems.at[w, i], place.device(b=1))
+            elif a and not via_x:
+                ship(w, held, over_y.at[w, i], y_sems.at[w, i], place.device(a=1))
+
+        return step
+
+    def second(w, i):
+        def step():
+            if i in VIA_X:
+                k = 4 + VIA_X.index(i)
+                landed(over_x.at[w, k], x_sems.at[w, k])
+                held = held_refs.at[w, slot(i, 1, 0)]
+                held[...] = held[...] + over_x[w, k]
+                ship(w, held, over_y.at[w, i], y_sems.at[w, i], place.device(a=1))
+            else:
+                k = 4 + (i - 1)
+                landed(over_y.at[w, k], y_sems.at[w, k])
+                held = held_refs.at[w, slot(i, 0, 1)]
+                held[...] = held[...] + over_y[w, k]
+                ship(w, held, over_x.at[w, i], x_sems.at[w, i], place.device(b=1))
+
+        return step
+
+    def third(w, i):
+        def step():
+            landed(over_x.at[w, i], x_sems.at[w, i])
+            landed(over_y.at[w, i], y_sems.at[w, i])
+            held = held_refs.at[w, slot(i, 0, 0)]
+            total = held[...].astype(jnp.float32) + over_x[w, i].astype(jnp.float32)
+            total = total + over_y[w, i].astype(jnp.float32)
+            held[...] = total.astype(jnp.bfloat16)
+            if i:
+                ship(w, held, over_z.at[w, i - 1], z_sems.at[w, i - 1], place.device(i=i))
+
+        return step
+
+    def last(w):
+        def step():
+            total = held_refs[w, 0].astype(jnp.float32)
+            for i in (1, 3, 2):
+                landed(over_z.at[w, i - 1], z_sems.at[w, i - 1])
+                total = total + over_z[w, i - 1].astype(jnp.float32)
+            out_refs[w][...] = total
+
+        return step
+
+    def finish():
+        for w in weights:
+            block = held_refs.at[w, 0]
+            for n in range(counts[w]):
+                send(
+                    block, block, send_sems.at[w, n], held_sems.at[w, 0], place.device(core=1)
+                ).wait_send()
+
+    steps = [begin]
+    per = len(chips)
+    for w in weights:
+        for n in range(per):
+            steps.append(fold(w * per + n))
+            if n == 11:
+                steps.append(second(w, 1))
+        for i in (3, 2, 0):
+            steps.append(second(w, i))
+        for i in (1, 3, 2, 0):
+            steps.append(third(w, i))
+    for w in weights:
+        steps.append(last(w))
+    return steps + [finish]
+
+
+def scatter_scratch(count):
+    blocks = lambda n: pltpu.VMEM((count, n, BLOCK_ROWS, BLOCK_COLS), jnp.bfloat16)
+    return [
+        blocks(16),
+        blocks(6),
+        blocks(6),
+        blocks(3),
+        pltpu.VMEM((4, BLOCK_ROWS, BLOCK_COLS), jnp.bfloat16),
+        pltpu.SemaphoreType.DMA((4,)),
+        pltpu.SemaphoreType.DMA((count, SCATTER_SENDS)),
+        pltpu.SemaphoreType.DMA((count, 16)),
+        pltpu.SemaphoreType.DMA((count, 6)),
+        pltpu.SemaphoreType.DMA((count, 6)),
+        pltpu.SemaphoreType.DMA((count, 3)),
+    ]
+
+
+def scatter_kernel(by_rows, *refs):
+    count = len(by_rows)
+    place = Place()
+    for step in scatter_actions(
+        place, by_rows, refs[:count], refs[count : 2 * count], *refs[2 * count :]
+    ):
+        step()
+
+
+def scatter_blocks(grads, by_rows, collective_id):
+    count = len(grads)
+    block = jax.ShapeDtypeStruct((BLOCK_ROWS, BLOCK_COLS), jnp.float32)
+    return pl.pallas_call(
+        functools.partial(scatter_kernel, by_rows),
+        in_specs=[pl.BlockSpec(memory_space=pl.ANY)] * count,
+        out_specs=[pl.BlockSpec(memory_space=pltpu.VMEM)] * count,
+        out_shape=[block] * count,
+        scratch_shapes=scatter_scratch(count),
+        compiler_params=pltpu.CompilerParams(
+            collective_id=collective_id, has_side_effects=True, vmem_limit_bytes=VMEM_LIMIT
+        ),
+        name="scatter_blocks",
+    )(*grads)
+
+
+def project_kernel(hidden_ref, weight_ref, out_ref):
+    rows = out_ref.shape[0]
+    span = -(-rows // 128) * 128
+    wide = dot_nn(hidden_ref[...], weight_ref[:, :span]).astype(jnp.bfloat16)
+    out_ref[...] = jnp.transpose(wide)[:rows]
+
+
+def project_qkv(hidden, weights):
+    tokens, width = hidden.shape
+    groups = weights.shape[1] // BLOCK_COLS
+    rows = 3 * D // groups
+    return pl.pallas_call(
+        project_kernel,
+        grid=(groups,),
+        in_specs=[
+            pl.BlockSpec((tokens, width), lambda g: (0, 0)),
+            pl.BlockSpec((width, BLOCK_COLS), lambda g: (0, g)),
+        ],
+        out_specs=pl.BlockSpec((rows, tokens), lambda g: (g, 0)),
+        out_shape=jax.ShapeDtypeStruct((groups * rows, tokens), jnp.bfloat16),
+        compiler_params=pltpu.CompilerParams(vmem_limit_bytes=VMEM_LIMIT),
+        name="project_qkv",
+    )(hidden, weights)
+
+
+def project_back_kernel(hidden_t_ref, weight_ref, grad_ref, proj_ref, grad_hidden_ref, out_ref):
+    group = pl.program_id(0)
+    rows = grad_ref.shape[0]
+    proj_cols = BLOCK_COLS - rows
+    grad = grad_ref[...]
+
+    @pl.when(group == 0)
+    def _():
+        grad_hidden_ref[...] = jnp.zeros_like(grad_hidden_ref)
+
+    grad_hidden_ref[...] += dot_nt(jnp.transpose(grad), weight_ref[:, :rows])
+    out_ref[:, :rows] = dot_nt(hidden_t_ref[...], grad).astype(jnp.bfloat16)
+    for g in range(D // proj_cols):
+
+        @pl.when(group == g)
+        def _():
+            out_ref[:, rows:] = proj_ref[:, g * proj_cols : (g + 1) * proj_cols]
+
+
+def project_back(hidden_t, weights, grad, grad_proj):
+    width, tokens = hidden_t.shape
+    groups = weights.shape[1] // BLOCK_COLS
+    rows = grad.shape[0] // groups
+    return pl.pallas_call(
+        project_back_kernel,
+        grid=(groups,),
+        in_specs=[
+            pl.BlockSpec((width, tokens), lambda g: (0, 0)),
+            pl.BlockSpec((width, BLOCK_COLS), lambda g: (0, g)),
+            pl.BlockSpec((rows, tokens), lambda g: (g, 0)),
+            pl.BlockSpec((width, D), lambda g: (0, 0)),
+        ],
+        out_specs=[
+            pl.BlockSpec((tokens, width), lambda g: (0, 0)),
+            pl.BlockSpec((width, BLOCK_COLS), lambda g: (0, g)),
+        ],
+        out_shape=[
+            jax.ShapeDtypeStruct((tokens, width), jnp.float32),
+            jax.ShapeDtypeStruct(weights.shape, jnp.bfloat16),
+        ],
+        compiler_params=pltpu.CompilerParams(vmem_limit_bytes=VMEM_LIMIT),
+        name="project_back",
+    )(hidden_t, weights, grad, grad_proj)
+
+
+def swap_columns(shard):
+    pairs = [(d, d ^ 1) for d in range(lax.axis_size("dp"))]
+    odd = lax.axis_index("dp") % 2
+    rows = shard.shape[0] // 2
+    own = lax.dynamic_slice_in_dim(shard, odd * rows, rows, axis=0)
+    other = lax.dynamic_slice_in_dim(shard, (1 - odd) * rows, rows, axis=0)
+    other = lax.ppermute(other, "dp", pairs)
+    return jnp.where(odd == 0, jnp.stack([own, other], 1), jnp.stack([other, own], 1))
+
+
+def swap_rows(block):
+    pairs = [(d, d ^ 1) for d in range(lax.axis_size("dp"))]
+    odd = lax.axis_index("dp") % 2
+    own = lax.dynamic_index_in_dim(block, odd, axis=1, keepdims=False)
+    other = lax.dynamic_index_in_dim(block, 1 - odd, axis=1, keepdims=False)
+    other = lax.ppermute(other, "dp", pairs)
+    return jnp.where(odd == 0, jnp.concatenate([own, other], 0), jnp.concatenate([other, own], 0))
 
 
 def swap_slots(values):
@@ -679,16 +1129,23 @@
     tokens = placed + unfilled * mask_token + grid_embed_slot(kind[0], tokens_count)
     tokens = tokens.reshape(regions, REGION, D)
 
-    qkv_full = gather_weight(w_qkv.astype(bf16))
-    proj_full = gather_weight(w_proj.astype(bf16))
-    fc1_full = gather_weight(w_fc1.astype(bf16))
-    fc2_full = gather_weight(w_fc2.astype(bf16).T, "dp", "band")
+    qkv_cols, proj_cols, fc1_cols = w_qkv.shape[1], w_proj.shape[1], w_fc1.shape[1]
+    swapped = swap_columns(jnp.concatenate([w_qkv, w_proj, w_fc1], axis=1).astype(bf16))
+    joined_block = jnp.concatenate(
+        [
+            swapped[:, :, :qkv_cols].reshape(-1, 2 * qkv_cols),
+            swapped[:, :, qkv_cols:-fc1_cols].reshape(-1, 2 * proj_cols),
+        ],
+        axis=1,
+    )
+    fc1_block = swapped[:, :, -fc1_cols:].reshape(-1, 2 * fc1_cols)
+    (joined_full,) = gather_blocks([joined_block], (False,), 0)
+    fc1_full, fc2_full = gather_blocks([fc1_block, w_fc2.astype(bf16).T], (False, True), 1)
+    proj_full = joined_full.reshape(D, -1, BLOCK_COLS)[:, :, 2 * qkv_cols :].reshape(D, D)
 
     normal_attn, root_attn = norm_parts(tokens)
     hidden = (normal_attn * (1.0 + scale_attn) + shift_attn).astype(bf16).reshape(tokens_count, D)
-    qkv = lax.dot_general(
-        qkv_full, hidden, (((0,), (1,)), ((), ())), preferred_element_type=jnp.float32
-    ).astype(bf16)
+    qkv = project_qkv(hidden, joined_full)
     qkv_heads = qkv.reshape(3 * HEADS, HEAD_DIM, tokens_count)
     attended, lse = attn_forward(kind, qkv_heads)
     attended_t = attended.reshape(D, tokens_count)
@@ -721,12 +1178,8 @@
     grad_heads = grad_attended.reshape(HEADS, HEAD_DIM, tokens_count)
     grad_qkv = attn_backward(kind, qkv_heads, attended, grad_heads, lse)
     grad_qkv = grad_qkv.reshape(3 * D, tokens_count)
-    grad_qkv_weight = lax.dot_general(
-        hidden, grad_qkv, (((0,), (1,)), ((), ())), preferred_element_type=jnp.float32
-    ).astype(bf16)
-    grad_hidden = lax.dot_general(
-        grad_qkv, qkv_full, (((0,), (1,)), ((), ())), preferred_element_type=jnp.float32
-    ).reshape(regions, REGION, D)
+    grad_hidden, grad_joined = project_back(hidden.T, joined_full, grad_qkv, grad_proj)
+    grad_hidden = grad_hidden.reshape(regions, REGION, D)
     grad_shift_attn = jnp.sum(grad_hidden, axis=1)
     grad_scale_attn = jnp.sum(grad_hidden * normal_attn, axis=1)
     grad_tokens = grad_middle + norm_back(grad_hidden, normal_attn, root_attn, scale_attn)
@@ -767,11 +1220,21 @@
     ).astype(jnp.float32)
     grad_mask_part = jnp.sum(unfilled * grad_tokens, axis=0)
 
-    red_qkv = scatter_grad(grad_qkv_weight)
-    red_proj = scatter_grad(grad_proj)
-    red_fc1 = scatter_grad(grad_fc1)
-    red_fc2 = scatter_grad(grad_fc2, "dp", "band").T
-
+    sum_fc1, sum_fc2 = scatter_blocks([grad_fc1, grad_fc2], (False, True), 2)
+    (sum_joined,) = scatter_blocks([grad_joined], (False,), 3)
+    sums = jnp.concatenate(
+        [
+            sum_joined[:, : 2 * qkv_cols].reshape(-1, 2, qkv_cols),
+            sum_joined[:, 2 * qkv_cols :].reshape(-1, 2, proj_cols),
+            sum_fc1.reshape(-1, 2, fc1_cols),
+        ],
+        axis=2,
+    )
+    sums = swap_rows(sums.astype(bf16)).astype(jnp.float32)
+    red_qkv = sums[:, :qkv_cols]
+    red_proj = sums[:, qkv_cols:-fc1_cols]
+    red_fc1 = sums[:, -fc1_cols:]
+    red_fc2 = sum_fc2.T
     grad_mask = lax.psum(grad_mask_part, ("dp", "band"))
     reduced = (red_qkv, red_proj, red_fc1, red_fc2, red_ada)
     local_squares = sum((jnp.sum(grad * grad) for grad in reduced))
@@ -790,7 +1253,7 @@
 
 def per_device(*arguments):
     cotangent = arguments[6]
-    if cotangent.shape[0] == lax.axis_size("band"):
+    if (lax.axis_size("dp"), lax.axis_size("band")) == (8, cotangent.shape[0]):
         return slot_device(*arguments)
     return general_device(*arguments)
 

time: 1370 us -> 963 us (0.70)
  waiting for transfers between devices: 736 us -> 13.7 us
  Pallas kernels: 173 us -> 562 us
  blocking collectives: 146 us -> 82.8 us
  matrix products: 85.6 us -> 36.6 us
  local copies, waits for them, and re-layouts: 96.4 us -> 119 us
    pallas_call x0 -> x6, Pallas kernels: none -> 389 us  [the longest x2 195 us: scatter_blocks(): pl.pallas_call(functools.partial(scatter_kernel, by_rows), in_specs=[pl.B...]
    reduce_scatter x4 -> x0, waiting for transfers between devices: 298 us -> none  [scatter_grad(): rows = lax.psum_scatter(grad, row_axis, scatter_dimension=0, tiled=True)]
    all_gather x7 -> x0, waiting for transfers between devices: 204 us -> none  [the longest x4 148 us: gather_weight(): return lax.all_gather(columns, row_axis, axis=0, tiled=True)]
    unnamed x20 -> x1, waiting for transfers between devices: 174 us -> 0.02 us
    all_to_all x3, waiting for transfers between devices: 58.1 us -> 0.01 us  [swap_slots(): lax.all_to_all(values, 'band', split_axis=0, concat_axis=0, tiled=True)]
    dot_general x3 -> x0, matrix products: 49.6 us -> none  [the longest x1 20.6 us: slot_device(): lax.dot_general(grad_qkv, qkv_full, (((0,), (1,)), ((), ())), preferred_e...]
    reshape x0 -> x13, local copies, waits for them, and re-layouts: none -> 36 us  [the longest x1 15.3 us: slot_device(): joined_full.reshape(D, -1, BLOCK_COLS)[:, :, 2 * qkv_cols:].reshape(D, D)]
    all_gather x1 -> x0, blocking collectives: 33.3 us -> none  [gather_weight(): columns = lax.all_gather(shard, column_axis, axis=1, tiled=True)]
  transfers between devices with their start and end apart: 22 -> 10, of which waited for: 14 -> 3; matrix products, arithmetic and copies ran while one was open for 15% -> 18% of each run, Pallas kernels for 7% -> 22%
where the time goes in v2:
time: 963 us; the launch traced here: 950 us
  Pallas kernels  562 us (58%)
  local copies, waits for them, and re-layouts  119 us (12%)
  other arithmetic  82.8 us (9%)
  blocking collectives  82.8 us (9%)
  matrix products  36.6 us (4%)
  starting transfers between devices  31.9 us (3%)
  between operations  21.4 us (2%)
  waiting for transfers between devices  13.7 us (1%)
    pallas_call x2, Pallas kernels, scatter_blocks(): pl.pallas_call(functools.partial(scatter_kernel, by_rows), in_specs=[pl.B...  195 us
    pallas_call x2, Pallas kernels, gather_blocks(): pl.pallas_call(functools.partial(gather_kernel, by_rows), in_specs=[pl.Bl...  149 us
    pallas_call x1, Pallas kernels, mlp_both(): pl.pallas_call(mlp_kernel, grid=(wide // tile,), in_specs=[whole((tokens,...  79.1 us
    pallas_call x1, Pallas kernels, attn_backward(): pl.pallas_call(attn_back_kernel, grid=(HEADS,), in_specs=[pl.BlockSpec(me...  48.3 us
    pallas_call x1, Pallas kernels, attn_forward(): pl.pallas_call(attn_kernel, grid=(HEADS,), in_specs=[pl.BlockSpec(memory_...  45.4 us
    psum x1, blocking collectives, slot_device(): lax.psum(local_squares, ('dp', 'band')) + jnp.sum(grad_mask * grad_mask)  37.7 us
    unnamed x67, local copies, waits for them, and re-layouts  33.9 us
    pallas_call x1, Pallas kernels, project_back(): pl.pallas_call(project_back_kernel, grid=(groups,), in_specs=[pl.BlockSpe...  30 us
  transfers between devices with their start and end apart: 10, of which 3 were waited for; matrix products, arithmetic and copies ran while one was open for 18% of the time, Pallas kernels for 22%

profile of v2, /device:TPU:0, one launch (start us, length us, event | category | flops | bytes accessed | tf_op | source)
XLA Modules:
  0.0 949.8 jit_solution(16523339807327093786)
XLA Ops:
  12.4 26.9 %all-gather = s32[8,4,8]{2,1,0:T(4,128)S(1)} all-gather(s32[1,4,8]{2,1,0:T(4,128)S(1)} %add_bitcast_fusion), channel_id=1, replica_groups=mesh['dp'=8,'band'=4] {'dp'}, dimensions={0}, use_global_device_ids=true | all-gather | bytes 1152 | tf_op jit(solution)/shard_map/all_gather | solution.py:1094
  64.4 6.1 copy.291
  70.5 6.3 copy.292
  88.3 52.5 %gather_blocks.2.weight_ref = bf16[1152,4608]{1,0:T(8,128)(2,1)} custom-call(bf16[144,1152]{1,0:T(8,128)(2,1)} %pad_maximum_fusion.2.refs_0_), custom_call_target="tpu_custom_call" | custom-call | tf_op jit(solution)/shard_map/gather_blocks/pallas_call | solution.py:722
  140.8 15.3 %copy.342 = bf16[1152,4608]{0,1:T(8,128)(2,1)} copy(bf16[1152,4608]{1,0:T(8,128)(2,1)} %gather_blocks.2.weight_ref) | data formatting | bytes 21233664 | tf_op jit(solution)/shard_map/reshape | solution.py:1144
  160.9 96.4 %gather_blocks.3 = (bf16[1152,4608]{1,0:T(8,128)(2,1)}, bf16[1152,4608]{1,0:T(8,128)(2,1)}) custom-call(bf16[144,1152]{1,0:T(8,128)(2,1)} %reshape.308.refs_0_, bf16[144,1152]{1,0:T(8,128)(2,1)} %convert_bitcast_fusion.refs_1_), custom_call_target="tpu_custom_call" | custom-call | tf_op jit(solution)/shard_map/gather_blocks/pallas_call | solution.py:722
  257.3 6.5 fusion.47
  263.8 6.1 copy.346
  279.4 7.3 all-to-all-done.2
  304.8 8.4 add_convert_fusion.2
  317.4 15.3 %project_qkv.1 = bf16[3456,1024]{1,0:T(8,128)(2,1)} custom-call(bf16[1024,1152]{1,0:T(8,128)(2,1)} %copy.302.hidden_ref, bf16[1152,4608]{1,0:T(8,128)(2,1)} %gather_blocks.2.weight_ref), custom_call_target="tpu_custom_call" | custom-call | tf_op jit(solution)/shard_map/project_qkv/pallas_call | solution.py:928
  332.7 45.4 %attn_forward.1 = (bf16[16,72,1024]{2,1,0:T(8,128)(2,1)}, f32[16,1,1024]{2,1,0:T(1,128)}) custom-call(s32[1]{0:T(128)} %dynamic_slice.19.kind_ref, bf16[48,72,1024]{2,1,0:T(8,128)(2,1)} %bitcast.89, bf16[48,72,1024]{2,1,0:T(8,128)(2,1)} %bitcast.90, bf16[48,72,1024]{2,1,0:T(8,128)(2,1)} %bitcast.91), custom_call_target="tpu_custom_call" | custom-call | tf_op jit(solution)/shard_map/attn_forward/pallas_call | solution.py:416
  382.4 9.7 %fusion.45 = (f32[4,256]{1,0:T(4,128)S(1)}, f32[4,256,1152]{2,1,0:T(8,128)S(1)}, f32[4,256,1152]{2,1,0:T(8,128)}) fusion(f32[4,256,1152]{2,1,0:T(8,128)} %bitcast.102, f32[4,1152]{1,0:T(4,128)S(1)} %get-tuple-element.257, bf16[4,256,1152]{2,1,0:T(8,128)(2,1)} %bitcast.118, bf16[1152,1152,1]{0,1,2:T(8,128)(2,1)} %bitcast.114), kind=kOutput, calls=%fused_computation.135 | convolution fusion | flops 2721446912 | bytes 19191808 | tf_op jit(solution)/shard_map/dot_general | solution.py:1152
  406.7 79.1 %mlp_both.1 = (f32[1024,1152]{1,0:T(8,128)}, f32[1024,1152]{1,0:T(8,128)}, bf16[1152,4608]{1,0:T(8,128)(2,1)}, bf16[1152,4608]{1,0:T(8,128)(2,1)}) custom-call(bf16[1024,1152]{1,0:T(8,128)(2,1)} %bitcast.101, bf16[1152,1024]{1,0:T(8,128)(2,1)} %bitcast.111, bf16[1024,1152]{1,0:T(8,128)(2,1)} %bitcast.99, bf16[1152,1024]{1,0:T(8,128)(2,1)} %bitcast.112, ...), custom_call_target="tpu_custom_call" | custom-call | tf_op jit(solution)/shard_map/mlp_both/pallas_call | solution.py:524
  492.8 9.4 multiply_reduce_fusion.1
  515.0 48.3 %attn_backward.1 = bf16[3,16,72,1024]{3,2,1,0:T(8,128)(2,1)} custom-call(s32[1]{0:T(128)} %dynamic_slice.19.kind_ref, bf16[48,72,1024]{2,1,0:T(8,128)(2,1)} %bitcast.92, bf16[48,72,1024]{2,1,0:T(8,128)(2,1)} %bitcast.93, bf16[48,72,1024]{2,1,0:T(8,128)(2,1)} %bitcast.94, bf16[16,72,1024]{2,1,0:T(8,128)(2,1)} %get-tuple-element.33.out_ref, ...), custom_call_target="tpu_custom_call" | custom-call | tf_op jit(solution)/shard_map/attn_backward/pallas_call | solution.py:471
  563.3 30.0 %project_back.1 = (f32[1024,1152]{1,0:T(8,128)}, bf16[1152,4608]{1,0:T(8,128)(2,1)}) custom-call(bf16[1152,1024]{1,0:T(8,128)(2,1)} %bitcast.97, bf16[1152,4608]{1,0:T(8,128)(2,1)} %gather_blocks.2.weight_ref, bf16[3456,1024]{1,0:T(8,128)(2,1)} %bitcast.96, bf16[1152,1152]{1,0:T(8,128)(2,1)} %convolution_convert_fusion.proj_ref), custom_call_target="tpu_custom_call" | custom-call | tf_op jit(solution)/shard_map/project_back/pallas_call | solution.py:965
  593.3 72.3 %scatter_blocks.2 = f32[144,1152]{1,0:T(8,128)} custom-call(bf16[1152,4608]{1,0:T(8,128)(2,1)} %get-tuple-element.40.refs_0_), custom_call_target="tpu_custom_call" | custom-call | tf_op jit(solution)/shard_map/scatter_blocks/pallas_call | solution.py:904
  666.8 6.5 copy.312
  673.3 6.7 multiply_reduce_fusion.6
  680.1 6.5 fusion.3
  689.7 122.3 %scatter_blocks.3 = (f32[144,1152]{1,0:T(8,128)}, f32[144,1152]{1,0:T(8,128)}) custom-call(bf16[1152,4608]{1,0:T(8,128)(2,1)} %get-tuple-element.41.refs_0_, bf16[1152,4608]{1,0:T(8,128)(2,1)} %get-tuple-element.42.refs_1_), custom_call_target="tpu_custom_call" | custom-call | tf_op jit(solution)/shard_map/scatter_blocks/pallas_call | solution.py:904
  830.5 18.2 %all_gather.7 = f32[8,16,864]{2,0,1:T(8,128)S(1)} all-gather(f32[8,4,864]{2,0,1:T(8,128)S(1)} %copy.322), channel_id=1, replica_groups=mesh['dp'=8,'band'=4] {'band'}, dimensions={1}, use_global_device_ids=true | all-gather | bytes 552960 | tf_op jit(solution)/shard_map/all_gather | solution.py:1205
  860.3 37.7 %all-reduce = (f32[]{:T(128)}, f32[1152]{0:T(1024)S(1)}) all-reduce(f32[]{:T(128)S(6)} %add.258, f32[1152]{0:T(1024)S(1)} %get-tuple-element.260), channel_id=1, replica_groups=mesh['dp'=8,'band'=4] {'dp','band'}, use_global_device_ids=true, to_apply=%region_22.23 | all-reduce | flops 1153 | bytes 9224 | tf_op jit(solution)/shard_map/psum | solution.py:1241
  (205 shorter events, 189.3 us)
Async XLA Ops:
  7.2 39.0 %copy-start.10 = (f32[288,432]{1,0:T(8,128)S(1)}, f32[288,432]{1,0:T(8,128)}, u32[]{:S(2)}) copy-start(f32[288,432]{1,0:T(8,128)} %param.33) | copy-start | bytes 1492996
  7.2 40.1 %copy-start.4 = (f32[288,576]{1,0:T(8,128)S(1)}, f32[288,576]{1,0:T(8,128)}, u32[]{:S(2)}) copy-start(f32[288,576]{1,0:T(8,128)} %param.35) | copy-start | bytes 1990660
  7.2 51.1 %all-to-all-start = ((s32[4,1,128]{2,1,0:T(1,128)}), s32[4,1,128]{2,1,0:T(1,128)S(1)}, u32[]{:S(2)}, u32[]{:S(2)}) async-start(s32[4,1,128]{2,1,0:T(1,128)} %bitcast.131), calls=%async_computation | async-start | bytes 4096 | tf_op jit(solution)/shard_map/all_to_all | solution.py:1007
  11.6 261.2 %reduce-scatter.2.cloned.1.call-start = ((), (), s32[]{:S(2)}) async-start(), calls=%async_computation.8 | async-start | bytes 573440 | tf_op jit(solution)/shard_map/reduce_scatter | solution.py:1112
  43.4 7.2 copy-start.5
  48.7 36.4 %collective-permute-start = (bf16[144,1152]{1,0:T(8,128)(2,1)}, bf16[144,1152]{1,0:T(8,128)(2,1)}, u32[]{:S(2)}, u32[]{:S(2)}) collective-permute-start(bf16[144,1152]{1,0:T(8,128)(2,1)} %get-tuple-element.251), channel_id=1, source_target_pairs={{0,4},{4,0},{8,12},{12,8},{16,20},{20,16},{24,28},{28,24},{1,5},{5... | collective-permute-start | bytes 995336 | tf_op jit(solution)/shard_map/ppermute | solution.py:993
  58.3 199.0 %all-to-all-start.1 = ((bf16[4,128,1152]{2,1,0:T(8,128)(2,1)}), bf16[4,128,1152]{2,1,0:T(8,128)(2,1)S(1)}, u32[]{:S(2)}, u32[]{:S(2)}) async-start(bf16[4,128,1152]{2,1,0:T(8,128)(2,1)} %param.25), calls=%async_computation.1 | async-start | bytes 2359296 | tf_op jit(solution)/shard_map/all_to_all | solution.py:1007
  70.5 10.6 %copy-start.13 = (f32[288,576]{1,0:T(8,128)S(1)}, f32[288,576]{1,0:T(8,128)}, u32[]{:S(2)}) copy-start(f32[288,576]{1,0:T(8,128)} %param.41) | copy-start | bytes 1990660
  70.5 11.8 %copy-start.14 = (f32[288,576]{1,0:T(8,128)S(1)}, f32[288,576]{1,0:T(8,128)}, u32[]{:S(2)}) copy-start(f32[288,576]{1,0:T(8,128)} %param.47) | copy-start | bytes 1990660
  156.1 101.2 %copy-start.20 = (f32[1152]{0:T(1024)S(1)}, f32[1152]{0:T(1024)}, u32[]{:S(2)}) copy-start(f32[1152]{0:T(1024)} %param.32) | copy-start | bytes 13828
  274.4 12.4 %all-to-all-start.2 = ((f32[8,4,864]{2,1,0:T(4,128)}), f32[8,4,864]{2,1,0:T(4,128)S(1)}, u32[]{:S(2)}, u32[]{:S(2)}) async-start(f32[8,4,864]{2,1,0:T(4,128)} %copy.295), calls=%async_computation.3 | async-start | bytes 229376 | tf_op jit(solution)/shard_map/all_to_all | solution.py:1113
  286.8 113.8 %all-to-all-start.3 = ((bf16[4,256,1152]{2,1,0:T(8,128)(2,1)}), bf16[4,256,1152]{2,1,0:T(8,128)(2,1)S(1)}, u32[]{:S(2)}, u32[]{:S(2)}) async-start(bf16[4,256,1152]{2,1,0:T(8,128)(2,1)} %param.31), calls=%async_computation.4 | async-start | bytes 4718592 | tf_op jit(solution)/shard_map/all_to_all | solution.py:1007
  502.2 8.0 copy-start.2
  812.0 9.6 %copy-start.7 = (f32[144,1152]{1,0:T(8,128)S(1)}, f32[144,1152]{1,0:T(8,128)}, u32[]{:S(2)}) copy-start(f32[144,1152]{1,0:T(8,128)} %get-tuple-element.44) | copy-start | bytes 1990660
  814.8 10.7 %all-to-all-start.6 = ((f32[8,4,864]{2,1,0:T(4,128)}), f32[8,4,864]{2,1,0:T(4,128)S(1)}, u32[]{:S(2)}, u32[]{:S(2)}) async-start(f32[8,4,864]{2,1,0:T(4,128)} %copy.321), calls=%async_computation.7 | async-start | bytes 229376 | tf_op jit(solution)/shard_map/all_to_all | solution.py:1204
  819.5 32.4 %collective-permute-start.1 = (bf16[144,1152]{1,0:T(8,128)(2,1)}, bf16[144,1152]{1,0:T(8,128)(2,1)S(1)}, u32[]{:S(2)}, u32[]{:S(2)}) collective-permute-start(bf16[144,1152]{1,0:T(8,128)(2,1)} %get-tuple-element.249), channel_id=1, source_target_pairs={{0,4},{4,0},{8,12},{12,8},{16,20},{20,16},{24,28},{28,24},{1,5},{5... | collective-permute-start | bytes 995336 | tf_op jit(solution)/shard_map/ppermute | solution.py:1002
  826.1 79.2 %all-to-all-start.5 = ((bf16[4,128,1152]{2,1,0:T(8,128)(2,1)}), bf16[4,128,1152]{2,1,0:T(8,128)(2,1)S(1)}, u32[]{:S(2)}, u32[]{:S(2)}) async-start(bf16[4,128,1152]{2,1,0:T(8,128)(2,1)} %bitcast.123), calls=%async_computation.6 | async-start | bytes 2359296 | tf_op jit(solution)/shard_map/all_to_all | solution.py:1218
  905.3 33.1 %all-to-all-start.4 = ((bf16[4,256,1152]{2,1,0:T(8,128)(2,1)}), bf16[4,256,1152]{2,1,0:T(8,128)(2,1)}, u32[]{:S(2)}, u32[]{:S(2)}) async-start(bf16[4,256,1152]{2,1,0:T(8,128)(2,1)} %get-tuple-element.246), calls=%async_computation.5 | async-start | bytes 4718592 | tf_op jit(solution)/shard_map/all_to_all | solution.py:1167
  913.4 11.4 %copy-start.21 = (f32[1152]{0:T(1024)S(1)}, f32[1152]{0:T(1024)}, u32[]{:S(2)}) copy-start(f32[1152]{0:T(1024)} %param.38) | copy-start | bytes 13828
  913.4 11.4 %copy-start.22 = (f32[1152]{0:T(1024)S(1)}, f32[1152]{0:T(1024)}, u32[]{:S(2)}) copy-start(f32[1152]{0:T(1024)} %param.44) | copy-start | bytes 13828
  913.4 12.0 %copy-start.12 = (f32[288,144]{0,1:T(8,128)S(1)}, f32[288,144]{0,1:T(8,128)}, u32[]{:S(2)}) copy-start(f32[288,144]{0,1:T(8,128)} %param.34) | copy-start | bytes 497668
  913.4 12.0 %copy-start.19 = (f32[288,144]{0,1:T(8,128)S(1)}, f32[288,144]{0,1:T(8,128)}, u32[]{:S(2)}) copy-start(f32[288,144]{0,1:T(8,128)} %param.40) | copy-start | bytes 497668
  924.8 7.0 copy-start.6
  924.8 7.0 copy-start.8
  (11 other events, 50.5 us)
Sparse Core Ops, SparseCore 0:
  46.2 22.5 reduce-scatter.1

commit v3 on v2

--- a/solution.py
+++ b/solution.py
@@ -387,7 +387,7 @@
     )
 
 
-def attn_kernel(kind_ref, q_ref, k_ref, v_ref, out_ref, lse_ref):
+def attn_head(kind_ref, q_ref, k_ref, v_ref, out_ref, lse_ref):
     tokens = q_ref.shape[2]
     regions = tokens // REGION
     other = jnp.where(kind_ref[0] == 1, MASKED, 0.0)
@@ -408,26 +408,7 @@
         lse_ref[0, :, cols] = peak * (SCORE_SCALE * LOG2E) + jnp.log2(total)
 
 
-def attn_forward(kind, qkv_heads):
-    tokens = qkv_heads.shape[2]
-    head = lambda part: pl.BlockSpec(
-        (1, HEAD_DIM, tokens), lambda h: (h + part * HEADS, 0, 0)
-    )
-    return pl.pallas_call(
-        attn_kernel,
-        grid=(HEADS,),
-        in_specs=[pl.BlockSpec(memory_space=pltpu.SMEM), head(0), head(1), head(2)],
-        out_specs=[head(0), pl.BlockSpec((1, 1, tokens), lambda h: (h, 0, 0))],
-        out_shape=[
-            jax.ShapeDtypeStruct((HEADS, HEAD_DIM, tokens), jnp.bfloat16),
-            jax.ShapeDtypeStruct((HEADS, 1, tokens), jnp.float32),
-        ],
-        compiler_params=pltpu.CompilerParams(vmem_limit_bytes=VMEM_LIMIT),
-        name="attn_forward",
-    )(kind, qkv_heads, qkv_heads, qkv_heads)
-
-
-def attn_back_kernel(kind_ref, q_ref, k_ref, v_ref, out_ref, grad_ref, lse_ref, grads_ref):
+def attn_head_back(kind_ref, q_ref, k_ref, v_ref, out_ref, grad_ref, lse_ref, grads_ref):
     tokens = q_ref.shape[2]
     regions = tokens // REGION
     other = jnp.where(kind_ref[0] == 1, MASKED, 0.0)
@@ -463,30 +444,6 @@
     grads_ref[2, 0] = grad_values.astype(jnp.bfloat16)
 
 
-def attn_backward(kind, qkv_heads, attended, grad_attended, lse):
-    tokens = qkv_heads.shape[2]
-    head = lambda part: pl.BlockSpec(
-        (1, HEAD_DIM, tokens), lambda h: (h + part * HEADS, 0, 0)
-    )
-    return pl.pallas_call(
-        attn_back_kernel,
-        grid=(HEADS,),
-        in_specs=[
-            pl.BlockSpec(memory_space=pltpu.SMEM),
-            head(0),
-            head(1),
-            head(2),
-            head(0),
-            head(0),
-            pl.BlockSpec((1, 1, tokens), lambda h: (h, 0, 0)),
-        ],
-        out_specs=pl.BlockSpec((3, 1, HEAD_DIM, tokens), lambda h: (0, h, 0, 0)),
-        out_shape=jax.ShapeDtypeStruct((3, HEADS, HEAD_DIM, tokens), jnp.bfloat16),
-        compiler_params=pltpu.CompilerParams(vmem_limit_bytes=VMEM_LIMIT),
-        name="attn_backward",
-    )(kind, qkv_heads, qkv_heads, qkv_heads, attended, grad_attended, lse)
-
-
 GELU_A = math.sqrt(2.0 / math.pi)
 GELU_B = 0.044715
 
@@ -912,6 +869,100 @@
         ),
         name="scatter_blocks",
     )(*grads)
+
+
+def spread(actions, steps):
+    middle = actions[1:-1]
+    groups = [[] for _ in range(steps)]
+    groups[0].append(actions[0])
+    for n, action in enumerate(middle):
+        groups[1 + n * (steps - 1) // len(middle)].append(action)
+    return groups, actions[-1]
+
+
+def run_actions(actions, steps, compute):
+    step = pl.program_id(0)
+    groups, finish = spread(actions, steps)
+    for n, group in enumerate(groups):
+
+        @pl.when(step == n)
+        def _():
+            for action in group:
+                action()
+
+    compute()
+    pl.when(step == steps - 1)(finish)
+
+
+def head_spec(part, tokens):
+    return pl.BlockSpec((1, HEAD_DIM, tokens), lambda h: (h + part * HEADS, 0, 0))
+
+
+def attn_gather_kernel(by_rows, *refs):
+    count = len(by_rows)
+    ins, own_refs = refs[:4], refs[4 : 4 + count]
+    outs = refs[4 + count : 6 + count]
+    full_refs = refs[6 + count : 6 + 2 * count]
+    actions = gather_actions(Place(), by_rows, own_refs, full_refs, *refs[6 + 2 * count :])
+    run_actions(actions, HEADS, lambda: attn_head(*ins, *outs))
+
+
+def attn_forward(kind, qkv_heads, blocks, by_rows, collective_id):
+    tokens = qkv_heads.shape[2]
+    count = len(blocks)
+    whole = jax.ShapeDtypeStruct((8 * BLOCK_ROWS, 4 * BLOCK_COLS), jnp.bfloat16)
+    block = pl.BlockSpec((BLOCK_ROWS, BLOCK_COLS), lambda h: (0, 0))
+    return pl.pallas_call(
+        functools.partial(attn_gather_kernel, by_rows),
+        grid=(HEADS,),
+        in_specs=[pl.BlockSpec(memory_space=pltpu.SMEM)]
+        + [head_spec(part, tokens) for part in range(3)]
+        + [block] * count,
+        out_specs=[head_spec(0, tokens), pl.BlockSpec((1, 1, tokens), lambda h: (h, 0, 0))]
+        + [pl.BlockSpec(memory_space=pl.ANY)] * count,
+        out_shape=[
+            jax.ShapeDtypeStruct((HEADS, HEAD_DIM, tokens), jnp.bfloat16),
+            jax.ShapeDtypeStruct((HEADS, 1, tokens), jnp.float32),
+        ]
+        + [whole] * count,
+        scratch_shapes=gather_scratch(count),
+        compiler_params=pltpu.CompilerParams(
+            collective_id=collective_id, has_side_effects=True, vmem_limit_bytes=VMEM_LIMIT
+        ),
+        name="attn_forward",
+    )(kind, qkv_heads, qkv_heads, qkv_heads, *blocks)
+
+
+def attn_scatter_kernel(by_rows, *refs):
+    count = len(by_rows)
+    ins, whole_refs = refs[:7], refs[7 : 7 + count]
+    outs = refs[7 + count : 8 + count]
+    sum_refs = refs[8 + count : 8 + 2 * count]
+    actions = scatter_actions(Place(), by_rows, whole_refs, sum_refs, *refs[8 + 2 * count :])
+    run_actions(actions, HEADS, lambda: attn_head_back(*ins, *outs))
+
+
+def attn_backward(kind, qkv_heads, attended, grad_attended, lse, grads, by_rows, collective_id):
+    tokens = qkv_heads.shape[2]
+    count = len(grads)
+    block = pl.BlockSpec((BLOCK_ROWS, BLOCK_COLS), lambda h: (0, 0))
+    return pl.pallas_call(
+        functools.partial(attn_scatter_kernel, by_rows),
+        grid=(HEADS,),
+        in_specs=[pl.BlockSpec(memory_space=pltpu.SMEM)]
+        + [head_spec(part, tokens) for part in (0, 1, 2, 0, 0)]
+        + [pl.BlockSpec((1, 1, tokens), lambda h: (h, 0, 0))]
+        + [pl.BlockSpec(memory_space=pl.ANY)] * count,
+        out_specs=[pl.BlockSpec((3, 1, HEAD_DIM, tokens), lambda h: (0, h, 0, 0))]
+        + [block] * count,
+        out_shape=[jax.ShapeDtypeStruct((3, HEADS, HEAD_DIM, tokens), jnp.bfloat16)]
+        + [jax.ShapeDtypeStruct((BLOCK_ROWS, BLOCK_COLS), jnp.float32)] * count,
+        scratch_shapes=scatter_scratch(count),
+        compiler_params=pltpu.CompilerParams(
+            collective_id=collective_id, has_side_effects=True, vmem_limit_bytes=VMEM_LIMIT
+        ),
+        name="attn_backward",
+    )(kind, qkv_heads, qkv_heads, qkv_heads, attended, grad_attended, lse, *grads)
 
 
 def project_kernel(hidden_ref, weight_ref, out_ref):
@@ -1140,14 +1191,15 @@
     )
     fc1_block = swapped[:, :, -fc1_cols:].reshape(-1, 2 * fc1_cols)
     (joined_full,) = gather_blocks([joined_block], (False,), 0)
-    fc1_full, fc2_full = gather_blocks([fc1_block, w_fc2.astype(bf16).T], (False, True), 1)
     proj_full = joined_full.reshape(D, -1, BLOCK_COLS)[:, :, 2 * qkv_cols :].reshape(D, D)
 
     normal_attn, root_attn = norm_parts(tokens)
     hidden = (normal_attn * (1.0 + scale_attn) + shift_attn).astype(bf16).reshape(tokens_count, D)
     qkv = project_qkv(hidden, joined_full)
     qkv_heads = qkv.reshape(3 * HEADS, HEAD_DIM, tokens_count)
-    attended, lse = attn_forward(kind, qkv_heads)
+    attended, lse, fc1_full, fc2_full = attn_forward(
+        kind, qkv_heads, [fc1_block, w_fc2.astype(bf16).T], (False, True), 1
+    )
     attended_t = attended.reshape(D, tokens_count)
     branch = lax.dot_general(
         attended_t, proj_full, (((0,), (0,)), ((), ())), preferred_element_type=jnp.float32
@@ -1176,7 +1228,9 @@
     grad_proj = dot_nn(attended_t, grad_branch).astype(bf16)
     grad_attended = dot_nt(proj_full, grad_branch).astype(bf16)
     grad_heads = grad_attended.reshape(HEADS, HEAD_DIM, tokens_count)
-    grad_qkv = attn_backward(kind, qkv_heads, attended, grad_heads, lse)
+    grad_qkv, sum_fc1, sum_fc2 = attn_backward(
+        kind, qkv_heads, attended, grad_heads, lse, [grad_fc1, grad_fc2], (False, True), 2
+    )
     grad_qkv = grad_qkv.reshape(3 * D, tokens_count)
     grad_hidden, grad_joined = project_back(hidden.T, joined_full, grad_qkv, grad_proj)
     grad_hidden = grad_hidden.reshape(regions, REGION, D)
@@ -1220,7 +1274,6 @@
     ).astype(jnp.float32)
     grad_mask_part = jnp.sum(unfilled * grad_tokens, axis=0)
 
-    sum_fc1, sum_fc2 = scatter_blocks([grad_fc1, grad_fc2], (False, True), 2)
     (sum_joined,) = scatter_blocks([grad_joined], (False,), 3)
     sums = jnp.concatenate(
         [

time: 963 us -> 884 us (0.918); the launches traced: 950 us -> 882 us
  Pallas kernels: 562 us -> 484 us
  local copies, waits for them, and re-layouts: 119 us -> 130 us
    pallas_call x2, Pallas kernels: 93.7 us -> 232 us  [the longest x1 131 us: attn_backward(): pl.pallas_call(functools.partial(attn_scatter_kernel, by_rows), grid=(HEA...]
    pallas_call x2 -> x1, Pallas kernels: 195 us -> 74.5 us  [scatter_blocks(): pl.pallas_call(functools.partial(scatter_kernel, by_rows), in_specs=[pl.B...]
    pallas_call x2 -> x1, Pallas kernels: 149 us -> 52.5 us  [gather_blocks(): pl.pallas_call(functools.partial(gather_kernel, by_rows), in_specs=[pl.Bl...]
    dot_general x1, local copies, waits for them, and re-layouts: 4.34 us -> 16.2 us  [slot_device(): lax.dot_general(attended_t, proj_full, (((0,), (0,)), ((), ())), preferre...]
    unnamed x67 -> x69, local copies, waits for them, and re-layouts: 33.9 us -> 34 us
  transfers between devices with their start and end apart: 10 -> 10, of which waited for: 3 -> 3; matrix products, arithmetic and copies ran while one was open for 18% -> 21% of each run, Pallas kernels for 22% -> 19%
where the time goes in v3:
time: 884 us; the launch traced here: 882 us
  Pallas kernels  484 us (55%)
  local copies, waits for them, and re-layouts  130 us (15%)
  blocking collectives  82.9 us (9%)
  other arithmetic  81.7 us (9%)
  matrix products  36.7 us (4%)
  starting transfers between devices  31.1 us (4%)
  between operations  21.5 us (2%)
  waiting for transfers between devices  13.7 us (2%)
    pallas_call x1, Pallas kernels, attn_backward(): pl.pallas_call(functools.partial(attn_scatter_kernel, by_rows), grid=(HEA...  131 us
    pallas_call x1, Pallas kernels, attn_forward(): pl.pallas_call(functools.partial(attn_gather_kernel, by_rows), grid=(HEAD...  101 us
    pallas_call x1, Pallas kernels, mlp_both(): pl.pallas_call(mlp_kernel, grid=(wide // tile,), in_specs=[whole((tokens,...  78.9 us
    pallas_call x1, Pallas kernels, scatter_blocks(): pl.pallas_call(functools.partial(scatter_kernel, by_rows), in_specs=[pl.B...  74.5 us
    pallas_call x1, Pallas kernels, gather_blocks(): pl.pallas_call(functools.partial(gather_kernel, by_rows), in_specs=[pl.Bl...  52.5 us
    psum x1, blocking collectives, slot_device(): lax.psum(local_squares, ('dp', 'band')) + jnp.sum(grad_mask * grad_mask)  37.8 us
    unnamed x69, local copies, waits for them, and re-layouts  34 us
    pallas_call x1, Pallas kernels, project_back(): pl.pallas_call(project_back_kernel, grid=(groups,), in_specs=[pl.BlockSpe...  30.2 us
  transfers between devices with their start and end apart: 10, of which 3 were waited for; matrix products, arithmetic and copies ran while one was open for 21% of the time, Pallas kernels for 19%

profile of v3, /device:TPU:0, one launch (start us, length us, event | category | flops | bytes accessed | tf_op | source)
XLA Modules:
  0.0 881.7 jit_solution(255573251417477936)
XLA Ops:
  12.4 26.9 %all-gather = s32[8,4,8]{2,1,0:T(4,128)S(1)} all-gather(s32[1,4,8]{2,1,0:T(4,128)S(1)} %add_bitcast_fusion), channel_id=1, replica_groups=mesh['dp'=8,'band'=4] {'dp'}, dimensions={0}, use_global_device_ids=true | all-gather | bytes 1152 | tf_op jit(solution)/shard_map/all_gather | solution.py:1145
  64.4 6.1 copy.291
  70.5 6.3 copy.292
  88.3 52.5 %gather_blocks.1.weight_ref = bf16[1152,4608]{1,0:T(8,128)(2,1)} custom-call(bf16[144,1152]{1,0:T(8,128)(2,1)} %pad_maximum_fusion.2.refs_0_), custom_call_target="tpu_custom_call" | custom-call | tf_op jit(solution)/shard_map/gather_blocks/pallas_call | solution.py:679
  142.1 15.2 %copy.342 = bf16[1152,4608]{0,1:T(8,128)(2,1)} copy(bf16[1152,4608]{1,0:T(8,128)(2,1)} %gather_blocks.1.weight_ref) | data formatting | bytes 21233664 | tf_op jit(solution)/shard_map/reshape | solution.py:1194
  160.8 6.4 fusion.47
  167.3 6.1 copy.346
  182.2 7.3 all-to-all-done.2
  201.3 6.1 copy.341
  207.4 8.4 add_convert_fusion.2
  220.1 15.3 %project_qkv.1 = bf16[3456,1024]{1,0:T(8,128)(2,1)} custom-call(bf16[1024,1152]{1,0:T(8,128)(2,1)} %copy.302.hidden_ref, bf16[1152,4608]{1,0:T(8,128)(2,1)} %gather_blocks.1.weight_ref), custom_call_target="tpu_custom_call" | custom-call | tf_op jit(solution)/shard_map/project_qkv/pallas_call | solution.py:979
  235.3 101.0 %attn_forward.1 = (bf16[16,72,1024]{2,1,0:T(8,128)(2,1)}, f32[16,1,1024]{2,1,0:T(1,128)}, bf16[1152,4608]{1,0:T(8,128)(2,1)}, bf16[1152,4608]{1,0:T(8,128)(2,1)}) custom-call(s32[1]{0:T(128)} %dynamic_slice.19.refs_0_, bf16[48,72,1024]{2,1,0:T(8,128)(2,1)} %bitcast.89, bf16[48,72,1024]{2,1,0:T(8,128)(2,1)} %bitcast.90, bf16[48,72,1024]{2,1,0:T(8,128)(2,1)} %bitcast.91, ...), custom_call_target="tpu_custom_call" | custom-call | tf_op jit(solution)/shard_map/attn_forward/pallas_call | solution.py:915
  336.3 16.2 %copy.304 = bf16[1024,1152]{1,0:T(8,128)(2,1)} copy(bf16[1024,1152]{0,1:T(8,128)(2,1)} %bitcast.108) | data formatting | bytes 4718592 | tf_op jit(solution)/shard_map/dot_general | solution.py:1204
  352.4 9.7 %fusion.45 = (f32[4,256]{1,0:T(4,128)S(1)}, f32[4,256,1152]{2,1,0:T(8,128)S(1)}, f32[4,256,1152]{2,1,0:T(8,128)}) fusion(f32[4,256,1152]{2,1,0:T(8,128)} %bitcast.101, f32[4,1152]{1,0:T(4,128)S(1)} %get-tuple-element.259, bf16[4,256,1152]{2,1,0:T(8,128)(2,1)} %bitcast.118, bf16[1152,1152,1]{0,1,2:T(8,128)(2,1)} %bitcast.114), kind=kOutput, calls=%fused_computation.135 | convolution fusion | flops 2721446912 | bytes 19191808 | tf_op jit(solution)/shard_map/dot_general | solution.py:1204
  376.5 78.9 %mlp_both.1 = (f32[1024,1152]{1,0:T(8,128)}, f32[1024,1152]{1,0:T(8,128)}, bf16[1152,4608]{1,0:T(8,128)(2,1)}, bf16[1152,4608]{1,0:T(8,128)(2,1)}) custom-call(bf16[1024,1152]{1,0:T(8,128)(2,1)} %bitcast.100, bf16[1152,1024]{1,0:T(8,128)(2,1)} %bitcast.110, bf16[1024,1152]{1,0:T(8,128)(2,1)} %bitcast.98, bf16[1152,1024]{1,0:T(8,128)(2,1)} %bitcast.111, ...), custom_call_target="tpu_custom_call" | custom-call | tf_op jit(solution)/shard_map/mlp_both/pallas_call | solution.py:481
  462.5 9.3 %multiply_reduce_fusion.1 = (f32[4,1152]{1,0:T(4,128)S(1)}, f32[4,256,1152]{2,1,0:T(8,128)S(1)}, bf16[4,256,1152]{2,1,0:T(8,128)(2,1)}, f32[4,1152]{1,0:T(4,128)S(1)}) fusion(f32[4,256,1152]{2,1,0:T(8,128)} %get-tuple-element.268, f32[4,256]{1,0:T(4,128)S(1)} %broadcast_multiply_fusion, f32[4,256,1152]{2,1,0:T(8,128)} %copy-done, ...), kind=kLoop, calls=%fused_computation.18 | loop fusion | flops 18865152 | bytes 28401664 | tf_op jit(solution)/shard_map/reduce_sum | solution.py:1226
  484.8 131.4 %attn_backward.1 = (bf16[3,16,72,1024]{3,2,1,0:T(8,128)(2,1)}, f32[144,1152]{1,0:T(8,128)}, f32[144,1152]{1,0:T(8,128)}) custom-call(s32[1]{0:T(128)} %dynamic_slice.19.refs_0_, bf16[48,72,1024]{2,1,0:T(8,128)(2,1)} %bitcast.92, bf16[48,72,1024]{2,1,0:T(8,128)(2,1)} %bitcast.93, bf16[48,72,1024]{2,1,0:T(8,128)(2,1)} %bitcast.94, ...), custom_call_target="tpu_custom_call" | custom-call | tf_op jit(solution)/shard_map/attn_backward/pallas_call | solution.py:949
  616.2 30.2 %project_back.1 = (f32[1024,1152]{1,0:T(8,128)}, bf16[1152,4608]{1,0:T(8,128)(2,1)}) custom-call(bf16[1152,1024]{1,0:T(8,128)(2,1)} %bitcast.96, bf16[1152,4608]{1,0:T(8,128)(2,1)} %gather_blocks.1.weight_ref, bf16[3456,1024]{1,0:T(8,128)(2,1)} %bitcast.112, bf16[1152,1152]{1,0:T(8,128)(2,1)} %convolution_convert_fusion.proj_ref), custom_call_target="tpu_custom_call" | custom-call | tf_op jit(solution)/shard_map/project_back/pallas_call | solution.py:1016
  646.4 74.5 %scatter_blocks.1 = f32[144,1152]{1,0:T(8,128)} custom-call(bf16[1152,4608]{1,0:T(8,128)(2,1)} %get-tuple-element.44.refs_0_), custom_call_target="tpu_custom_call" | custom-call | tf_op jit(solution)/shard_map/scatter_blocks/pallas_call | solution.py:861
  722.2 6.2 copy.312
  728.3 6.7 multiply_reduce_fusion.6
  735.1 6.8 fusion.3
  762.3 18.2 %all_gather.7 = f32[8,16,864]{2,0,1:T(8,128)S(1)} all-gather(f32[8,4,864]{2,0,1:T(8,128)S(1)} %copy.322), channel_id=1, replica_groups=mesh['dp'=8,'band'=4] {'band'}, dimensions={1}, use_global_device_ids=true | all-gather | bytes 552960 | tf_op jit(solution)/shard_map/all_gather | solution.py:1259
  792.1 37.8 %all-reduce = (f32[]{:T(128)}, f32[1152]{0:T(1024)S(1)}) all-reduce(f32[]{:T(128)S(6)} %add.258, f32[1152]{0:T(1024)S(1)} %get-tuple-element.262), channel_id=1, replica_groups=mesh['dp'=8,'band'=4] {'dp','band'}, use_global_device_ids=true, to_apply=%region_22.23 | all-reduce | flops 1153 | bytes 9224 | tf_op jit(solution)/shard_map/psum | solution.py:1294
  (205 shorter events, 176.8 us)
Async XLA Ops:
  7.2 39.0 %copy-start.10 = (f32[288,432]{1,0:T(8,128)S(1)}, f32[288,432]{1,0:T(8,128)}, u32[]{:S(2)}) copy-start(f32[288,432]{1,0:T(8,128)} %param.33) | copy-start | bytes 1492996
  7.2 40.1 %copy-start.4 = (f32[288,576]{1,0:T(8,128)S(1)}, f32[288,576]{1,0:T(8,128)}, u32[]{:S(2)}) copy-start(f32[288,576]{1,0:T(8,128)} %param.35) | copy-start | bytes 1990660
  7.2 51.1 %all-to-all-start = ((s32[4,1,128]{2,1,0:T(1,128)}), s32[4,1,128]{2,1,0:T(1,128)S(1)}, u32[]{:S(2)}, u32[]{:S(2)}) async-start(s32[4,1,128]{2,1,0:T(1,128)} %bitcast.131), calls=%async_computation | async-start | bytes 4096 | tf_op jit(solution)/shard_map/all_to_all | solution.py:1058
  11.6 164.7 %reduce-scatter.2.cloned.1.call-start = ((), (), s32[]{:S(2)}) async-start(), calls=%async_computation.8 | async-start | bytes 573440 | tf_op jit(solution)/shard_map/reduce_scatter | solution.py:1163
  43.4 7.2 copy-start.5
  48.7 36.4 %collective-permute-start = (bf16[144,1152]{1,0:T(8,128)(2,1)}, bf16[144,1152]{1,0:T(8,128)(2,1)}, u32[]{:S(2)}, u32[]{:S(2)}) collective-permute-start(bf16[144,1152]{1,0:T(8,128)(2,1)} %get-tuple-element.253), channel_id=1, source_target_pairs={{0,4},{4,0},{8,12},{12,8},{16,20},{20,16},{24,28},{28,24},{1,5},{5... | collective-permute-start | bytes 995336 | tf_op jit(solution)/shard_map/ppermute | solution.py:1044
  58.3 102.5 %all-to-all-start.1 = ((bf16[4,128,1152]{2,1,0:T(8,128)(2,1)}), bf16[4,128,1152]{2,1,0:T(8,128)(2,1)S(1)}, u32[]{:S(2)}, u32[]{:S(2)}) async-start(bf16[4,128,1152]{2,1,0:T(8,128)(2,1)} %param.25), calls=%async_computation.1 | async-start | bytes 2359296 | tf_op jit(solution)/shard_map/all_to_all | solution.py:1058
  70.5 10.6 %copy-start.13 = (f32[288,576]{1,0:T(8,128)S(1)}, f32[288,576]{1,0:T(8,128)}, u32[]{:S(2)}) copy-start(f32[288,576]{1,0:T(8,128)} %param.41) | copy-start | bytes 1990660
  70.5 11.8 %copy-start.14 = (f32[288,576]{1,0:T(8,128)S(1)}, f32[288,576]{1,0:T(8,128)}, u32[]{:S(2)}) copy-start(f32[288,576]{1,0:T(8,128)} %param.47) | copy-start | bytes 1990660
  177.9 11.6 %all-to-all-start.2 = ((f32[8,4,864]{2,1,0:T(4,128)}), f32[8,4,864]{2,1,0:T(4,128)S(1)}, u32[]{:S(2)}, u32[]{:S(2)}) async-start(f32[8,4,864]{2,1,0:T(4,128)} %copy.295), calls=%async_computation.3 | async-start | bytes 229376 | tf_op jit(solution)/shard_map/all_to_all | solution.py:1164
  189.5 181.0 %all-to-all-start.3 = ((bf16[4,256,1152]{2,1,0:T(8,128)(2,1)}), bf16[4,256,1152]{2,1,0:T(8,128)(2,1)S(1)}, u32[]{:S(2)}, u32[]{:S(2)}) async-start(bf16[4,256,1152]{2,1,0:T(8,128)(2,1)} %param.31), calls=%async_computation.4 | async-start | bytes 4718592 | tf_op jit(solution)/shard_map/all_to_all | solution.py:1058
  471.9 8.0 copy-start.2
  744.5 9.0 %copy-start.7 = (f32[144,1152]{1,0:T(8,128)S(1)}, f32[144,1152]{1,0:T(8,128)}, u32[]{:S(2)}) copy-start(f32[144,1152]{1,0:T(8,128)} %get-tuple-element.46) | copy-start | bytes 1990660
  746.6 10.7 %all-to-all-start.6 = ((f32[8,4,864]{2,1,0:T(4,128)}), f32[8,4,864]{2,1,0:T(4,128)S(1)}, u32[]{:S(2)}, u32[]{:S(2)}) async-start(f32[8,4,864]{2,1,0:T(4,128)} %copy.321), calls=%async_computation.7 | async-start | bytes 229376 | tf_op jit(solution)/shard_map/all_to_all | solution.py:1258
  751.3 32.4 %collective-permute-start.1 = (bf16[144,1152]{1,0:T(8,128)(2,1)}, bf16[144,1152]{1,0:T(8,128)(2,1)S(1)}, u32[]{:S(2)}, u32[]{:S(2)}) collective-permute-start(bf16[144,1152]{1,0:T(8,128)(2,1)} %get-tuple-element.251), channel_id=1, source_target_pairs={{0,4},{4,0},{8,12},{12,8},{16,20},{20,16},{24,28},{28,24},{1,5},{5... | collective-permute-start | bytes 995336 | tf_op jit(solution)/shard_map/ppermute | solution.py:1053
  757.9 79.3 %all-to-all-start.5 = ((bf16[4,128,1152]{2,1,0:T(8,128)(2,1)}), bf16[4,128,1152]{2,1,0:T(8,128)(2,1)S(1)}, u32[]{:S(2)}, u32[]{:S(2)}) async-start(bf16[4,128,1152]{2,1,0:T(8,128)(2,1)} %bitcast.123), calls=%async_computation.6 | async-start | bytes 2359296 | tf_op jit(solution)/shard_map/all_to_all | solution.py:1272
  837.2 33.1 %all-to-all-start.4 = ((bf16[4,256,1152]{2,1,0:T(8,128)(2,1)}), bf16[4,256,1152]{2,1,0:T(8,128)(2,1)}, u32[]{:S(2)}, u32[]{:S(2)}) async-start(bf16[4,256,1152]{2,1,0:T(8,128)(2,1)} %get-tuple-element.248), calls=%async_computation.5 | async-start | bytes 4718592 | tf_op jit(solution)/shard_map/all_to_all | solution.py:1219
  845.3 11.4 %copy-start.22 = (f32[1152]{0:T(1024)S(1)}, f32[1152]{0:T(1024)}, u32[]{:S(2)}) copy-start(f32[1152]{0:T(1024)} %param.38) | copy-start | bytes 13828
  845.3 11.4 %copy-start.23 = (f32[1152]{0:T(1024)S(1)}, f32[1152]{0:T(1024)}, u32[]{:S(2)}) copy-start(f32[1152]{0:T(1024)} %param.44) | copy-start | bytes 13828
  845.3 12.0 %copy-start.12 = (f32[288,144]{0,1:T(8,128)S(1)}, f32[288,144]{0,1:T(8,128)}, u32[]{:S(2)}) copy-start(f32[288,144]{0,1:T(8,128)} %param.34) | copy-start | bytes 497668
  845.3 12.0 %copy-start.20 = (f32[288,144]{0,1:T(8,128)S(1)}, f32[288,144]{0,1:T(8,128)}, u32[]{:S(2)}) copy-start(f32[288,144]{0,1:T(8,128)} %param.40) | copy-start | bytes 497668
  856.7 7.0 copy-start.6
  856.7 7.0 copy-start.8
  856.7 7.0 copy-start.15
  (12 other events, 49.7 us)
Sparse Core Ops, SparseCore 0:
  46.2 22.5 reduce-scatter.1

commit v4 on v0

--- a/solution.py
+++ b/solution.py
@@ -1,8 +1,11 @@
+import functools
 import math
 
 import jax
 import jax.numpy as jnp
 from jax import lax
+from jax.experimental import pallas as pl
+from jax.experimental.pallas import tpu as pltpu
 from jax.sharding import PartitionSpec as P
 
 D = 1152
@@ -129,7 +132,7 @@
     return (weight_new, first_new, second_new)
 
 
-def per_device(
+def general_device(
     kept_tokens,
     kept_index,
     resolution,
@@ -366,6 +369,1646 @@
     )
 
 
+MASKED = -1e30
+SCORE_SCALE = HEAD_DIM ** (-0.5)
+LOG2E = math.log2(math.e)
+VMEM_LIMIT = 63 * 1024 * 1024
+
+
+def dot_nn(left, right):
+    return lax.dot_general(
+        left, right, (((1,), (0,)), ((), ())), preferred_element_type=jnp.float32
+    )
+
+
+def dot_nt(left, right):
+    return lax.dot_general(
+        left, right, (((1,), (1,)), ((), ())), preferred_element_type=jnp.float32
+    )
+
+
+def masked_scores(keys, queries, block, other):
+    raw = dot_nn(keys, queries)
+    parts = [
+        raw[r * REGION : (r + 1) * REGION] + (0.0 if r == block else other)
+        for r in range(keys.shape[0] // REGION)
+    ]
+    return jnp.concatenate(parts, axis=0)
+
+
+def attn_head(other, queries, keys_t, values_t, out_ref, rows, lse_ref):
+    keys = jnp.transpose(keys_t)
+    for block in range(keys.shape[0] // REGION):
+        cols = slice(block * REGION, (block + 1) * REGION)
+        scores = masked_scores(keys, queries[:, cols], block, other)
+        peak = jnp.max(scores, axis=0, keepdims=True)
+        weights = jnp.exp2((scores - peak) * (SCORE_SCALE * LOG2E))
+        total = jnp.sum(weights, axis=0, keepdims=True)
+        mixed = dot_nn(values_t, weights.astype(jnp.bfloat16))
+        out_ref[rows, cols] = (mixed / total).astype(jnp.bfloat16)
+        lse_ref[:, cols] = peak * (SCORE_SCALE * LOG2E) + jnp.log2(total)
+
+
+def attn_head_back(other, queries, keys_t, values_t, out, grad, lse_ref, grads_ref, rows):
+    tokens = queries.shape[1]
+    keys = jnp.transpose(keys_t)
+    values = jnp.transpose(values_t)
+    grad_keys = jnp.zeros((HEAD_DIM, tokens), jnp.float32)
+    grad_values = jnp.zeros((HEAD_DIM, tokens), jnp.float32)
+    dots = jnp.sum(out.astype(jnp.float32) * grad.astype(jnp.float32), axis=0, keepdims=True)
+    for block in range(tokens // REGION):
+        cols = slice(block * REGION, (block + 1) * REGION)
+        scores = masked_scores(keys, queries[:, cols], block, other)
+        weights = jnp.exp2(scores * (SCORE_SCALE * LOG2E) - lse_ref[:, cols])
+        grad_weights = dot_nn(values, grad[:, cols])
+        grad_scores = (weights * (grad_weights - dots[:, cols])).astype(jnp.bfloat16)
+        grad_values += dot_nt(grad[:, cols], weights.astype(jnp.bfloat16))
+        grad_keys += dot_nt(queries[:, cols], grad_scores)
+        grads_ref[0, rows, cols] = (dot_nn(keys_t, grad_scores) * SCORE_SCALE).astype(jnp.bfloat16)
+    grads_ref[1, rows] = (grad_keys * SCORE_SCALE).astype(jnp.bfloat16)
+    grads_ref[2, rows] = grad_values.astype(jnp.bfloat16)
+
+
+GELU_A = math.sqrt(2.0 / math.pi)
+GELU_B = 0.044715
+
+
+def mlp_kernel(h_ref, ht_ref, g_ref, gt_ref, up_ref, down_ref, out_ref, grad_ref, gup_ref, gdown_ref):
+    step = pl.program_id(0)
+
+    @pl.when(step == 0)
+    def _():
+        out_ref[...] = jnp.zeros_like(out_ref)
+        grad_ref[...] = jnp.zeros_like(grad_ref)
+
+    up = up_ref[...]
+    down = down_ref[...]
+    upward = dot_nn(h_ref[...], up)
+    square = upward * upward
+    curve = jnp.tanh(GELU_A * upward * (1.0 + GELU_B * square))
+    half = 0.5 * (1.0 + curve)
+    active = (upward * half).astype(jnp.bfloat16)
+    slope = half + 0.5 * upward * (1.0 - curve * curve) * GELU_A * (
+        1.0 + 3.0 * GELU_B * square
+    )
+    grad_upward = (dot_nn(g_ref[...], down) * slope).astype(jnp.bfloat16)
+    out_ref[...] += dot_nt(active, down)
+    grad_ref[...] += dot_nt(grad_upward, up)
+    gup_ref[...] = dot_nn(ht_ref[...], grad_upward).astype(jnp.bfloat16)
+    gdown_ref[...] = dot_nn(gt_ref[...], active).astype(jnp.bfloat16)
+
+
+def mlp_both(hidden, hidden_t, grad, grad_t, up, down_t, tile):
+    tokens, width = hidden.shape
+    wide = up.shape[1]
+    whole = lambda shape: pl.BlockSpec(shape, lambda f: (0, 0))
+    part = pl.BlockSpec((width, tile), lambda f: (0, f))
+    return pl.pallas_call(
+        mlp_kernel,
+        grid=(wide // tile,),
+        in_specs=[
+            whole((tokens, width)),
+            whole((width, tokens)),
+            whole((tokens, width)),
+            whole((width, tokens)),
+            part,
+            part,
+        ],
+        out_specs=[whole((tokens, width)), whole((tokens, width)), part, part],
+        out_shape=[
+            jax.ShapeDtypeStruct((tokens, width), jnp.float32),
+            jax.ShapeDtypeStruct((tokens, width), jnp.float32),
+            jax.ShapeDtypeStruct((width, wide), jnp.bfloat16),
+            jax.ShapeDtypeStruct((width, wide), jnp.bfloat16),
+        ],
+        compiler_params=pltpu.CompilerParams(vmem_limit_bytes=VMEM_LIMIT),
+        name="mlp_both",
+    )(hidden, hidden_t, grad, grad_t, up, down_t)
+
+
+BLOCK_ROWS = 144
+BLOCK_COLS = 1152
+def flip(index):
+    return index + 1 - 2 * (index % 2)
+
+
+def along_z(z, step):
+    return (z, flip(z), (z + 2) % 4, 3 - z)[step]
+
+
+class Place:
+    def __init__(self):
+        dp = lax.axis_index("dp")
+        band = lax.axis_index("band")
+        self.z, self.y, self.x, self.core = dp // 2, dp % 2, band // 2, band % 2
+
+    def chip(self, i, a, b):
+        return (along_z(self.z, i), flip(self.y) if a else self.y, flip(self.x) if b else self.x)
+
+    def device(self, i=0, a=0, b=0, core=0):
+        z, y, x = self.chip(i, a, b)
+        return (z * 2 + y, x * 2 + (flip(self.core) if core else self.core))
+
+    def partners(self, band=False, dp=False):
+        found = [
+            self.device(core=1),
+            self.device(b=1),
+            self.device(a=1),
+            self.device(i=1),
+            self.device(i=2),
+            self.device(i=3),
+        ]
+        if band:
+            found.append(self.device(b=1, core=1))
+        if dp:
+            found += [self.device(i=i, a=1) for i in (1, 2, 3)]
+        return found
+
+    def dp(self, i=0, a=0):
+        z, y, _ = self.chip(i, a, 0)
+        return z * 2 + y
+
+    def band(self, b=0, core=0):
+        x = flip(self.x) if b else self.x
+        return x * 2 + (flip(self.core) if core else self.core)
+
+    def block(self, by_rows, i, a, b, core=0):
+        z, y, x = self.chip(i, a, b)
+        c = flip(self.core) if core else self.core
+        if by_rows:
+            row, col = z * 2 + y, x * 2 + c
+        else:
+            row, col = (x * 2 + c) * 2 + y, z
+        return (
+            pl.ds(pl.multiple_of(row * BLOCK_ROWS, 16), BLOCK_ROWS),
+            pl.ds(pl.multiple_of(col * BLOCK_COLS, 128), BLOCK_COLS),
+        )
+
+
+def greet(place, band=False, dp=False):
+    barrier = pltpu.get_barrier_semaphore()
+    partners = place.partners(band, dp)
+    for partner in partners:
+        pl.semaphore_signal(
+            barrier, inc=1, device_id=partner, device_id_type=pl.DeviceIdType.MESH
+        )
+    pl.semaphore_wait(barrier, len(partners))
+
+
+def send(source, target, send_sem, recv_sem, device):
+    return pltpu.make_async_remote_copy(
+        src_ref=source,
+        dst_ref=target,
+        send_sem=send_sem,
+        recv_sem=recv_sem,
+        device_id=device,
+        device_id_type=pl.DeviceIdType.MESH,
+    )
+
+
+CHIPS = [(i, a, b) for i in range(4) for a in range(2) for b in range(2)]
+
+
+def slot(piece):
+    return piece[0] * 4 + piece[1] * 2 + piece[2]
+
+
+def parent(piece, via_x, sides_by_z):
+    i, a, b = piece
+    if a and b:
+        return (0, 0, 1) if i in via_x else (0, 1, 0)
+    if (a or b) and not (i == 1 and sides_by_z):
+        return (0, a, b)
+    return (i, 0, 0)
+
+
+def moved(piece, step):
+    return (piece[0] ^ step[0], piece[1] ^ step[1], piece[2] ^ step[2])
+
+
+def children(piece, via_x, sides_by_z):
+    return [
+        (other, parent(other, via_x, sides_by_z))
+        for other in CHIPS
+        if any(other) and moved(other, parent(other, via_x, sides_by_z)) == piece
+    ]
+
+
+GATHER_SENDS = 31
+ARRIVALS = [
+    (1, 0, 0), (0, 1, 0), (0, 0, 1), (3, 0, 0), (1, 0, 1), (1, 1, 0), (2, 0, 0), (3, 1, 0),
+    (3, 0, 1), (2, 0, 1), (2, 1, 0), (0, 1, 1), (1, 1, 1), (3, 1, 1), (2, 1, 1),
+]
+
+
+def gather_actions(
+    place, plans, own_refs, full_refs, local_sems, send_sems, link_sems, core_sems, meet=None
+):
+    weights = range(len(own_refs))
+    counts = [0] * len(own_refs)
+
+    def ship(w, source, piece, name, sems, device):
+        target = full_refs[w].at[place.block(plans[w][0], *piece)]
+        send(source, target, send_sems.at[w, counts[w]], sems.at[w, slot(name)], device).start()
+        counts[w] += 1
+
+    def pass_on(w, source, piece):
+        for child, step in children(piece, plans[w][1], False):
+            ship(w, source, piece, child, link_sems, place.device(*step))
+        ship(w, source, piece, piece, core_sems, place.device(core=1))
+
+    def arrive(w, piece, core=0):
+        target = full_refs[w].at[place.block(plans[w][0], *piece, core)]
+        sems = core_sems if core else link_sems
+        send(
+            target, target, send_sems.at[w, 0], sems.at[w, slot(piece)], place.device(core=1)
+        ).wait_recv()
+        return target
+
+    def keep(w):
+        return pltpu.make_async_copy(
+            own_refs[w], full_refs[w].at[place.block(plans[w][0], 0, 0, 0)], local_sems.at[w]
+        )
+
+    def begin():
+        (meet or greet)(place)
+        for w in weights:
+            keep(w).start()
+            pass_on(w, own_refs[w], (0, 0, 0))
+
+    def relay(w, piece):
+        def step():
+            pass_on(w, arrive(w, piece), piece)
+
+        return step
+
+    def finish():
+        for w in weights:
+            for piece in CHIPS:
+                arrive(w, piece, core=1)
+            keep(w).wait()
+            for n in range(counts[w]):
+                send(
+                    own_refs[w], own_refs[w], send_sems.at[w, n], link_sems.at[w, 0],
+                    place.device(core=1),
+                ).wait_send()
+
+    return [begin] + [relay(w, piece) for w in weights for piece in ARRIVALS] + [finish]
+
+
+def gather_scratch(count):
+    return [
+        pltpu.SemaphoreType.DMA((count,)),
+        pltpu.SemaphoreType.DMA((count, GATHER_SENDS)),
+        pltpu.SemaphoreType.DMA((count, 16)),
+        pltpu.SemaphoreType.DMA((count, 16)),
+    ]
+
+
+BAND_PEERS = ((0, 1), (1, 0), (1, 1))
+DP_PEERS = ((1, 0), (0, 1), (3, 0), (1, 1), (2, 0), (3, 1), (2, 1))
+
+
+def swap_band(place, source, target, local_sem, send_sems, recv_sems):
+    def copies():
+        found = []
+        for n, (b, core) in enumerate(BAND_PEERS):
+            found.append(
+                send(
+                    source.at[place.band(b, core)],
+                    target.at[place.band()],
+                    send_sems.at[n],
+                    recv_sems.at[n],
+                    place.device(b=b, core=core),
+                )
+            )
+        local = pltpu.make_async_copy(
+            source.at[place.band()], target.at[place.band()], local_sem.at[0]
+        )
+        return found, local
+
+    def start():
+        found, local = copies()
+        for copy in found:
+            copy.start()
+        local.start()
+
+    def wait():
+        found, local = copies()
+        for copy in found:
+            copy.wait()
+        local.wait()
+
+    return start, wait
+
+
+def swap_scratch():
+    return [
+        pltpu.SemaphoreType.DMA((1,)),
+        pltpu.SemaphoreType.DMA((3,)),
+        pltpu.SemaphoreType.DMA((3,)),
+    ]
+
+
+def head_kernel(
+    block_ref,
+    cond_ref,
+    ada_ref,
+    kept_ref,
+    index_ref,
+    full_ref,
+    mod_ref,
+    conds_ref,
+    kept_out,
+    index_out,
+    part_ref,
+    got_ref,
+    sums_ref,
+    cond_sends,
+    cond_recvs,
+    part_sends,
+    part_recvs,
+    mod_sends,
+    mod_recvs,
+    *rest,
+):
+    place = Place()
+    slots, _, _, cols = part_ref.shape
+    images = part_ref.shape[2]
+    plans = ((False, (0,)),)
+    actions = gather_actions(
+        place, plans, [block_ref], [full_ref], *rest[:4], meet=lambda _: None
+    )
+    kept_start, kept_wait = swap_band(place, kept_ref, kept_out, *rest[4:7])
+    index_start, index_wait = swap_band(place, index_ref, index_out, *rest[7:10])
+
+    def to_dp(n, source, target, sends, recvs):
+        i, a = DP_PEERS[n]
+        return send(source, target, sends.at[n], recvs.at[n], place.device(i=i, a=a))
+
+    greet(place, band=True, dp=True)
+    own = place.dp()
+    cond_copies = [
+        to_dp(n, cond_ref, conds_ref.at[own], cond_sends, cond_recvs) for n in range(7)
+    ]
+    for copy in cond_copies:
+        copy.start()
+    actions[0]()
+    index_start()
+    conds_ref[own] = cond_ref[...]
+    for copy in cond_copies:
+        copy.wait()
+    for s in range(slots):
+        rows = conds_ref[:, s].reshape(-1, cond_ref.shape[-1]).astype(jnp.bfloat16)
+        product = dot_nn(rows, ada_ref[...])
+        part_ref[s] = product.reshape(-1, cond_ref.shape[1], cols)[:, :images]
+    part_copies = [
+        send(
+            part_ref.at[place.band(b, core)],
+            got_ref.at[n],
+            part_sends.at[n],
+            part_recvs.at[n],
+            place.device(b=b, core=core),
+        )
+        for n, (b, core) in enumerate(BAND_PEERS)
+    ]
+    for copy in part_copies:
+        copy.start()
+    for action in actions[1:4]:
+        action()
+    kept_start()
+    for action in actions[4:8]:
+        action()
+    for copy in part_copies:
+        copy.wait()
+    sums_ref[...] = part_ref[place.band()] + got_ref[0] + got_ref[1] + got_ref[2]
+    mod_copies = [
+        to_dp(n, sums_ref.at[place.dp(*DP_PEERS[n])], mod_ref.at[own], mod_sends, mod_recvs)
+        for n in range(7)
+    ]
+    for copy in mod_copies:
+        copy.start()
+    mod_ref[own] = sums_ref[own]
+    for action in actions[8:]:
+        action()
+    for copy in mod_copies:
+        copy.wait()
+    index_wait()
+    kept_wait()
+
+
+def head(block, cond, ada, kept, index, collective_id):
+    slots, images_pad, width = cond.shape
+    images = 4
+    cols = ada.shape[1]
+    groups = lax.axis_size("dp")
+    vmem = pl.BlockSpec(memory_space=pltpu.VMEM)
+    hbm = pl.BlockSpec(memory_space=pl.ANY)
+    f32 = jnp.float32
+    return pl.pallas_call(
+        head_kernel,
+        in_specs=[vmem, vmem, vmem, hbm, hbm],
+        out_specs=[hbm, vmem, vmem, hbm, hbm],
+        out_shape=[
+            jax.ShapeDtypeStruct((8 * BLOCK_ROWS, 4 * BLOCK_COLS), jnp.bfloat16),
+            jax.ShapeDtypeStruct((groups, images, cols), f32),
+            jax.ShapeDtypeStruct((groups,) + cond.shape, f32),
+            jax.ShapeDtypeStruct(kept.shape, kept.dtype),
+            jax.ShapeDtypeStruct(index.shape, index.dtype),
+        ],
+        scratch_shapes=[
+            pltpu.VMEM((slots, groups, images, cols), f32),
+            pltpu.VMEM((3, groups, images, cols), f32),
+            pltpu.VMEM((groups, images, cols), f32),
+            pltpu.SemaphoreType.DMA((7,)),
+            pltpu.SemaphoreType.DMA((7,)),
+            pltpu.SemaphoreType.DMA((3,)),
+            pltpu.SemaphoreType.DMA((3,)),
+            pltpu.SemaphoreType.DMA((7,)),
+            pltpu.SemaphoreType.DMA((7,)),
+        ]
+        + gather_scratch(1)
+        + swap_scratch()
+        + swap_scratch(),
+        compiler_params=pltpu.CompilerParams(
+            collective_id=collective_id, has_side_effects=True, vmem_limit_bytes=VMEM_LIMIT
+        ),
+        name="head",
+    )(block, cond, ada, kept, index)
+
+
+FOLDS = [
+    (1, 1, 1), (3, 1, 1), (2, 1, 1), (0, 1, 1), (1, 0, 0), (1, 1, 0), (1, 0, 1), (3, 1, 0),
+    (3, 0, 1), (2, 1, 0), (2, 0, 1), (0, 1, 0), (0, 0, 1), (3, 0, 0), (2, 0, 0), (0, 0, 0),
+]
+STAGES = 4
+
+
+def scatter_actions(
+    place,
+    plans,
+    grad_refs,
+    out_refs,
+    held_refs,
+    over_refs,
+    stage,
+    stage_sems,
+    send_sems,
+    held_sems,
+    over_sems,
+    meet=None,
+):
+    weights = range(len(grad_refs))
+    counts = [0] * len(grad_refs)
+    order = [(w, piece) for w in weights for piece in FOLDS]
+
+    def ship(w, source, target, recv_sem, device):
+        send(source, target, send_sems.at[w, counts[w]], recv_sem, device).start()
+        counts[w] += 1
+
+    def landed(target, recv_sem):
+        send(target, target, send_sems.at[0, 0], recv_sem, place.device(core=1)).wait_recv()
+
+    def begin():
+        (meet or greet)(place)
+        for w, piece in order:
+            source = grad_refs[w].at[place.block(plans[w][0], *piece, 1)]
+            s = slot(piece)
+            ship(w, source, held_refs.at[w, s], held_sems.at[w, s], place.device(core=1))
+
+    def load(n):
+        w, piece = order[n]
+        return pltpu.make_async_copy(
+            grad_refs[w].at[place.block(plans[w][0], *piece)],
+            stage.at[n % STAGES],
+            stage_sems.at[n % STAGES],
+        )
+
+    def up(w, piece):
+        step = parent(piece, plans[w][1], True)
+        s = slot(piece)
+        ship(
+            w, held_refs.at[w, s], over_refs.at[w, s - 1], over_sems.at[w, s - 1], place.device(*step)
+        )
+
+    def fold(n):
+        def step():
+            if n == 0:
+                for ahead in range(STAGES - 1):
+                    load(ahead).start()
+            if n + STAGES - 1 < len(order):
+                load(n + STAGES - 1).start()
+            w, piece = order[n]
+            s = slot(piece)
+            load(n).wait()
+            landed(held_refs.at[w, s], held_sems.at[w, s])
+            held = held_refs.at[w, s]
+            held[...] = held[...] + stage[n % STAGES]
+            if not children(piece, plans[w][1], True):
+                up(w, piece)
+
+        return step
+
+    def combine(w, piece):
+        def step():
+            held = held_refs.at[w, slot(piece)]
+            total = held[...].astype(jnp.float32)
+            for child, _ in children(piece, plans[w][1], True):
+                k = slot(child) - 1
+                landed(over_refs.at[w, k], over_sems.at[w, k])
+                total = total + over_refs[w, k].astype(jnp.float32)
+            if any(piece):
+                held[...] = total.astype(jnp.bfloat16)
+                up(w, piece)
+            else:
+                out_refs[w][...] = total.astype(jnp.bfloat16)
+
+        return step
+
+    def finish():
+        for w in weights:
+            block = held_refs.at[w, 0]
+            for n in range(counts[w]):
+                send(
+                    block, block, send_sems.at[w, n], held_sems.at[w, 0], place.device(core=1)
+                ).wait_send()
+
+    inner = lambda w: [p for p in FOLDS if any(p) and children(p, plans[w][1], True)]
+    early = [[p for p in inner(w) if p[0] and (p[1] or p[2])] for w in weights]
+    late = [[p for p in inner(w) if p not in early[w]] for w in weights]
+    steps = [begin] + [fold(n) for n in range(len(order))]
+    steps += [combine(w, p) for w in weights for p in early[w]]
+    steps += [combine(w, p) for w in weights for p in late[w]]
+    steps += [combine(w, (0, 0, 0)) for w in weights]
+    return steps + [finish]
+
+
+def scatter_scratch(count):
+    blocks = lambda n: pltpu.VMEM((count, n, BLOCK_ROWS, BLOCK_COLS), jnp.bfloat16)
+    return [
+        blocks(16),
+        blocks(15),
+        pltpu.VMEM((STAGES, BLOCK_ROWS, BLOCK_COLS), jnp.bfloat16),
+        pltpu.SemaphoreType.DMA((STAGES,)),
+        pltpu.SemaphoreType.DMA((count, 31)),
+        pltpu.SemaphoreType.DMA((count, 16)),
+        pltpu.SemaphoreType.DMA((count, 15)),
+    ]
+
+
+def to_dp_peer(place, n, source, target, sends, recvs):
+    i, a = DP_PEERS[n]
+    return send(source, target, sends.at[n], recvs.at[n], place.device(i=i, a=a))
+
+
+def to_band_peer(place, n, source, target, sends, recvs):
+    b, core = BAND_PEERS[n]
+    return send(source, target, sends.at[n], recvs.at[n], place.device(b=b, core=core))
+
+
+def square_sum(values):
+    wide = values.astype(jnp.float32)
+    return jnp.sum(jnp.sum(wide * wide, axis=0, keepdims=True), axis=1, keepdims=True)
+
+
+def tail_kernel(
+    grad_ref,
+    kind_ref,
+    fc1_ref,
+    fc2_ref,
+    index_ref,
+    index_t_ref,
+    scales_ref,
+    sums_ref,
+    conds_ref,
+    tokens_hbm,
+    middle_hbm,
+    hidden_hbm,
+    own_ref,
+    other_ref,
+    fc1_other_ref,
+    ada_ref,
+    mask_out,
+    square_out,
+    kept_out,
+    tokens,
+    grad_middle,
+    grad_hidden,
+    kept_total,
+    kept,
+    six,
+    mask_own,
+    mods_own,
+    mods_dp,
+    mods_all,
+    mask_band,
+    mask_sum,
+    mask_dp,
+    square_own,
+    square_band,
+    square_sum_ref,
+    square_dp,
+    load_sems,
+    y_sends,
+    y_recvs,
+    dp_sends,
+    dp_recvs,
+    band_sends,
+    band_recvs,
+    *rest,
+):
+    place = Place()
+    plans = ((False, (0,)),)
+    actions = scatter_actions(
+        place, plans, [grad_ref], [own_ref], *rest[:7], meet=lambda _: None
+    )
+    kept_start, kept_wait = swap_band(place, kept, kept_out, *rest[7:10])
+    across = lambda n, source, target: send(
+        source, target, y_sends.at[n], y_recvs.at[n], place.device(a=1)
+    )
+    to_dp = lambda k, n, source, target: to_dp_peer(
+        place, n, source, target, dp_sends.at[k], dp_recvs.at[k]
+    )
+    to_band = lambda k, n, source, target: to_band_peer(
+        place, n, source, target, band_sends.at[k], band_recvs.at[k]
+    )
+    greet(place, band=True, dp=True)
+    own = place.dp()
+    loads = [
+        pltpu.make_async_copy(source, target, load_sems.at[n])
+        for n, (source, target) in enumerate(
+            [(tokens_hbm, tokens), (middle_hbm, grad_middle), (hidden_hbm, grad_hidden)]
+        )
+    ]
+    for copy in loads:
+        copy.start()
+    actions[0]()
+    fc1_copy = across(0, fc1_ref, fc1_other_ref)
+    fc1_copy.start()
+    for action in actions[1:6]:
+        action()
+    for copy in loads:
+        copy.wait()
+
+    count = tokens.shape[0]
+    regions = count // REGION
+    done = 6
+    for region in range(regions):
+        spot = slice(region * REGION, (region + 1) * REGION)
+        grad = grad_hidden[spot]
+        normal, root = norm_parts(tokens[spot])
+        scale = scales_ref[SCALE_ATTN, region : region + 1]
+        grad_tokens = grad_middle[spot] + norm_back(grad, normal, root, scale)
+        six[0, region : region + 1] = column_sum(grad)
+        six[1, region : region + 1] = column_sum(grad * normal)
+        for k in range(4):
+            six[2 + k, region : region + 1] = sums_ref[region, k : k + 1]
+        unfilled = 1.0 - jnp.sum(chosen_rows(index_ref, region), axis=1, keepdims=True)
+        masked = column_sum(unfilled * grad_tokens)
+        columns = lax.broadcasted_iota(jnp.int32, (index_t_ref.shape[0], REGION), 1)
+        select = (index_t_ref[...] == columns + region * REGION).astype(jnp.float32)
+        added = dot_nn(select.astype(jnp.bfloat16), grad_tokens.astype(jnp.bfloat16))
+        if region == 0:
+            mask_own[...] = jnp.broadcast_to(masked, mask_own.shape)
+            kept_total[...] = added
+        else:
+            mask_own[...] += jnp.broadcast_to(masked, mask_own.shape)
+            kept_total[...] += added
+        for action in actions[done : done + 3]:
+            action()
+        done += 3
+    kept[...] = kept_total[...].astype(jnp.bfloat16).reshape(kept.shape)
+    images = six.shape[1]
+    first = lax.broadcasted_iota(jnp.int32, six.shape[1:], 0) == 0
+    flat = []
+    for k in range(6):
+        part = six[k]
+        flat.append(
+            jnp.where(kind_ref[0] == 1, part, jnp.where(first, column_sum(part), 0.0))
+        )
+    flat = jnp.concatenate(flat, axis=1)
+    groups, padded, cols = mods_own.shape
+    for d in range(groups):
+        mods_own[d, :images] = flat[:, d * cols : (d + 1) * cols]
+        mods_own[d, images:] = jnp.zeros((padded - images, cols), jnp.float32)
+
+    early = [to_dp(0, n, mods_own.at[place.dp(*DP_PEERS[n])], mods_dp.at[own]) for n in range(7)]
+    early += [to_band(0, n, mask_own, mask_band.at[n]) for n in range(3)]
+    for copy in early:
+        copy.start()
+    kept_start()
+    mods_dp[own] = mods_own[own]
+    for action in actions[done : done + 3]:
+        action()
+    done += 3
+    for copy in early:
+        copy.wait()
+    mask_sum[...] = mask_own[...] + mask_band[0] + mask_band[1] + mask_band[2]
+    second = [to_band(1, n, mods_dp, mods_all.at[place.band()]) for n in range(3)]
+    second += [to_dp(1, n, mask_sum, mask_dp.at[n]) for n in range(7)]
+    for copy in second:
+        copy.start()
+    mods_all[place.band()] = mods_dp[...]
+    fc1_copy.wait()
+    for action in actions[done : done + 3]:
+        action()
+    done += 3
+    for copy in second:
+        copy.wait()
+    total = mask_sum[...]
+    for n in range(7):
+        total = total + mask_dp[n]
+    mask_out[...] = total
+    width = ada_ref.shape[0]
+    ada = jnp.zeros(ada_ref.shape, jnp.float32)
+    for s in range(conds_ref.shape[1]):
+        ada += lax.dot_general(
+            conds_ref[:, s].reshape(-1, width),
+            mods_all[s].reshape(-1, ada_ref.shape[1]),
+            (((0,), (0,)), ((), ())),
+            precision=lax.Precision.HIGHEST,
+            preferred_element_type=jnp.float32,
+        )
+    ada_ref[...] = ada
+    squares = square_sum(ada) + square_sum(fc1_ref[...]) + square_sum(fc2_ref[...])
+    for action in actions[done:-1]:
+        action()
+    last = across(1, own_ref, other_ref)
+    last.start()
+    squares = squares + square_sum(own_ref[...])
+    square_own[...] = jnp.broadcast_to(squares, square_own.shape)
+    third = [to_band(2, n, square_own, square_band.at[n]) for n in range(3)]
+    for copy in third:
+        copy.start()
+    for copy in third:
+        copy.wait()
+    square_sum_ref[...] = square_own[...] + square_band[0] + square_band[1] + square_band[2]
+    fourth = [to_dp(2, n, square_sum_ref, square_dp.at[n]) for n in range(7)]
+    for copy in fourth:
+        copy.start()
+    for copy in fourth:
+        copy.wait()
+    total = square_sum_ref[...]
+    for n in range(7):
+        total = total + square_dp[n]
+    square_out[...] = total
+    last.wait()
+    kept_wait()
+    actions[-1]()
+
+
+def tail(
+    grad, kind, fc1, fc2, index, mod, sums, conds, tokens, grad_middle, grad_hidden, bands, collective_id
+):
+    f32, bf16 = jnp.float32, jnp.bfloat16
+    vmem = pl.BlockSpec(memory_space=pltpu.VMEM)
+    hbm = pl.BlockSpec(memory_space=pl.ANY)
+    block = jax.ShapeDtypeStruct((BLOCK_ROWS, BLOCK_COLS), bf16)
+    squares = (8, 128)
+    mask = (8, D)
+    count, width = tokens.shape
+    places = index.shape[1]
+    groups, _, padded, rows_ada = conds.shape
+    cols_ada = 6 * D // groups
+    mods = (groups, padded, cols_ada)
+    kept = (bands, places // bands, width)
+    dma = pltpu.SemaphoreType.DMA
+    return pl.pallas_call(
+        tail_kernel,
+        in_specs=[hbm, pl.BlockSpec(memory_space=pltpu.SMEM)] + [vmem] * 7 + [hbm] * 3,
+        out_specs=[vmem] * 6 + [hbm],
+        out_shape=[
+            block,
+            block,
+            block,
+            jax.ShapeDtypeStruct((rows_ada, cols_ada), f32),
+            jax.ShapeDtypeStruct(mask, f32),
+            jax.ShapeDtypeStruct(squares, f32),
+            jax.ShapeDtypeStruct(kept, bf16),
+        ],
+        scratch_shapes=[
+            pltpu.VMEM((count, width), f32),
+            pltpu.VMEM((count, width), f32),
+            pltpu.VMEM((count, width), f32),
+            pltpu.VMEM((places, width), f32),
+            pltpu.VMEM(kept, bf16),
+            pltpu.VMEM(mod.shape, f32),
+            pltpu.VMEM(mask, f32),
+            pltpu.VMEM(mods, f32),
+            pltpu.VMEM(mods, f32),
+            pltpu.VMEM((bands,) + mods, f32),
+            pltpu.VMEM((3,) + mask, f32),
+            pltpu.VMEM(mask, f32),
+            pltpu.VMEM((7,) + mask, f32),
+            pltpu.VMEM(squares, f32),
+            pltpu.VMEM((3,) + squares, f32),
+            pltpu.VMEM(squares, f32),
+            pltpu.VMEM((7,) + squares, f32),
+            dma((3,)),
+            dma((2,)),
+            dma((2,)),
+            dma((3, 7)),
+            dma((3, 7)),
+            dma((3, 3)),
+            dma((3, 3)),
+        ]
+        + scatter_scratch(1)
+        + swap_scratch(),
+        compiler_params=pltpu.CompilerParams(
+            collective_id=collective_id, has_side_effects=True, vmem_limit_bytes=VMEM_LIMIT
+        ),
+        name="tail",
+    )(
+        grad, kind, fc1, fc2, index, index.reshape(places, 1), mod, sums, conds,
+        tokens, grad_middle, grad_hidden,
+    )
+
+
+def adam_kernel(odd_ref, factor_ref, own_ref, other_ref, fc1_ref, fc1_other_ref, fc2_ref, ada_ref, *refs):
+    weights, outs = refs[:15], refs[15:]
+    odd = odd_ref[0] == 1
+    factor = factor_ref[0]
+    qkv = weights[0].shape[1]
+    proj = weights[1].shape[0]
+    fc1 = weights[2].shape[1]
+
+    def pair(own, other):
+        own, other = own[...].astype(jnp.float32), other[...].astype(jnp.float32)
+        return jnp.where(odd, other, own), jnp.where(odd, own, other)
+
+    def half(block, first, cols):
+        return jnp.where(
+            odd, block[:, first + cols : first + 2 * cols], block[:, first : first + cols]
+        )
+
+    def step(n, rows, grad):
+        new = adamw(weights[n][rows], weights[5 + n][rows], weights[10 + n][rows], grad * factor)
+        for k in range(3):
+            outs[5 * k + n][rows] = new[k]
+
+    projs = []
+    for k, block in enumerate(pair(own_ref, other_ref)):
+        rows = slice(k * BLOCK_ROWS, (k + 1) * BLOCK_ROWS)
+        step(0, rows, half(block, 0, qkv))
+        projs.append(half(block, 2 * qkv, proj))
+    step(1, slice(None), jnp.transpose(jnp.concatenate(projs, axis=0)))
+    for k, block in enumerate(pair(fc1_ref, fc1_other_ref)):
+        rows = slice(k * BLOCK_ROWS, (k + 1) * BLOCK_ROWS)
+        step(2, rows, half(block, 0, fc1))
+    step(3, slice(None), fc2_ref[...].astype(jnp.float32))
+    step(4, slice(None), ada_ref[...])
+
+
+def adam_all(odd, factor, sums, weights):
+    turn = lambda values: [v.T if n % 5 in (1, 3) else v for n, v in enumerate(values)]
+    weights = turn(weights)
+    vmem = pl.BlockSpec(memory_space=pltpu.VMEM)
+    smem = pl.BlockSpec(memory_space=pltpu.SMEM)
+    new = pl.pallas_call(
+        adam_kernel,
+        in_specs=[smem, smem] + [vmem] * (6 + 15),
+        out_specs=[vmem] * 15,
+        out_shape=[jax.ShapeDtypeStruct(w.shape, w.dtype) for w in weights],
+        compiler_params=pltpu.CompilerParams(vmem_limit_bytes=VMEM_LIMIT),
+        name="adam_all",
+    )(odd, factor, *sums, *weights)
+    return turn(new)
+
+
+def spread(actions, slots):
+    middle = actions[1:-1]
+    groups = [[] for _ in range(slots)]
+    groups[0].append(actions[0])
+    for n, action in enumerate(middle):
+        groups[1 + n * (slots - 1) // len(middle)].append(action)
+    return groups, actions[-1]
+
+
+def run_slot(step, groups, first, count, stride=1):
+    for k in range(count):
+        group = groups[first + k * stride]
+
+        @pl.when(step == k)
+        def _():
+            for action in group:
+                action()
+
+
+def fixed(*shape):
+    return pl.BlockSpec(shape, lambda *_: (0,) * len(shape))
+
+
+def once(*shape):
+    return pl.BlockSpec(shape, lambda *_: (0,) * len(shape), pipeline_mode=pl.Buffered(1))
+
+
+def chosen_rows(index_ref, region):
+    rows = lax.broadcasted_iota(jnp.int32, (REGION, index_ref.shape[1]), 0) + region * REGION
+    return (rows == index_ref[...]).astype(jnp.float32)
+
+
+GATHER_PLANS = ((False, (0,)), (True, (3,)))
+SCATTER_PLANS = ((False, (0, 3)), (True, (0, 3)))
+SHIFT_ATTN, SCALE_ATTN, GATE_ATTN, SHIFT_MLP, SCALE_MLP, GATE_MLP = range(6)
+GRANULE = 16
+PAIR = 2 * HEAD_DIM
+PAIRS = HEADS // 2
+
+
+def embed_tokens(kind_ref, kept_ref, index_ref, mask_ref, table_ref, mod_ref, tokens, hidden, hidden_t):
+    count = tokens.shape[0]
+    small = kind_ref[0] == 1
+    for region in range(count // REGION):
+        select = chosen_rows(index_ref, region)
+        placed = dot_nn(select.astype(jnp.bfloat16), kept_ref[...])
+        unfilled = 1.0 - jnp.sum(select, axis=1, keepdims=True)
+        tokens[pl.ds(region * REGION, REGION)] = placed + unfilled * mask_ref[...]
+
+    def add_place(g, carry):
+        first = pl.multiple_of((g % 2) * GRANULE, GRANULE)
+        wide = table_ref[0, pl.ds(g // 2, 1), :] + table_ref[1, pl.ds(first, GRANULE), :]
+        narrow = table_ref[0, pl.ds(g % 16, 1), :] + table_ref[1, :GRANULE]
+        place = jnp.where(small, narrow, wide)
+        spot = pl.ds(pl.multiple_of(g * GRANULE, GRANULE), GRANULE)
+        tokens[spot, :] = tokens[spot, :] + place
+        return carry
+
+    lax.fori_loop(0, count // GRANULE, add_place, 0)
+    for region in range(count // REGION):
+        spot = slice(region * REGION, (region + 1) * REGION)
+        normal, _ = norm_parts(tokens[spot])
+        value = normal * (1.0 + mod_ref[SCALE_ATTN, region : region + 1])
+        value = (value + mod_ref[SHIFT_ATTN, region : region + 1]).astype(jnp.bfloat16)
+        hidden[spot] = value
+        hidden_t[:, spot] = jnp.transpose(value)
+
+
+def forward_kernel(
+    kind_ref,
+    kept_ref,
+    index_ref,
+    mask_ref,
+    table_ref,
+    mod_ref,
+    weight_ref,
+    fc1_ref,
+    fc2_ref,
+    swap_ref,
+    qkv_out,
+    attended_out,
+    lse_out,
+    branch_out,
+    middle_out,
+    hidden_out,
+    hidden_t_out,
+    gated_out,
+    gated_t_out,
+    tokens_hbm,
+    normed_t_hbm,
+    proj_hbm,
+    grad_hbm,
+    fc1_full,
+    fc2_full,
+    tokens,
+    normed,
+    normed_t,
+    qkv,
+    attended,
+    proj,
+    grad,
+    out_sems,
+    *sems,
+):
+    step = pl.program_id(0)
+    rows = qkv_out.shape[0]
+    groups = qkv.shape[0] // rows
+    regions = tokens.shape[0] // REGION
+    cols = D // groups
+    place = Place()
+    meet = functools.partial(greet, band=True)
+    actions = gather_actions(
+        place, GATHER_PLANS, [fc1_ref, fc2_ref], [fc1_full, fc2_full], *sems[:4], meet=meet
+    )
+    swap_start, swap_wait = swap_band(place, swap_ref, grad, *sems[4:])
+    actions.insert(4, swap_start)
+    slots, finish = spread(actions, groups + 2 * PAIRS + regions)
+    outward = [
+        pltpu.make_async_copy(source, target, out_sems.at[n])
+        for n, (source, target) in enumerate(
+            [(tokens, tokens_hbm), (normed_t, normed_t_hbm), (proj, proj_hbm), (grad, grad_hbm)]
+        )
+    ]
+
+    run_slot(step, slots, 0, groups)
+
+    @pl.when(step == 0)
+    def _():
+        embed_tokens(
+            kind_ref, kept_ref, index_ref, mask_ref, table_ref, mod_ref, tokens, normed, normed_t
+        )
+        outward[0].start()
+        outward[1].start()
+
+    @pl.when(step < groups)
+    def _():
+        span = -(-rows // 128) * 128
+        wide = dot_nn(normed[...], weight_ref[:, :span]).astype(jnp.bfloat16)
+        part = jnp.transpose(wide)[:rows]
+        qkv_out[...] = part
+        qkv[pl.ds(pl.multiple_of(step * rows, 16), rows), :] = part
+        for g in range(groups):
+
+            @pl.when(step == g)
+            def _():
+                proj[:, g * cols : (g + 1) * cols] = weight_ref[:, rows:]
+
+    pair = step - groups
+
+    @pl.when((pair >= 0) & (pair < PAIRS))
+    def _():
+        @pl.when(pair == 0)
+        def _():
+            outward[2].start()
+
+        other = jnp.where(kind_ref[0] == 1, MASKED, 0.0)
+        spot = lambda part: pl.ds(pl.multiple_of(part * D + pair * PAIR, 16), PAIR)
+        for half in range(2):
+            run_slot(pair, slots, groups + half, PAIRS, 2)
+            head = slice(half * HEAD_DIM, (half + 1) * HEAD_DIM)
+            attn_head(
+                other,
+                qkv[spot(0), :][head],
+                qkv[spot(1), :][head],
+                qkv[spot(2), :][head],
+                attended_out,
+                head,
+                lse_out.at[half],
+            )
+        attended[spot(0), :] = attended_out[...]
+
+    region = step - groups - PAIRS
+    run_slot(region, slots, groups + 2 * PAIRS, regions)
+
+    @pl.when(region >= 0)
+    def _():
+        @pl.when(region == 0)
+        def _():
+            swap_wait()
+            outward[3].start()
+
+        spot = pl.ds(pl.multiple_of(region * REGION, REGION), REGION)
+        part = lambda k: mod_ref[k, pl.ds(region, 1), :]
+        branch = dot_nn(jnp.transpose(attended[:, spot]), proj[...])
+        middle = tokens[spot, :] + part(GATE_ATTN) * branch
+        normal, _ = norm_parts(middle)
+        hidden = (normal * (1.0 + part(SCALE_MLP)) + part(SHIFT_MLP)).astype(jnp.bfloat16)
+        gated = (part(GATE_MLP) * grad[region].astype(jnp.float32)).astype(jnp.bfloat16)
+        branch_out[...] = branch
+        middle_out[...] = middle
+        hidden_out[...] = hidden
+        hidden_t_out[...] = jnp.transpose(hidden)
+        gated_out[...] = gated
+        gated_t_out[...] = jnp.transpose(gated)
+
+    @pl.when(region == regions - 1)
+    def _():
+        finish()
+        for copy in outward:
+            copy.wait()
+
+
+def forward(kind, kept, index, mask, tables, mod, weights, blocks, swap, collective_id):
+    width = kept.shape[1]
+    regions = mod.shape[1]
+    count = regions * REGION
+    groups = weights.shape[1] // BLOCK_COLS
+    rows = 3 * D // groups
+    shape = jax.ShapeDtypeStruct
+    bf16, f32 = jnp.bfloat16, jnp.float32
+    group = lambda s: jnp.minimum(s, groups - 1)
+    pair = lambda s: jnp.clip(s - groups, 0, PAIRS - 1)
+    region = lambda s: jnp.clip(s - groups - PAIRS, 0, regions - 1)
+    token_rows = pl.BlockSpec((REGION, width), lambda s: (region(s), 0))
+    token_cols = pl.BlockSpec((width, REGION), lambda s: (0, region(s)))
+    hbm = pl.BlockSpec(memory_space=pl.ANY)
+    whole = shape((8 * BLOCK_ROWS, 4 * BLOCK_COLS), bf16)
+    return pl.pallas_call(
+        forward_kernel,
+        grid=(groups + PAIRS + regions,),
+        in_specs=[
+            pl.BlockSpec(memory_space=pltpu.SMEM),
+            once(*kept.shape),
+            once(*index.shape),
+            once(1, width),
+            once(*tables.shape),
+            once(*mod.shape),
+            pl.BlockSpec((width, BLOCK_COLS), lambda s: (0, group(s))),
+            once(BLOCK_ROWS, BLOCK_COLS),
+            once(BLOCK_ROWS, BLOCK_COLS),
+            hbm,
+        ],
+        out_specs=[
+            pl.BlockSpec((rows, count), lambda s: (group(s), 0)),
+            pl.BlockSpec((PAIR, count), lambda s: (pair(s), 0)),
+            pl.BlockSpec((2, 1, count), lambda s: (pair(s), 0, 0)),
+            token_rows,
+            token_rows,
+            token_rows,
+            token_cols,
+            token_rows,
+            token_cols,
+        ]
+        + [hbm] * 6,
+        out_shape=[
+            shape((3 * D, count), bf16),
+            shape((D, count), bf16),
+            shape((HEADS, 1, count), f32),
+            shape((count, width), f32),
+            shape((count, width), f32),
+            shape((count, width), bf16),
+            shape((width, count), bf16),
+            shape((count, width), bf16),
+            shape((width, count), bf16),
+            shape((count, width), f32),
+            shape((width, count), bf16),
+            shape((width, width), bf16),
+            shape(swap.shape, swap.dtype),
+            whole,
+            whole,
+        ],
+        scratch_shapes=[
+            pltpu.VMEM((count, width), f32),
+            pltpu.VMEM((count, width), bf16),
+            pltpu.VMEM((width, count), bf16),
+            pltpu.VMEM((3 * D, count), bf16),
+            pltpu.VMEM((D, count), bf16),
+            pltpu.VMEM((width, width), bf16),
+            pltpu.VMEM(swap.shape, swap.dtype),
+            pltpu.SemaphoreType.DMA((4,)),
+        ]
+        + gather_scratch(2)
+        + swap_scratch(),
+        compiler_params=pltpu.CompilerParams(
+            collective_id=collective_id, has_side_effects=True, vmem_limit_bytes=VMEM_LIMIT
+        ),
+        name="forward",
+    )(kind, kept, index, mask, tables, mod, weights, *blocks, swap)
+
+
+def backward_kernel(
+    kind_ref,
+    q_ref,
+    k_ref,
+    v_ref,
+    attended_ref,
+    grad_ref,
+    lse_ref,
+    weight_ref,
+    normed_t_ref,
+    proj_ref,
+    fc1_ref,
+    fc2_ref,
+    swap_ref,
+    out_ref,
+    fc1_sum,
+    fc2_sum,
+    hidden_hbm,
+    swapped_hbm,
+    grads,
+    staged,
+    grad_hidden,
+    out_sem,
+    *sems,
+):
+    step = pl.program_id(0)
+    rows = grads.shape[0] // (pl.num_programs(0) - PAIRS)
+    groups = grads.shape[0] // rows
+    cols = BLOCK_COLS - rows
+    place = Place()
+    meet = functools.partial(greet, band=True)
+    swap_start, swap_wait = swap_band(place, swap_ref, swapped_hbm, *sems[7:])
+    actions = scatter_actions(
+        place, SCATTER_PLANS, [fc1_ref, fc2_ref], [fc1_sum, fc2_sum], *sems[:7], meet=meet
+    )
+    actions.insert(len(actions) // 2, swap_start)
+    slots, finish = spread(actions, 2 * PAIRS + groups)
+
+    @pl.when(step < PAIRS)
+    def _():
+        other = jnp.where(kind_ref[0] == 1, MASKED, 0.0)
+        for half in range(2):
+            run_slot(step, slots, half, PAIRS, 2)
+            head = slice(half * HEAD_DIM, (half + 1) * HEAD_DIM)
+            attn_head_back(
+                other,
+                q_ref[head],
+                k_ref[head],
+                v_ref[head],
+                attended_ref[head],
+                grad_ref[head],
+                lse_ref.at[half],
+                staged,
+                head,
+            )
+        for part in range(3):
+            spot = pl.ds(pl.multiple_of(part * D + step * PAIR, 16), PAIR)
+            grads[spot, :] = staged[part]
+
+    group = step - PAIRS
+    run_slot(group, slots, 2 * PAIRS, groups)
+
+    @pl.when(group >= 0)
+    def _():
+        grad = grads[pl.ds(pl.multiple_of(group * rows, 16), rows), :]
+        added = dot_nt(jnp.transpose(grad), weight_ref[:, :rows])
+
+        @pl.when(group == 0)
+        def _():
+            grad_hidden[...] = added
+
+        @pl.when(group > 0)
+        def _():
+            grad_hidden[...] += added
+
+        out_ref[:, :rows] = dot_nt(normed_t_ref[...], grad).astype(jnp.bfloat16)
+        for g in range(groups):
+
+            @pl.when(group == g)
+            def _():
+                out_ref[:, rows:] = proj_ref[:, g * cols : (g + 1) * cols]
+
+    @pl.when(group == groups - 1)
+    def _():
+        outward = pltpu.make_async_copy(grad_hidden, hidden_hbm, out_sem.at[0])
+        outward.start()
+        finish()
+        swap_wait()
+        outward.wait()
+
+
+def backward(
+    kind, qkv, attended, grad_attended, lse, weights, normed_t, grad_proj, grads, swap, collective_id
+):
+    width, count = normed_t.shape
+    groups = weights.shape[1] // BLOCK_COLS
+    shape = jax.ShapeDtypeStruct
+    bf16, f32 = jnp.bfloat16, jnp.float32
+    pair = lambda s: jnp.minimum(s, PAIRS - 1)
+    group = lambda s: jnp.maximum(s - PAIRS, 0)
+    heads = lambda part: pl.BlockSpec((PAIR, count), lambda s: (pair(s) + part * PAIRS, 0))
+    hbm = pl.BlockSpec(memory_space=pl.ANY)
+    block = shape((BLOCK_ROWS, BLOCK_COLS), bf16)
+    return pl.pallas_call(
+        backward_kernel,
+        grid=(PAIRS + groups,),
+        in_specs=[
+            pl.BlockSpec(memory_space=pltpu.SMEM),
+            heads(0),
+            heads(1),
+            heads(2),
+            heads(0),
+            heads(0),
+            pl.BlockSpec((2, 1, count), lambda s: (pair(s), 0, 0)),
+            pl.BlockSpec((width, BLOCK_COLS), lambda s: (0, group(s))),
+            once(width, count),
+            once(width, D),
+            hbm,
+            hbm,
+            hbm,
+        ],
+        out_specs=[
+            pl.BlockSpec((width, BLOCK_COLS), lambda s: (0, group(s))),
+            fixed(BLOCK_ROWS, BLOCK_COLS),
+            fixed(BLOCK_ROWS, BLOCK_COLS),
+            hbm,
+            hbm,
+        ],
+        out_shape=[
+            shape(weights.shape, bf16),
+            block,
+            block,
+            shape((count, width), f32),
+            shape(swap.shape, swap.dtype),
+        ],
+        scratch_shapes=[
+            pltpu.VMEM((3 * D, count), bf16),
+            pltpu.VMEM((3, PAIR, count), bf16),
+            pltpu.VMEM((count, width), f32),
+            pltpu.SemaphoreType.DMA((1,)),
+        ]
+        + scatter_scratch(2)
+        + swap_scratch(),
+        compiler_params=pltpu.CompilerParams(
+            collective_id=collective_id, has_side_effects=True, vmem_limit_bytes=VMEM_LIMIT
+        ),
+        name="backward",
+    )(kind, qkv, qkv, qkv, attended, grad_attended, lse, weights, normed_t, grad_proj, *grads, swap)
+
+
+def local_call(kernel, grid, in_specs, out_specs, out_shape, scratch, name, *operands):
+    return pl.pallas_call(
+        kernel,
+        grid=grid,
+        in_specs=in_specs,
+        out_specs=out_specs,
+        out_shape=out_shape,
+        scratch_shapes=scratch,
+        compiler_params=pltpu.CompilerParams(vmem_limit_bytes=VMEM_LIMIT),
+        name=name,
+    )(*operands)
+
+
+def column_sum(values):
+    return jnp.sum(values, axis=0, keepdims=True)
+
+
+def after_kernel(
+    output_ref,
+    grad_hidden_ref,
+    middle_ref,
+    branch_ref,
+    grad_ref,
+    attended_ref,
+    proj_ref,
+    mod_ref,
+    block_ref,
+    grad_middle_ref,
+    grad_proj_ref,
+    grad_attended_ref,
+    sums_ref,
+    total_ref,
+):
+    region = pl.program_id(0)
+    part = lambda k: mod_ref[k, pl.ds(region, 1), :]
+    output = output_ref[...]
+    grad_hidden = grad_hidden_ref[...]
+    middle = middle_ref[...]
+    grad = grad_ref[...].astype(jnp.float32)
+    block_ref[...] = (middle + part(GATE_MLP) * output).astype(jnp.bfloat16)
+    normal, root = norm_parts(middle)
+    grad_middle = grad + norm_back(grad_hidden, normal, root, part(SCALE_MLP))
+    grad_middle_ref[...] = grad_middle
+    sums_ref[0, 0:1] = column_sum(grad_middle * branch_ref[...])
+    sums_ref[0, 1:2] = column_sum(grad_hidden)
+    sums_ref[0, 2:3] = column_sum(grad_hidden * normal)
+    sums_ref[0, 3:4] = column_sum(grad * output)
+    grad_branch = (part(GATE_ATTN) * grad_middle).astype(jnp.bfloat16)
+    grad_attended_ref[...] = dot_nt(proj_ref[...], grad_branch).astype(jnp.bfloat16)
+    added = dot_nn(attended_ref[...], grad_branch)
+
+    @pl.when(region == 0)
+    def _():
+        total_ref[...] = added
+
+    @pl.when(region > 0)
+    def _():
+        total_ref[...] += added
+
+    @pl.when(region == pl.num_programs(0) - 1)
+    def _():
+        grad_proj_ref[...] = total_ref[...].astype(jnp.bfloat16)
+
+
+def after_mlp(output, grad_hidden, middle, branch, grad, attended_t, proj, mod):
+    count, width = middle.shape
+    regions = count // REGION
+    rows = pl.BlockSpec((REGION, width), lambda r: (r, 0))
+    columns = pl.BlockSpec((width, REGION), lambda r: (0, r))
+    shape = jax.ShapeDtypeStruct
+    return local_call(
+        after_kernel,
+        (regions,),
+        [rows, rows, rows, rows, rows, columns, fixed(width, width), fixed(*mod.shape)],
+        [
+            rows,
+            rows,
+            fixed(width, width),
+            columns,
+            pl.BlockSpec((1, 4, width), lambda r: (r, 0, 0)),
+        ],
+        [
+            shape((count, width), jnp.bfloat16),
+            shape((count, width), jnp.float32),
+            shape((width, width), jnp.bfloat16),
+            shape((width, count), jnp.bfloat16),
+            shape((regions, 4, width), jnp.float32),
+        ],
+        [pltpu.VMEM((width, width), jnp.float32)],
+        "after_mlp",
+        output,
+        grad_hidden,
+        middle,
+        branch,
+        grad,
+        attended_t,
+        proj,
+        mod,
+    )
+
+
+def swap_columns(shard):
+    pairs = [(d, d ^ 1) for d in range(lax.axis_size("dp"))]
+    odd = lax.axis_index("dp") % 2
+    rows = shard.shape[0] // 2
+    own = lax.dynamic_slice_in_dim(shard, odd * rows, rows, axis=0)
+    other = lax.dynamic_slice_in_dim(shard, (1 - odd) * rows, rows, axis=0)
+    other = lax.ppermute(other, "dp", pairs)
+    return jnp.where(odd == 0, jnp.stack([own, other], 1), jnp.stack([other, own], 1))
+
+
+def norm_parts(values):
+    center = jnp.mean(values, axis=-1, keepdims=True)
+    spread = jnp.mean((values - center) ** 2, axis=-1, keepdims=True)
+    root = lax.rsqrt(spread + 1e-06)
+    return ((values - center) * root, root)
+
+
+def norm_back(grad, normal, root, scales):
+    inner = grad * (1.0 + scales)
+    return root * (
+        inner
+        - jnp.mean(inner, axis=-1, keepdims=True)
+        - normal * jnp.mean(inner * normal, axis=-1, keepdims=True)
+    )
+
+
+def embed_tables(count):
+    quarter = D // 4
+    omegas = 1.0 / 10000.0 ** (jnp.arange(quarter, dtype=jnp.float32) / quarter)
+    angles = jnp.arange(count, dtype=jnp.float32)[:, None] * omegas
+    return jnp.concatenate([jnp.sin(angles), jnp.cos(angles)], axis=-1)
+
+
+def slot_device(
+    kept_tokens,
+    kept_index,
+    resolution,
+    labels,
+    timesteps,
+    class_table,
+    cotangent,
+    mask_token,
+    w_qkv,
+    w_proj,
+    w_fc1,
+    w_fc2,
+    w_ada,
+    mask_first,
+    first_qkv,
+    first_proj,
+    first_fc1,
+    first_fc2,
+    first_ada,
+    mask_second,
+    second_qkv,
+    second_proj,
+    second_fc1,
+    second_fc2,
+    second_ada,
+):
+    highest = lax.Precision.HIGHEST
+    bf16 = jnp.bfloat16
+    bands = lax.axis_size("band")
+    groups = lax.axis_size("dp")
+    band = lax.axis_index("band")
+    slots, local_rows, _ = cotangent.shape
+    tokens_count = bands * local_rows
+    regions = tokens_count // REGION
+    images = labels.shape[1]
+
+    qkv_cols, proj_cols, fc1_cols = w_qkv.shape[1], w_proj.shape[1], w_fc1.shape[1]
+    swapped = swap_columns(jnp.concatenate([w_qkv, w_proj, w_fc1], axis=1).astype(bf16))
+    joined_block = jnp.concatenate(
+        [
+            swapped[:, :, :qkv_cols].reshape(-1, 2 * qkv_cols),
+            swapped[:, :, qkv_cols:-fc1_cols].reshape(-1, 2 * proj_cols),
+        ],
+        axis=1,
+    )
+    fc1_block = swapped[:, :, -fc1_cols:].reshape(-1, 2 * fc1_cols)
+    fc2_block = w_fc2.astype(bf16).T
+
+    rows_ada, cols_ada = w_ada.shape
+    table_part = lax.dynamic_slice_in_dim(class_table, band * rows_ada, rows_ada, axis=1)
+    chosen = labels.reshape(-1, 1) == jnp.arange(class_table.shape[0])[None, :]
+    features = band * rows_ada + jnp.arange(rows_ada)
+    half_width = D // 2
+    frequency = jnp.exp(
+        -math.log(10000.0) * (features % half_width).astype(jnp.float32) / half_width
+    )
+    angles = timesteps.reshape(-1, 1).astype(jnp.float32) * frequency
+    waves = jnp.where(features < half_width, jnp.cos(angles), jnp.sin(angles))
+    condition = jnp.matmul(chosen.astype(jnp.float32), table_part, precision=highest) + waves
+    cond = jax.nn.silu(condition).astype(bf16).astype(jnp.float32)
+    cond = jnp.pad(cond.reshape(slots, images, rows_ada), ((0, 0), (0, 8 - images), (0, 0)))
+
+    kind = lax.dynamic_slice_in_dim(resolution, band, 1)
+    joined_full, modulation, conds, kept, index = head(
+        joined_block, cond, w_ada.astype(bf16), kept_tokens, kept_index[:, None, :], 0
+    )
+    kept = kept.reshape(-1, D)
+    index = index.reshape(1, -1)
+    modulation = modulation.transpose(1, 0, 2).reshape(images, 6, D).transpose(1, 0, 2)
+    mod = jnp.where(kind[0] == 1, modulation, modulation[:, :1])
+    table = embed_tables(SIDE)
+    blank = jnp.zeros_like(table)
+    tables = jnp.stack(
+        [jnp.concatenate([table, blank], axis=1), jnp.concatenate([blank, table], axis=1)]
+    )
+    (
+        qkv,
+        attended_t,
+        lse,
+        branch,
+        middle,
+        hidden_mlp,
+        hidden_mlp_t,
+        grad_output,
+        grad_output_t,
+        tokens,
+        normed_t,
+        proj_full,
+        grad_out,
+        fc1_full,
+        fc2_full,
+    ) = forward(
+        kind,
+        kept,
+        index,
+        mask_token[None],
+        tables,
+        mod,
+        joined_full,
+        [fc1_block, fc2_block],
+        cotangent,
+        1,
+    )
+    grad_out = grad_out.reshape(tokens_count, D)
+    output, grad_hidden_mlp, grad_fc1, grad_fc2 = mlp_both(
+        hidden_mlp, hidden_mlp_t, grad_output, grad_output_t, fc1_full, fc2_full, 512
+    )
+    block_slot, grad_middle, grad_proj, grad_attended, sums_mlp = after_mlp(
+        output, grad_hidden_mlp, middle, branch, grad_out, attended_t, proj_full, mod
+    )
+    grad_joined, sum_fc1, sum_fc2, grad_hidden, block_out = backward(
+        kind,
+        qkv,
+        attended_t,
+        grad_attended,
+        lse,
+        joined_full,
+        normed_t,
+        grad_proj,
+        [grad_fc1, grad_fc2],
+        block_slot.reshape(bands, local_rows, D),
+        2,
+    )
+    sum_joined, other_joined, other_fc1, red_ada, grad_mask, squares, grad_kept = tail(
+        grad_joined,
+        kind,
+        sum_fc1,
+        sum_fc2,
+        index,
+        mod,
+        sums_mlp,
+        conds,
+        tokens,
+        grad_middle,
+        grad_hidden,
+        bands,
+        3,
+    )
+    kept_grad = grad_kept.astype(jnp.float32)
+    grad_mask = grad_mask[0]
+    norm_value = jnp.sqrt(squares[0, 0] + jnp.sum(grad_mask * grad_mask))
+    factor = clip_level / jnp.maximum(norm_value, clip_level)
+    mask_new = adamw(mask_token, mask_first, mask_second, grad_mask * factor)
+    odd = (lax.axis_index("dp") % 2).astype(jnp.int32)
+    new = adam_all(
+        odd[None],
+        factor[None],
+        [sum_joined, other_joined, sum_fc1, other_fc1, sum_fc2, red_ada],
+        [
+            w_qkv, w_proj, w_fc1, w_fc2, w_ada,
+            first_qkv, first_proj, first_fc1, first_fc2, first_ada,
+            second_qkv, second_proj, second_fc1, second_fc2, second_ada,
+        ],
+    )
+    return (
+        (block_out, kept_grad, norm_value)
+        + (mask_new[0], *new[:5])
+        + (mask_new[1], *new[5:10])
+        + (mask_new[2], *new[10:])
+    )
+
+
+def per_device(*arguments):
+    cotangent = arguments[6]
+    if (lax.axis_size("dp"), lax.axis_size("band")) == (8, cotangent.shape[0]):
+        return slot_device(*arguments)
+    return general_device(*arguments)
+
+
 def solution(mesh):
     in_specs = (
         P("dp", "band", None),

time: 2250 us -> 616 us (0.27)
  waiting for transfers between devices: 1270 us -> 0.01 us
  Pallas kernels: 0 us -> 576 us
  matrix products: 572 us -> 2.38 us
  local copies, waits for them, and re-layouts: 188 us -> 11.8 us
  other arithmetic: 108 us -> 13.7 us
  blocking collectives: 81.1 us -> 0 us
    pallas_call x0 -> x7, Pallas kernels: none -> 576 us  [the longest x1 145 us: backward(): pl.pallas_call(backward_kernel, grid=(PAIRS + groups,), in_specs=[pl.Bloc...]
    dot_general x45 -> x1, matrix products: 572 us -> 2.38 us  [slot_device(): jnp.matmul(chosen.astype(jnp.float32), table_part, precision=highest)]
    all_gather x12 -> x0, waiting for transfers between devices: 453 us -> none  [the longest x1 90.2 us: per_device(): lax.all_gather(cols_ada, 'band', axis=0, tiled=True)]
    reduce_scatter x8 -> x0, waiting for transfers between devices: 432 us -> none  [the longest x1 120 us: per_device(): lax.psum_scatter(grad_ada.astype(jnp.bfloat16), 'band', scatter_dimension...]
    unnamed x30 -> x0, waiting for transfers between devices: 386 us -> none
    unnamed x142 -> x18, local copies, waits for them, and re-layouts: 64.8 us -> 3.31 us
    gather x3 -> x0, local copies, waits for them, and re-layouts: 59 us -> none  [the longest x1 56 us: pick_rows(): return table_rows[picks]]
    reduce_sum x16 -> x1, other arithmetic: 44.8 us -> 1.38 us  [slot_device(): norm_value = jnp.sqrt(squares[0, 0] + jnp.sum(grad_mask * grad_mask))]
  transfers between devices with their start and end apart: 25 -> 1, of which waited for: 21 -> 0; matrix products, arithmetic and copies ran while one was open for 21% -> 1% of each run, Pallas kernels for 0% -> 0%
where the time goes in v4:
time: 616 us; the launch traced here: 611 us
  Pallas kernels  576 us (94%)
  other arithmetic  13.7 us (2%)
  local copies, waits for them, and re-layouts  11.8 us (2%)
    pallas_call x1, Pallas kernels, backward(): pl.pallas_call(backward_kernel, grid=(PAIRS + groups,), in_specs=[pl.Bloc...  145 us
    pallas_call x1, Pallas kernels, forward(): pl.pallas_call(forward_kernel, grid=(groups + PAIRS + regions,), in_specs...  144 us
    pallas_call x1, Pallas kernels, tail(): pl.pallas_call(tail_kernel, in_specs=[hbm, pl.BlockSpec(memory_space=pltp...  97.1 us
    pallas_call x1, Pallas kernels, head(): pl.pallas_call(head_kernel, in_specs=[vmem, vmem, vmem, hbm, hbm], out_sp...  79.4 us
    pallas_call x1, Pallas kernels, mlp_both(): pl.pallas_call(mlp_kernel, grid=(wide // tile,), in_specs=[whole((tokens,...  78.9 us
    pallas_call x1, Pallas kernels, local_call(): pl.pallas_call(kernel, grid=grid, in_specs=in_specs, out_specs=out_specs,...  19.7 us
  transfers between devices with their start and end apart: 1, of which 0 were waited for; matrix products, arithmetic and copies ran while one was open for 1% of the time, Pallas kernels for 0%

profile of v4, /device:TPU:0, one launch (start us, length us, event | category | flops | bytes accessed | tf_op | source)
XLA Modules:
  0.0 611.0 jit_solution(13989583391784553391)
XLA Ops:
  0.7 1.2 convert.14
  1.9 1.1 convert.12
  3.0 1.0 convert.13
  4.8 3.0 collective-permute-start
  8.4 2.4 multiply_convert_fusion
  10.9 0.8 convert_element_type.39.ada_ref
  11.7 0.8 convert_bitcast_fusion.fc2_ref
  14.9 0.7 pad_maximum_fusion.1.table_ref
  16.9 0.8 pad_maximum_fusion.block_ref
  17.8 79.4 %head.1 = (bf16[1152,4608]{1,0:T(8,128)(2,1)}, f32[8,4,864]{2,1,0:T(4,128)}, f32[8,4,8,288]{3,2,1,0:T(8,128)}, bf16[4,128,1152]{2,1,0:T(8,128)(2,1)}, s32[4,1,128]{2,1,0:T(1,128)}) custom-call(bf16[144,1152]{1,0:T(8,128)(2,1)} %pad_maximum_fusion.block_ref, f32[4,8,288]{2,1,0:T(8,128)} %pad_convert_fusion.cond_ref, ...), custom_call_target="tpu_custom_call" | custom-call | tf_op jit(solution)/shard_map/head/pallas_call | solution.py:808
  97.2 0.9 copy.60
  98.6 1.0 reshape.111.fc1_ref
  99.6 1.5 copy.63.index_t_ref
  101.8 144.0 %forward.1 = (bf16[3456,1024]{1,0:T(8,128)(2,1)}, bf16[1152,1024]{1,0:T(8,128)(2,1)}, f32[16,1,1024]{2,1,0:T(1,128)}, f32[1024,1152]{1,0:T(8,128)}, f32[1024,115...) custom-call(s32[1]{0:T(128)} %dynamic_slice.12.kind_ref, ...), custom_call_target="tpu_custom_call" | custom-call | tf_op jit(solution)/shard_map/forward/pallas_call | solution.py:1495
  245.8 78.9 %mlp_both.1 = (f32[1024,1152]{1,0:T(8,128)}, f32[1024,1152]{1,0:T(8,128)}, bf16[1152,4608]{1,0:T(8,128)(2,1)}, bf16[1152,4608]{1,0:T(8,128)(2,1)}) custom-call(bf16[1024,1152]{1,0:T(8,128)(2,1)} %get-tuple-element.83.h_ref, bf16[1152,1024]{1,0:T(8,128)(2,1)} %get-tuple-element.84.ht_ref, bf16[1024,1152]{1,0:T(8,128)(2,1)} %get-tuple-element.85.g_ref, ...), custom_call_target="tpu_custom_call" | custom-call | tf_op jit(solution)/shard_map/mlp_both/pallas_call | solution.py:466
  324.6 19.7 %after_mlp.1 = (bf16[1024,1152]{1,0:T(8,128)(2,1)}, f32[1024,1152]{1,0:T(8,128)}, bf16[1152,1152]{1,0:T(8,128)(2,1)}, bf16[1152,1024]{1,0:T(8,128)(2,1)}, f32[4,4,1152]{2,1,0:T(4,128)}) custom-call(f32[1024,1152]{1,0:T(8,128)} %get-tuple-element.89.output_ref, f32[1024,1152]{1,0:T(8,128)} %get-tuple-element.90.grad_hidden_ref, ...), custom_call_target="tpu_custom_call" | custom-call | tf_op jit(solution)/shard_map/after_mlp/pallas_call | solution.py:1709
  344.4 145.2 %backward.1 = (bf16[1152,4608]{1,0:T(8,128)(2,1)}, bf16[144,1152]{1,0:T(8,128)(2,1)}, bf16[144,1152]{1,0:T(8,128)(2,1)}, f32[1024,1152]{1,0:T(8,128)}, bf16[4,256,1152]{2,1,0:T(8,128)(2,1)}) custom-call(s32[1]{0:T(128)} %dynamic_slice.12.kind_ref, bf16[3456,1024]{1,0:T(8,128)(2,1)} %get-tuple-element.81.q_ref.k_ref.v_ref, ...), custom_call_target="tpu_custom_call" | custom-call | tf_op jit(solution)/shard_map/backward/pallas_call | solution.py:1661
  489.6 97.1 %tail.1 = (bf16[144,1152]{1,0:T(8,128)(2,1)}, bf16[144,1152]{1,0:T(8,128)(2,1)}, bf16[144,1152]{1,0:T(8,128)(2,1)}, f32[288,864]{1,0:T(8,128)}, f32[8,1152]{1,0:...) custom-call(bf16[1152,4608]{1,0:T(8,128)(2,1)} %get-tuple-element.103.grad_ref, s32[1]{0:T(128)} %dynamic_slice.12.kind_ref, ...), custom_call_target="tpu_custom_call" | custom-call | tf_op jit(solution)/shard_map/tail/pallas_call | solution.py:1176
  586.7 1.2 slice.22
  587.8 1.4 multiply_reduce_fusion.1
  590.6 0.8 multiply_reduce_fusion
  591.4 2.8 convert_element_type.41
  594.9 11.3 %adam_all.1 = (f32[288,432]{1,0:T(8,128)}, f32[144,288]{1,0:T(8,128)}, f32[288,576]{1,0:T(8,128)}, f32[144,1152]{1,0:T(8,128)}, f32[288,864]{1,0:T(8,128)}, /*in...) custom-call(s32[1]{0:T(128)} %bitcast.15.odd_ref, ...), custom_call_target="tpu_custom_call" | custom-call | tf_op jit(solution)/shard_map/adam_all/pallas_call | solution.py:1267
  606.2 3.3 copy.72
  (49 shorter events, 6.2 us)
Async XLA Ops:
  1.8 6.4 %copy-start.6 = (s32[4,4]{1,0:T(4,128)S(1)}, s32[4,4]{1,0:T(4,128)}, u32[]{:S(2)}) copy-start(s32[4,4]{1,0:T(4,128)} %param.29) | copy-start | bytes 196
  1.9 6.5 %copy-start.5 = (s32[4,4]{1,0:T(4,128)S(1)}, s32[4,4]{1,0:T(4,128)}, u32[]{:S(2)}) copy-start(s32[4,4]{1,0:T(4,128)} %param.28) | copy-start | bytes 196
  4.1 6.8 %copy-start = (f32[288,864]{1,0:T(8,128)S(1)}, f32[288,864]{1,0:T(8,128)}, u32[]{:S(2)}) copy-start(f32[288,864]{1,0:T(8,128)} %refs_4_.1) | copy-start | bytes 2985988
  4.6 7.1 %copy-start.1 = (f32[1152,144]{0,1:T(8,128)S(1)}, f32[1152,144]{0,1:T(8,128)}, u32[]{:S(2)}) copy-start(f32[1152,144]{0,1:T(8,128)} %param.36) | copy-start | bytes 1990660
  4.7 7.7 %copy-start.2 = (f32[1152]{0:T(1024)S(1)}, f32[1152]{0:T(1024)}, u32[]{:S(2)}) copy-start(f32[1152]{0:T(1024)} %param.32) | copy-start | bytes 13828
  4.7 8.3 %copy-start.7 = (s32[4]{0:T(128)S(1)}, s32[4]{0:T(128)}, u32[]{:S(2)}) copy-start(s32[4]{0:T(128)} %param.27) | copy-start | bytes 52
  4.8 10.9 %collective-permute-start = (bf16[144,1152]{1,0:T(8,128)(2,1)S(1)}, bf16[144,1152]{1,0:T(8,128)(2,1)S(1)}, u32[]{:S(2)}, u32[]{:S(2)}) collective-permute-start(bf16[144,1152]{1,0:T(8,128)(2,1)S(1)} %get-tuple-element.137), channel_id=1, source_target_pairs={{0,4},{4,0},{8,12},{12,8},{16,20},{20,16},{24,28},{28,24},{1,5},{5... | collective-permute-start | bytes 995336 | tf_op jit(solution)/shard_map/ppermute | solution.py:1815
  586.6 7.6 %copy-start.3 = (f32[1152]{0:T(1024)S(1)}, f32[1152]{0:T(1024)}, u32[]{:S(2)}) copy-start(f32[1152]{0:T(1024)} %param.38) | copy-start | bytes 13828
  586.6 7.6 %copy-start.4 = (f32[1152]{0:T(1024)S(1)}, f32[1152]{0:T(1024)}, u32[]{:S(2)}) copy-start(f32[1152]{0:T(1024)} %param.44) | copy-start | bytes 13828

commit v5 on v4

--- a/solution.py
+++ b/solution.py
@@ -595,15 +595,9 @@
 
 
 GATHER_SENDS = 31
-ARRIVALS = [
-    (1, 0, 0), (0, 1, 0), (0, 0, 1), (3, 0, 0), (1, 0, 1), (1, 1, 0), (2, 0, 0), (3, 1, 0),
-    (3, 0, 1), (2, 0, 1), (2, 1, 0), (0, 1, 1), (1, 1, 1), (3, 1, 1), (2, 1, 1),
-]
-
-
-def gather_actions(
-    place, plans, own_refs, full_refs, local_sems, send_sems, link_sems, core_sems, meet=None
-):
+
+
+def gather_actions(place, plans, own_refs, full_refs, local_sems, send_sems, link_sems, core_sems):
     weights = range(len(own_refs))
     counts = [0] * len(own_refs)
 
@@ -614,7 +608,8 @@
 
     def pass_on(w, source, piece):
         for child, step in children(piece, plans[w][1], False):
-            ship(w, source, piece, child, link_sems, place.device(*step))
+            if step[0] < 2:
+                ship(w, source, piece, child, link_sems, place.device(*step))
         ship(w, source, piece, piece, core_sems, place.device(core=1))
 
     def arrive(w, piece, core=0):
@@ -631,16 +626,15 @@
         )
 
     def begin():
-        (meet or greet)(place)
         for w in weights:
             keep(w).start()
             pass_on(w, own_refs[w], (0, 0, 0))
 
-    def relay(w, piece):
-        def step():
-            pass_on(w, arrive(w, piece), piece)
-
-        return step
+    def relay(w, *piece):
+        pass_on(w, arrive(w, piece), piece)
+
+    def late(w, i):
+        ship(w, own_refs[w], (0, 0, 0), (i, 0, 0), link_sems, place.device(i))
 
     def finish():
         for w in weights:
@@ -653,7 +647,7 @@
                     place.device(core=1),
                 ).wait_send()
 
-    return [begin] + [relay(w, piece) for w in weights for piece in ARRIVALS] + [finish]
+    return begin, relay, late, finish
 
 
 def gather_scratch(count):
@@ -736,9 +730,14 @@
     slots, _, _, cols = part_ref.shape
     images = part_ref.shape[2]
     plans = ((False, (0,)),)
-    actions = gather_actions(
-        place, plans, [block_ref], [full_ref], *rest[:4], meet=lambda _: None
-    )
+    begin, relay, late, finish = gather_actions(
+        place, plans, [block_ref], [full_ref], *rest[:4]
+    )
+
+    def relays(*pieces):
+        for piece in pieces:
+            relay(0, *piece)
+
     kept_start, kept_wait = swap_band(place, kept_ref, kept_out, *rest[4:7])
     index_start, index_wait = swap_band(place, index_ref, index_out, *rest[7:10])
 
@@ -753,15 +752,20 @@
     ]
     for copy in cond_copies:
         copy.start()
-    actions[0]()
+    begin()
     index_start()
     conds_ref[own] = cond_ref[...]
+    late(0, 3)
+    relays((1, 0, 0))
     for copy in cond_copies:
         copy.wait()
     for s in range(slots):
         rows = conds_ref[:, s].reshape(-1, cond_ref.shape[-1]).astype(jnp.bfloat16)
         product = dot_nn(rows, ada_ref[...])
         part_ref[s] = product.reshape(-1, cond_ref.shape[1], cols)[:, :images]
+    relays((0, 1, 0))
+    late(0, 2)
+    relays((1, 0, 1), (1, 1, 0), (3, 0, 0))
     part_copies = [
         send(
             part_ref.at[place.band(b, core)],
@@ -774,14 +778,12 @@
     ]
     for copy in part_copies:
         copy.start()
-    for action in actions[1:4]:
-        action()
+    relays((3, 0, 1), (2, 0, 0), (0, 0, 1), (0, 1, 1), (3, 1, 0))
     kept_start()
-    for action in actions[4:8]:
-        action()
     for copy in part_copies:
         copy.wait()
     sums_ref[...] = part_ref[place.band()] + got_ref[0] + got_ref[1] + got_ref[2]
+    relays((1, 1, 1))
     mod_copies = [
         to_dp(n, sums_ref.at[place.dp(*DP_PEERS[n])], mod_ref.at[own], mod_sends, mod_recvs)
         for n in range(7)
@@ -789,8 +791,8 @@
     for copy in mod_copies:
         copy.start()
     mod_ref[own] = sums_ref[own]
-    for action in actions[8:]:
-        action()
+    relays((2, 0, 1), (3, 1, 1), (2, 1, 0), (2, 1, 1))
+    finish()
     for copy in mod_copies:
         copy.wait()
     index_wait()
@@ -837,16 +839,13 @@
     )(block, cond, ada, kept, index)
 
 
-FOLDS = [
-    (1, 1, 1), (3, 1, 1), (2, 1, 1), (0, 1, 1), (1, 0, 0), (1, 1, 0), (1, 0, 1), (3, 1, 0),
-    (3, 0, 1), (2, 1, 0), (2, 0, 1), (0, 1, 0), (0, 0, 1), (3, 0, 0), (2, 0, 0), (0, 0, 0),
-]
 STAGES = 4
 
 
 def scatter_actions(
     place,
     plans,
+    order,
     grad_refs,
     out_refs,
     held_refs,
@@ -856,11 +855,9 @@
     send_sems,
     held_sems,
     over_sems,
-    meet=None,
 ):
     weights = range(len(grad_refs))
     counts = [0] * len(grad_refs)
-    order = [(w, piece) for w in weights for piece in FOLDS]
 
     def ship(w, source, target, recv_sem, device):
         send(source, target, send_sems.at[w, counts[w]], recv_sem, device).start()
@@ -870,14 +867,15 @@
         send(target, target, send_sems.at[0, 0], recv_sem, place.device(core=1)).wait_recv()
 
     def begin():
-        (meet or greet)(place)
-        for w, piece in order:
+        for ahead in range(STAGES - 1):
+            load(ahead).start()
+        for w, *piece in order:
             source = grad_refs[w].at[place.block(plans[w][0], *piece, 1)]
             s = slot(piece)
             ship(w, source, held_refs.at[w, s], held_sems.at[w, s], place.device(core=1))
 
     def load(n):
-        w, piece = order[n]
+        w, *piece = order[n]
         return pltpu.make_async_copy(
             grad_refs[w].at[place.block(plans[w][0], *piece)],
             stage.at[n % STAGES],
@@ -892,38 +890,29 @@
         )
 
     def fold(n):
-        def step():
-            if n == 0:
-                for ahead in range(STAGES - 1):
-                    load(ahead).start()
-            if n + STAGES - 1 < len(order):
-                load(n + STAGES - 1).start()
-            w, piece = order[n]
-            s = slot(piece)
-            load(n).wait()
-            landed(held_refs.at[w, s], held_sems.at[w, s])
-            held = held_refs.at[w, s]
-            held[...] = held[...] + stage[n % STAGES]
-            if not children(piece, plans[w][1], True):
-                up(w, piece)
-
-        return step
-
-    def combine(w, piece):
-        def step():
-            held = held_refs.at[w, slot(piece)]
-            total = held[...].astype(jnp.float32)
-            for child, _ in children(piece, plans[w][1], True):
-                k = slot(child) - 1
-                landed(over_refs.at[w, k], over_sems.at[w, k])
-                total = total + over_refs[w, k].astype(jnp.float32)
-            if any(piece):
-                held[...] = total.astype(jnp.bfloat16)
-                up(w, piece)
-            else:
-                out_refs[w][...] = total.astype(jnp.bfloat16)
-
-        return step
+        if n + STAGES - 1 < len(order):
+            load(n + STAGES - 1).start()
+        w, *piece = order[n]
+        s = slot(piece)
+        load(n).wait()
+        landed(held_refs.at[w, s], held_sems.at[w, s])
+        held = held_refs.at[w, s]
+        held[...] = held[...] + stage[n % STAGES]
+        if not children(tuple(piece), plans[w][1], True):
+            up(w, piece)
+
+    def combine(w, *piece):
+        held = held_refs.at[w, slot(piece)]
+        total = held[...].astype(jnp.float32)
+        for child, _ in children(piece, plans[w][1], True):
+            k = slot(child) - 1
+            landed(over_refs.at[w, k], over_sems.at[w, k])
+            total = total + over_refs[w, k].astype(jnp.float32)
+        if any(piece):
+            held[...] = total.astype(jnp.bfloat16)
+            up(w, piece)
+        else:
+            out_refs[w][...] = total.astype(jnp.bfloat16)
 
     def finish():
         for w in weights:
@@ -933,14 +922,7 @@
                     block, block, send_sems.at[w, n], held_sems.at[w, 0], place.device(core=1)
                 ).wait_send()
 
-    inner = lambda w: [p for p in FOLDS if any(p) and children(p, plans[w][1], True)]
-    early = [[p for p in inner(w) if p[0] and (p[1] or p[2])] for w in weights]
-    late = [[p for p in inner(w) if p not in early[w]] for w in weights]
-    steps = [begin] + [fold(n) for n in range(len(order))]
-    steps += [combine(w, p) for w in weights for p in early[w]]
-    steps += [combine(w, p) for w in weights for p in late[w]]
-    steps += [combine(w, (0, 0, 0)) for w in weights]
-    return steps + [finish]
+    return begin, fold, combine, finish
 
 
 def scatter_scratch(count):
@@ -1019,9 +1001,20 @@
 ):
     place = Place()
     plans = ((False, (0,)),)
-    actions = scatter_actions(
-        place, plans, [grad_ref], [own_ref], *rest[:7], meet=lambda _: None
-    )
+    order = [
+        (3, 1, 1), (0, 1, 1), (3, 0, 1), (1, 0, 0), (1, 1, 0), (2, 1, 1), (3, 1, 0), (3, 0, 0),
+        (1, 1, 1), (2, 0, 1), (1, 0, 1), (2, 1, 0), (0, 0, 1), (0, 0, 0), (0, 1, 0), (2, 0, 0),
+    ]
+    begin, fold, combine, finish = scatter_actions(
+        place, plans, [(0,) + piece for piece in order], [grad_ref], [own_ref], *rest[:7]
+    )
+
+    left = list(range(len(order)))
+
+    def folds(count):
+        for _ in range(count):
+            fold(left.pop(0))
+
     kept_start, kept_wait = swap_band(place, kept, kept_out, *rest[7:10])
     across = lambda n, source, target: send(
         source, target, y_sends.at[n], y_recvs.at[n], place.device(a=1)
@@ -1042,18 +1035,21 @@
     ]
     for copy in loads:
         copy.start()
-    actions[0]()
+    begin()
     fc1_copy = across(0, fc1_ref, fc1_other_ref)
     fc1_copy.start()
-    for action in actions[1:6]:
-        action()
+    folds(4)
     for copy in loads:
         copy.wait()
 
     count = tokens.shape[0]
     regions = count // REGION
-    done = 6
     for region in range(regions):
+        if region == 2:
+            combine(0, 3, 0, 1)
+        folds((0, 2, 2, 2)[region])
+        if region == 3:
+            combine(0, 2, 0, 1)
         spot = slice(region * REGION, (region + 1) * REGION)
         grad = grad_hidden[spot]
         normal, root = norm_parts(tokens[spot])
@@ -1074,9 +1070,6 @@
         else:
             mask_own[...] += jnp.broadcast_to(masked, mask_own.shape)
             kept_total[...] += added
-        for action in actions[done : done + 3]:
-            action()
-        done += 3
     kept[...] = kept_total[...].astype(jnp.bfloat16).reshape(kept.shape)
     images = six.shape[1]
     first = lax.broadcasted_iota(jnp.int32, six.shape[1:], 0) == 0
@@ -1098,9 +1091,10 @@
         copy.start()
     kept_start()
     mods_dp[own] = mods_own[own]
-    for action in actions[done : done + 3]:
-        action()
-    done += 3
+    combine(0, 3, 0, 0)
+    folds(5)
+    combine(0, 1, 0, 1)
+    folds(1)
     for copy in early:
         copy.wait()
     mask_sum[...] = mask_own[...] + mask_band[0] + mask_band[1] + mask_band[2]
@@ -1110,9 +1104,9 @@
         copy.start()
     mods_all[place.band()] = mods_dp[...]
     fc1_copy.wait()
-    for action in actions[done : done + 3]:
-        action()
-    done += 3
+    combine(0, 2, 0, 0)
+    combine(0, 0, 1, 0)
+    combine(0, 0, 0, 1)
     for copy in second:
         copy.wait()
     total = mask_sum[...]
@@ -1131,8 +1125,7 @@
         )
     ada_ref[...] = ada
     squares = square_sum(ada) + square_sum(fc1_ref[...]) + square_sum(fc2_ref[...])
-    for action in actions[done:-1]:
-        action()
+    combine(0, 0, 0, 0)
     last = across(1, own_ref, other_ref)
     last.start()
     squares = squares + square_sum(own_ref[...])
@@ -1154,7 +1147,7 @@
     square_out[...] = total
     last.wait()
     kept_wait()
-    actions[-1]()
+    finish()
 
 
 def tail(
@@ -1275,13 +1268,9 @@
     return turn(new)
 
 
-def spread(actions, slots):
-    middle = actions[1:-1]
-    groups = [[] for _ in range(slots)]
-    groups[0].append(actions[0])
-    for n, action in enumerate(middle):
-        groups[1 + n * (slots - 1) // len(middle)].append(action)
-    return groups, actions[-1]
+def run(actions):
+    for action in actions:
+        action()
 
 
 def run_slot(step, groups, first, count, stride=1):
@@ -1290,8 +1279,7 @@
 
         @pl.when(step == k)
         def _():
-            for action in group:
-                action()
+            run(group)
 
 
 def fixed(*shape):
@@ -1308,17 +1296,43 @@
 
 
 GATHER_PLANS = ((False, (0,)), (True, (3,)))
-SCATTER_PLANS = ((False, (0, 3)), (True, (0, 3)))
+SCATTER_PLANS = ((False, (0,)), (True, (0, 3)))
+FORWARD_STEPS = [
+    (0, 1, 3), (5, 0, 1, 0, 0), (5, 0, 3), (6, 0, 0, 1, 0), (6, 0, 0, 0, 1), (9, 1, 0, 0, 1),
+    (12, 0, 1, 0, 1), (12, 0, 1, 1, 0), (12, 1, 1, 0, 0), (13, 0, 2), (14, 0, 3, 0, 0), (15,),
+    (16, 1, 0, 1, 0), (16, 1, 3, 0, 0), (16, 0, 3, 0, 1), (17, 1, 2), (18, 0, 0, 1, 1),
+    (21, 0, 1, 1, 1), (22, 0, 2, 0, 0), (22, 1, 1, 0, 1), (22, 1, 2, 0, 0), (26, 1, 1, 1, 0),
+    (27, 0, 2, 1, 0), (27, 1, 3, 1, 0), (28, 1, 3, 0, 1), (29, 0, 2, 0, 1), (30, 1, 0, 1, 1),
+    (30, 1, 1, 1, 1), (30, 1, 2, 0, 1), (31, 0, 3, 1, 0), (31, 0, 2, 1, 1), (32, 0, 3, 1, 1),
+    (32, 1, 3, 1, 1), (32, 1, 2, 1, 0), (32, 1, 2, 1, 1),
+]
+BACKWARD_STEPS = [
+    (0, 0, 0, 1, 1, 0), (0,), (0, 0, 0, 0, 0, 1), (0, 0, 0, 3, 1, 1), (0, 0, 0, 1, 1, 1),
+    (0, 0, 0, 1, 0, 1), (1, 0, 1, 1, 0, 0), (1, 0, 1, 1, 1, 1), (1, 0, 1, 3, 1, 1),
+    (2, 0, 1, 1, 1, 0), (2, 0, 0, 2, 0, 0), (2, 0, 0, 3, 0, 1), (3, 1, 0, 3, 0, 1),
+    (3, 0, 0, 2, 1, 1), (3, 0, 1, 3, 0, 1), (4, 0, 1, 0, 1, 1), (4, 0, 0, 3, 0, 0),
+    (6, 1, 0, 1, 0, 1), (6, 0, 0, 3, 1, 0), (6, 0, 1, 1, 0, 1), (6, 0, 1, 2, 1, 0),
+    (7, 0, 1, 3, 1, 0), (7, 0, 1, 0, 0, 0), (7, 0, 0, 0, 0, 0), (10, 0, 0, 1, 0, 0),
+    (10, 0, 1, 2, 0, 1), (10, 1, 0, 3, 0, 0), (10, 1, 1, 3, 1, 0), (11, 0, 1, 3, 0, 0),
+    (11, 0, 1, 2, 1, 1), (11, 0, 1, 0, 1, 0), (11, 0, 0, 2, 0, 1), (12, 0, 0, 0, 1, 0),
+    (13, 1, 0, 2, 0, 1), (13, 1, 1, 3, 0, 0), (14, 0, 0, 2, 1, 0), (14, 1, 1, 1, 0, 1),
+    (15, 0, 0, 0, 1, 1), (17, 1, 0, 2, 0, 0), (17, 0, 1, 2, 0, 0), (17, 1, 1, 2, 0, 1),
+    (17, 0, 1, 0, 0, 1), (18, 1, 0, 0, 1, 0), (19, 1, 0, 0, 0, 1), (19, 1, 1, 2, 0, 0),
+    (19, 1, 1, 0, 0, 1), (20, 1, 1, 0, 1, 0), (21, 1, 0, 0, 0, 0), (23, 1, 1, 0, 0, 0),
+]
 SHIFT_ATTN, SCALE_ATTN, GATE_ATTN, SHIFT_MLP, SCALE_MLP, GATE_MLP = range(6)
 GRANULE = 16
 PAIR = 2 * HEAD_DIM
 PAIRS = HEADS // 2
 
 
-def embed_tokens(kind_ref, kept_ref, index_ref, mask_ref, table_ref, mod_ref, tokens, hidden, hidden_t):
+def embed_tokens(
+    slots, kind_ref, kept_ref, index_ref, mask_ref, table_ref, mod_ref, tokens, hidden, hidden_t
+):
     count = tokens.shape[0]
     small = kind_ref[0] == 1
     for region in range(count // REGION):
+        run(slots[region])
         select = chosen_rows(index_ref, region)
         placed = dot_nn(select.astype(jnp.bfloat16), kept_ref[...])
         unfilled = 1.0 - jnp.sum(select, axis=1, keepdims=True)
@@ -1335,6 +1349,7 @@
 
     lax.fori_loop(0, count // GRANULE, add_place, 0)
     for region in range(count // REGION):
+        run(slots[count // REGION + region])
         spot = slice(region * REGION, (region + 1) * REGION)
         normal, _ = norm_parts(tokens[spot])
         value = normal * (1.0 + mod_ref[SCALE_ATTN, region : region + 1])
@@ -1385,13 +1400,18 @@
     regions = tokens.shape[0] // REGION
     cols = D // groups
     place = Place()
-    meet = functools.partial(greet, band=True)
-    actions = gather_actions(
-        place, GATHER_PLANS, [fc1_ref, fc2_ref], [fc1_full, fc2_full], *sems[:4], meet=meet
+    begin, relay, late, finish = gather_actions(
+        place, GATHER_PLANS, [fc1_ref, fc2_ref], [fc1_full, fc2_full], *sems[:4]
     )
     swap_start, swap_wait = swap_band(place, swap_ref, grad, *sems[4:])
-    actions.insert(4, swap_start)
-    slots, finish = spread(actions, groups + 2 * PAIRS + regions)
+    first_qkv = 1 + 2 * regions
+    first_head = first_qkv + groups
+    first_region = first_head + HEADS
+    slots = [[] for _ in range(first_region + regions)]
+    slots[0] += [functools.partial(greet, place, band=True), begin]
+    for when, *what in FORWARD_STEPS:
+        action = {0: swap_start, 2: late, 4: relay}[len(what)]
+        slots[when].append(functools.partial(action, *what))
     outward = [
         pltpu.make_async_copy(source, target, out_sems.at[n])
         for n, (source, target) in enumerate(
@@ -1399,15 +1419,25 @@
         )
     ]
 
-    run_slot(step, slots, 0, groups)
-
     @pl.when(step == 0)
     def _():
+        run(slots[0])
         embed_tokens(
-            kind_ref, kept_ref, index_ref, mask_ref, table_ref, mod_ref, tokens, normed, normed_t
+            slots[1:first_qkv],
+            kind_ref,
+            kept_ref,
+            index_ref,
+            mask_ref,
+            table_ref,
+            mod_ref,
+            tokens,
+            normed,
+            normed_t,
         )
         outward[0].start()
         outward[1].start()
+
+    run_slot(step, slots, first_qkv, groups)
 
     @pl.when(step < groups)
     def _():
@@ -1433,7 +1463,7 @@
         other = jnp.where(kind_ref[0] == 1, MASKED, 0.0)
         spot = lambda part: pl.ds(pl.multiple_of(part * D + pair * PAIR, 16), PAIR)
         for half in range(2):
-            run_slot(pair, slots, groups + half, PAIRS, 2)
+            run_slot(pair, slots, first_head + half, PAIRS, 2)
             head = slice(half * HEAD_DIM, (half + 1) * HEAD_DIM)
             attn_head(
                 other,
@@ -1447,7 +1477,7 @@
         attended[spot(0), :] = attended_out[...]
 
     region = step - groups - PAIRS
-    run_slot(region, slots, groups + 2 * PAIRS, regions)
+    run_slot(region, slots, first_region, regions)
 
     @pl.when(region >= 0)
     def _():
@@ -1585,13 +1615,22 @@
     groups = grads.shape[0] // rows
     cols = BLOCK_COLS - rows
     place = Place()
-    meet = functools.partial(greet, band=True)
     swap_start, swap_wait = swap_band(place, swap_ref, swapped_hbm, *sems[7:])
-    actions = scatter_actions(
-        place, SCATTER_PLANS, [fc1_ref, fc2_ref], [fc1_sum, fc2_sum], *sems[:7], meet=meet
-    )
-    actions.insert(len(actions) // 2, swap_start)
-    slots, finish = spread(actions, 2 * PAIRS + groups)
+    order = [what[1:] for _, *what in BACKWARD_STEPS if what and not what[0]]
+    begin, fold, combine, finish = scatter_actions(
+        place, SCATTER_PLANS, order, [fc1_ref, fc2_ref], [fc1_sum, fc2_sum], *sems[:7]
+    )
+    slots = [[] for _ in range(HEADS + 2 * groups)]
+    slots[0] += [functools.partial(greet, place, band=True), begin]
+    folded = 0
+    for when, *what in BACKWARD_STEPS:
+        if not what:
+            slots[when].append(swap_start)
+        elif what[0]:
+            slots[when].append(functools.partial(combine, *what[1:]))
+        else:
+            slots[when].append(functools.partial(fold, folded))
+            folded += 1
 
     @pl.when(step < PAIRS)
     def _():
@@ -1615,7 +1654,7 @@
             grads[spot, :] = staged[part]
 
     group = step - PAIRS
-    run_slot(group, slots, 2 * PAIRS, groups)
+    run_slot(group, slots, HEADS, groups, 2)
 
     @pl.when(group >= 0)
     def _():
@@ -1630,6 +1669,7 @@
         def _():
             grad_hidden[...] += added
 
+        run_slot(group, slots, HEADS + 1, groups, 2)
         out_ref[:, :rows] = dot_nt(normed_t_ref[...], grad).astype(jnp.bfloat16)
         for g in range(groups):
 

time: 616 us -> 533 us (0.87)
  Pallas kernels: 576 us -> 493 us
    pallas_call x1, Pallas kernels: 144 us -> 114 us  [forward(): pl.pallas_call(forward_kernel, grid=(groups + PAIRS + regions,), in_specs...]
    pallas_call x1, Pallas kernels: 145 us -> 120 us  [backward(): pl.pallas_call(backward_kernel, grid=(PAIRS + groups,), in_specs=[pl.Bloc...]
    pallas_call x1, Pallas kernels: 97.1 us -> 80.1 us  [tail(): pl.pallas_call(tail_kernel, in_specs=[hbm, pl.BlockSpec(memory_space=pltp...]
    pallas_call x1, Pallas kernels: 79.4 us -> 68.4 us  [head(): pl.pallas_call(head_kernel, in_specs=[vmem, vmem, vmem, hbm, hbm], out_sp...]
where the time goes in v5:
time: 533 us; the launch traced here: 528 us
  Pallas kernels  493 us (92%)
  other arithmetic  13.7 us (3%)
  local copies, waits for them, and re-layouts  11.8 us (2%)
    pallas_call x1, Pallas kernels, backward(): pl.pallas_call(backward_kernel, grid=(PAIRS + groups,), in_specs=[pl.Bloc...  120 us
    pallas_call x1, Pallas kernels, forward(): pl.pallas_call(forward_kernel, grid=(groups + PAIRS + regions,), in_specs...  114 us
    pallas_call x1, Pallas kernels, tail(): pl.pallas_call(tail_kernel, in_specs=[hbm, pl.BlockSpec(memory_space=pltp...  80.1 us
    pallas_call x1, Pallas kernels, mlp_both(): pl.pallas_call(mlp_kernel, grid=(wide // tile,), in_specs=[whole((tokens,...  78.9 us
    pallas_call x1, Pallas kernels, head(): pl.pallas_call(head_kernel, in_specs=[vmem, vmem, vmem, hbm, hbm], out_sp...  68.4 us
    pallas_call x1, Pallas kernels, local_call(): pl.pallas_call(kernel, grid=grid, in_specs=in_specs, out_specs=out_specs,...  19.7 us
    pallas_call x1, Pallas kernels, adam_all(): pl.pallas_call(adam_kernel, in_specs=[smem, smem] + [vmem] * (6 + 15), ou...  11.3 us
  transfers between devices with their start and end apart: 1, of which 0 were waited for; matrix products, arithmetic and copies ran while one was open for 1% of the time, Pallas kernels for 0%

profile of v5, /device:TPU:0, one launch (start us, length us, event | category | flops | bytes accessed | tf_op | source)
XLA Modules:
  0.0 528.2 jit_solution(2753274250137615482)
XLA Ops:
  0.7 1.2 convert.14
  1.9 1.1 convert.12
  3.0 1.0 convert.13
  4.8 3.0 collective-permute-start
  8.4 2.4 multiply_convert_fusion
  10.9 0.8 convert_element_type.39.ada_ref
  11.7 0.8 convert_bitcast_fusion.fc2_ref
  14.9 0.7 pad_maximum_fusion.1.table_ref
  16.9 0.8 pad_maximum_fusion.block_ref
  17.8 68.4 %head.1 = (bf16[1152,4608]{1,0:T(8,128)(2,1)}, f32[8,4,864]{2,1,0:T(4,128)}, f32[8,4,8,288]{3,2,1,0:T(8,128)}, bf16[4,128,1152]{2,1,0:T(8,128)(2,1)}, s32[4,1,128]{2,1,0:T(1,128)}) custom-call(bf16[144,1152]{1,0:T(8,128)(2,1)} %pad_maximum_fusion.block_ref, f32[4,8,288]{2,1,0:T(8,128)} %pad_convert_fusion.cond_ref, ...), custom_call_target="tpu_custom_call" | custom-call | tf_op jit(solution)/shard_map/head/pallas_call | solution.py:810
  86.2 0.9 copy.60
  87.6 1.0 reshape.111.fc1_ref
  88.6 1.5 copy.63.index_t_ref
  90.8 114.1 %forward.1 = (bf16[3456,1024]{1,0:T(8,128)(2,1)}, bf16[1152,1024]{1,0:T(8,128)(2,1)}, f32[16,1,1024]{2,1,0:T(1,128)}, f32[1024,1152]{1,0:T(8,128)}, f32[1024,115...) custom-call(s32[1]{0:T(128)} %dynamic_slice.12.kind_ref, ...), custom_call_target="tpu_custom_call" | custom-call | tf_op jit(solution)/shard_map/forward/pallas_call | solution.py:1525
  204.9 78.9 %mlp_both.1 = (f32[1024,1152]{1,0:T(8,128)}, f32[1024,1152]{1,0:T(8,128)}, bf16[1152,4608]{1,0:T(8,128)(2,1)}, bf16[1152,4608]{1,0:T(8,128)(2,1)}) custom-call(bf16[1024,1152]{1,0:T(8,128)(2,1)} %get-tuple-element.83.h_ref, bf16[1152,1024]{1,0:T(8,128)(2,1)} %get-tuple-element.84.ht_ref, bf16[1024,1152]{1,0:T(8,128)(2,1)} %get-tuple-element.85.g_ref, ...), custom_call_target="tpu_custom_call" | custom-call | tf_op jit(solution)/shard_map/mlp_both/pallas_call | solution.py:466
  283.8 19.7 %after_mlp.1 = (bf16[1024,1152]{1,0:T(8,128)(2,1)}, f32[1024,1152]{1,0:T(8,128)}, bf16[1152,1152]{1,0:T(8,128)(2,1)}, bf16[1152,1024]{1,0:T(8,128)(2,1)}, f32[4,4,1152]{2,1,0:T(4,128)}) custom-call(f32[1024,1152]{1,0:T(8,128)} %get-tuple-element.89.output_ref, f32[1024,1152]{1,0:T(8,128)} %get-tuple-element.90.grad_hidden_ref, ...), custom_call_target="tpu_custom_call" | custom-call | tf_op jit(solution)/shard_map/after_mlp/pallas_call | solution.py:1749
  303.5 120.3 %backward.1 = (bf16[1152,4608]{1,0:T(8,128)(2,1)}, bf16[144,1152]{1,0:T(8,128)(2,1)}, bf16[144,1152]{1,0:T(8,128)(2,1)}, f32[1024,1152]{1,0:T(8,128)}, bf16[4,256,1152]{2,1,0:T(8,128)(2,1)}) custom-call(s32[1]{0:T(128)} %dynamic_slice.12.kind_ref, bf16[3456,1024]{1,0:T(8,128)(2,1)} %get-tuple-element.81.q_ref.k_ref.v_ref, ...), custom_call_target="tpu_custom_call" | custom-call | tf_op jit(solution)/shard_map/backward/pallas_call | solution.py:1701
  423.8 80.1 %tail.1 = (bf16[144,1152]{1,0:T(8,128)(2,1)}, bf16[144,1152]{1,0:T(8,128)(2,1)}, bf16[144,1152]{1,0:T(8,128)(2,1)}, f32[288,864]{1,0:T(8,128)}, f32[8,1152]{1,0:...) custom-call(bf16[1152,4608]{1,0:T(8,128)(2,1)} %get-tuple-element.103.grad_ref, s32[1]{0:T(128)} %dynamic_slice.12.kind_ref, ...), custom_call_target="tpu_custom_call" | custom-call | tf_op jit(solution)/shard_map/tail/pallas_call | solution.py:1169
  503.9 1.2 slice.22
  505.1 1.4 multiply_reduce_fusion.1
  507.8 0.8 multiply_reduce_fusion
  508.6 2.8 convert_element_type.41
  512.1 11.3 %adam_all.1 = (f32[288,432]{1,0:T(8,128)}, f32[144,288]{1,0:T(8,128)}, f32[288,576]{1,0:T(8,128)}, f32[144,1152]{1,0:T(8,128)}, f32[288,864]{1,0:T(8,128)}, /*in...) custom-call(s32[1]{0:T(128)} %bitcast.15.odd_ref, ...), custom_call_target="tpu_custom_call" | custom-call | tf_op jit(solution)/shard_map/adam_all/pallas_call | solution.py:1260
  523.4 3.3 copy.72
  (49 shorter events, 6.2 us)
Async XLA Ops:
  1.8 6.4 %copy-start.6 = (s32[4,4]{1,0:T(4,128)S(1)}, s32[4,4]{1,0:T(4,128)}, u32[]{:S(2)}) copy-start(s32[4,4]{1,0:T(4,128)} %param.29) | copy-start | bytes 196
  1.9 6.5 %copy-start.5 = (s32[4,4]{1,0:T(4,128)S(1)}, s32[4,4]{1,0:T(4,128)}, u32[]{:S(2)}) copy-start(s32[4,4]{1,0:T(4,128)} %param.28) | copy-start | bytes 196
  4.1 6.8 %copy-start = (f32[288,864]{1,0:T(8,128)S(1)}, f32[288,864]{1,0:T(8,128)}, u32[]{:S(2)}) copy-start(f32[288,864]{1,0:T(8,128)} %refs_4_.1) | copy-start | bytes 2985988
  4.6 7.1 %copy-start.1 = (f32[1152,144]{0,1:T(8,128)S(1)}, f32[1152,144]{0,1:T(8,128)}, u32[]{:S(2)}) copy-start(f32[1152,144]{0,1:T(8,128)} %param.36) | copy-start | bytes 1990660
  4.7 7.7 %copy-start.2 = (f32[1152]{0:T(1024)S(1)}, f32[1152]{0:T(1024)}, u32[]{:S(2)}) copy-start(f32[1152]{0:T(1024)} %param.32) | copy-start | bytes 13828
  4.7 8.3 %copy-start.7 = (s32[4]{0:T(128)S(1)}, s32[4]{0:T(128)}, u32[]{:S(2)}) copy-start(s32[4]{0:T(128)} %param.27) | copy-start | bytes 52
  4.8 10.9 %collective-permute-start = (bf16[144,1152]{1,0:T(8,128)(2,1)S(1)}, bf16[144,1152]{1,0:T(8,128)(2,1)S(1)}, u32[]{:S(2)}, u32[]{:S(2)}) collective-permute-start(bf16[144,1152]{1,0:T(8,128)(2,1)S(1)} %get-tuple-element.137), channel_id=1, source_target_pairs={{0,4},{4,0},{8,12},{12,8},{16,20},{20,16},{24,28},{28,24},{1,5},{5... | collective-permute-start | bytes 995336 | tf_op jit(solution)/shard_map/ppermute | solution.py:1855
  503.9 7.6 %copy-start.3 = (f32[1152]{0:T(1024)S(1)}, f32[1152]{0:T(1024)}, u32[]{:S(2)}) copy-start(f32[1152]{0:T(1024)} %param.38) | copy-start | bytes 13828
  503.9 7.6 %copy-start.4 = (f32[1152]{0:T(1024)S(1)}, f32[1152]{0:T(1024)}, u32[]{:S(2)}) copy-start(f32[1152]{0:T(1024)} %param.44) | copy-start | bytes 13828

commit v6 on v5

--- a/solution.py
+++ b/solution.py
@@ -433,14 +433,7 @@
 GELU_B = 0.044715
 
 
-def mlp_kernel(h_ref, ht_ref, g_ref, gt_ref, up_ref, down_ref, out_ref, grad_ref, gup_ref, gdown_ref):
-    step = pl.program_id(0)
-
-    @pl.when(step == 0)
-    def _():
-        out_ref[...] = jnp.zeros_like(out_ref)
-        grad_ref[...] = jnp.zeros_like(grad_ref)
-
+def mlp_tile(h_ref, ht_ref, g_ref, gt_ref, up_ref, down_ref, out_ref, grad_ref, gup_ref, gdown_ref):
     up = up_ref[...]
     down = down_ref[...]
     upward = dot_nn(h_ref[...], up)
@@ -456,34 +449,6 @@
     grad_ref[...] += dot_nt(grad_upward, up)
     gup_ref[...] = dot_nn(ht_ref[...], grad_upward).astype(jnp.bfloat16)
     gdown_ref[...] = dot_nn(gt_ref[...], active).astype(jnp.bfloat16)
-
-
-def mlp_both(hidden, hidden_t, grad, grad_t, up, down_t, tile):
-    tokens, width = hidden.shape
-    wide = up.shape[1]
-    whole = lambda shape: pl.BlockSpec(shape, lambda f: (0, 0))
-    part = pl.BlockSpec((width, tile), lambda f: (0, f))
-    return pl.pallas_call(
-        mlp_kernel,
-        grid=(wide // tile,),
-        in_specs=[
-            whole((tokens, width)),
-            whole((width, tokens)),
-            whole((tokens, width)),
-            whole((width, tokens)),
-            part,
-            part,
-        ],
-        out_specs=[whole((tokens, width)), whole((tokens, width)), part, part],
-        out_shape=[
-            jax.ShapeDtypeStruct((tokens, width), jnp.float32),
-            jax.ShapeDtypeStruct((tokens, width), jnp.float32),
-            jax.ShapeDtypeStruct((width, wide), jnp.bfloat16),
-            jax.ShapeDtypeStruct((width, wide), jnp.bfloat16),
-        ],
-        compiler_params=pltpu.CompilerParams(vmem_limit_bytes=VMEM_LIMIT),
-        name="mlp_both",
-    )(hidden, hidden_t, grad, grad_t, up, down_t)
 
 
 BLOCK_ROWS = 144
@@ -959,7 +924,6 @@
     fc1_ref,
     fc2_ref,
     index_ref,
-    index_t_ref,
     scales_ref,
     sums_ref,
     conds_ref,
@@ -1059,11 +1023,11 @@
         six[1, region : region + 1] = column_sum(grad * normal)
         for k in range(4):
             six[2 + k, region : region + 1] = sums_ref[region, k : k + 1]
-        unfilled = 1.0 - jnp.sum(chosen_rows(index_ref, region), axis=1, keepdims=True)
+        select = chosen_rows(index_ref, region)
+        unfilled = 1.0 - jnp.sum(select, axis=1, keepdims=True)
         masked = column_sum(unfilled * grad_tokens)
-        columns = lax.broadcasted_iota(jnp.int32, (index_t_ref.shape[0], REGION), 1)
-        select = (index_t_ref[...] == columns + region * REGION).astype(jnp.float32)
-        added = dot_nn(select.astype(jnp.bfloat16), grad_tokens.astype(jnp.bfloat16))
+        select = jnp.transpose(select).astype(jnp.bfloat16)
+        added = dot_nn(select, grad_tokens.astype(jnp.bfloat16))
         if region == 0:
             mask_own[...] = jnp.broadcast_to(masked, mask_own.shape)
             kept_total[...] = added
@@ -1168,7 +1132,7 @@
     dma = pltpu.SemaphoreType.DMA
     return pl.pallas_call(
         tail_kernel,
-        in_specs=[hbm, pl.BlockSpec(memory_space=pltpu.SMEM)] + [vmem] * 7 + [hbm] * 3,
+        in_specs=[hbm, pl.BlockSpec(memory_space=pltpu.SMEM)] + [vmem] * 6 + [hbm] * 3,
         out_specs=[vmem] * 6 + [hbm],
         out_shape=[
             block,
@@ -1212,15 +1176,32 @@
         ),
         name="tail",
     )(
-        grad, kind, fc1, fc2, index, index.reshape(places, 1), mod, sums, conds,
+        grad, kind, fc1, fc2, index, mod, sums, conds,
         tokens, grad_middle, grad_hidden,
     )
 
 
-def adam_kernel(odd_ref, factor_ref, own_ref, other_ref, fc1_ref, fc1_other_ref, fc2_ref, ada_ref, *refs):
-    weights, outs = refs[:15], refs[15:]
+def finish_kernel(
+    odd_ref,
+    square_ref,
+    mask_grad_ref,
+    kept_ref,
+    block_ref,
+    own_ref,
+    other_ref,
+    fc1_ref,
+    fc1_other_ref,
+    fc2_ref,
+    ada_ref,
+    *refs,
+):
+    weights, outs = refs[:18], refs[18:36]
+    norm_ref, kept_out, block_out = refs[36:]
     odd = odd_ref[0] == 1
-    factor = factor_ref[0]
+    mask_grad = mask_grad_ref[0:1]
+    norm = jnp.sqrt(square_ref[0:1, 0:1] + square_sum(mask_grad))
+    factor = clip_level / jnp.maximum(norm, clip_level)
+    norm_ref[...] = norm
     qkv = weights[0].shape[1]
     proj = weights[1].shape[0]
     fc1 = weights[2].shape[1]
@@ -1235,9 +1216,9 @@
         )
 
     def step(n, rows, grad):
-        new = adamw(weights[n][rows], weights[5 + n][rows], weights[10 + n][rows], grad * factor)
+        new = adamw(weights[n][rows], weights[6 + n][rows], weights[12 + n][rows], grad * factor)
         for k in range(3):
-            outs[5 * k + n][rows] = new[k]
+            outs[6 * k + n][rows] = new[k]
 
     projs = []
     for k, block in enumerate(pair(own_ref, other_ref)):
@@ -1250,22 +1231,30 @@
         step(2, rows, half(block, 0, fc1))
     step(3, slice(None), fc2_ref[...].astype(jnp.float32))
     step(4, slice(None), ada_ref[...])
-
-
-def adam_all(odd, factor, sums, weights):
-    turn = lambda values: [v.T if n % 5 in (1, 3) else v for n, v in enumerate(values)]
+    step(5, slice(None), mask_grad)
+    kept_out[...] = kept_ref[...].astype(jnp.float32)
+    block_out[...] = block_ref[...]
+
+
+def finish_all(odd, squares, mask_grad, kept, block, sums, weights):
+    turn = lambda values: [v.T if n % 6 in (1, 3) else v for n, v in enumerate(values)]
     weights = turn(weights)
     vmem = pl.BlockSpec(memory_space=pltpu.VMEM)
-    smem = pl.BlockSpec(memory_space=pltpu.SMEM)
-    new = pl.pallas_call(
-        adam_kernel,
-        in_specs=[smem, smem] + [vmem] * (6 + 15),
-        out_specs=[vmem] * 15,
-        out_shape=[jax.ShapeDtypeStruct(w.shape, w.dtype) for w in weights],
+    shape = jax.ShapeDtypeStruct
+    found = pl.pallas_call(
+        finish_kernel,
+        in_specs=[pl.BlockSpec(memory_space=pltpu.SMEM)] + [vmem] * (4 + 6 + 18),
+        out_specs=[vmem] * 21,
+        out_shape=[shape(w.shape, w.dtype) for w in weights]
+        + [
+            shape((1, 1), jnp.float32),
+            shape(kept.shape, jnp.float32),
+            shape(block.shape, block.dtype),
+        ],
         compiler_params=pltpu.CompilerParams(vmem_limit_bytes=VMEM_LIMIT),
-        name="adam_all",
-    )(odd, factor, *sums, *weights)
-    return turn(new)
+        name="finish_all",
+    )(odd, squares, mask_grad, kept, block, *sums, *weights)
+    return turn(found[:18]), *found[18:]
 
 
 def run(actions):
@@ -1745,105 +1734,137 @@
     )(kind, qkv, qkv, qkv, attended, grad_attended, lse, weights, normed_t, grad_proj, *grads, swap)
 
 
-def local_call(kernel, grid, in_specs, out_specs, out_shape, scratch, name, *operands):
-    return pl.pallas_call(
-        kernel,
-        grid=grid,
-        in_specs=in_specs,
-        out_specs=out_specs,
-        out_shape=out_shape,
-        scratch_shapes=scratch,
-        compiler_params=pltpu.CompilerParams(vmem_limit_bytes=VMEM_LIMIT),
-        name=name,
-    )(*operands)
-
-
 def column_sum(values):
     return jnp.sum(values, axis=0, keepdims=True)
 
 
-def after_kernel(
-    output_ref,
-    grad_hidden_ref,
+def mlp_kernel(
+    h_ref,
+    ht_ref,
+    g_ref,
+    gt_ref,
+    up_ref,
+    down_ref,
     middle_ref,
     branch_ref,
     grad_ref,
     attended_ref,
     proj_ref,
     mod_ref,
+    gup_ref,
+    gdown_ref,
     block_ref,
     grad_middle_ref,
     grad_proj_ref,
     grad_attended_ref,
     sums_ref,
+    output_ref,
+    grad_hidden_ref,
     total_ref,
 ):
-    region = pl.program_id(0)
-    part = lambda k: mod_ref[k, pl.ds(region, 1), :]
-    output = output_ref[...]
-    grad_hidden = grad_hidden_ref[...]
-    middle = middle_ref[...]
-    grad = grad_ref[...].astype(jnp.float32)
-    block_ref[...] = (middle + part(GATE_MLP) * output).astype(jnp.bfloat16)
-    normal, root = norm_parts(middle)
-    grad_middle = grad + norm_back(grad_hidden, normal, root, part(SCALE_MLP))
-    grad_middle_ref[...] = grad_middle
-    sums_ref[0, 0:1] = column_sum(grad_middle * branch_ref[...])
-    sums_ref[0, 1:2] = column_sum(grad_hidden)
-    sums_ref[0, 2:3] = column_sum(grad_hidden * normal)
-    sums_ref[0, 3:4] = column_sum(grad * output)
-    grad_branch = (part(GATE_ATTN) * grad_middle).astype(jnp.bfloat16)
-    grad_attended_ref[...] = dot_nt(proj_ref[...], grad_branch).astype(jnp.bfloat16)
-    added = dot_nn(attended_ref[...], grad_branch)
-
-    @pl.when(region == 0)
+    step = pl.program_id(0)
+    regions = mod_ref.shape[1]
+    region = step - (pl.num_programs(0) - regions)
+
+    @pl.when(step == 0)
     def _():
-        total_ref[...] = added
-
-    @pl.when(region > 0)
+        output_ref[...] = jnp.zeros_like(output_ref)
+        grad_hidden_ref[...] = jnp.zeros_like(grad_hidden_ref)
+
+    @pl.when(region < 0)
     def _():
-        total_ref[...] += added
-
-    @pl.when(region == pl.num_programs(0) - 1)
+        mlp_tile(
+            h_ref, ht_ref, g_ref, gt_ref, up_ref, down_ref, output_ref, grad_hidden_ref, gup_ref, gdown_ref
+        )
+
+    @pl.when(region >= 0)
     def _():
-        grad_proj_ref[...] = total_ref[...].astype(jnp.bfloat16)
-
-
-def after_mlp(output, grad_hidden, middle, branch, grad, attended_t, proj, mod):
-    count, width = middle.shape
+        spot = pl.ds(pl.multiple_of(region * REGION, REGION), REGION)
+        part = lambda k: mod_ref[k, pl.ds(region, 1), :]
+        output = output_ref[spot, :]
+        grad_hidden = grad_hidden_ref[spot, :]
+        middle = middle_ref[...]
+        grad = grad_ref[...].astype(jnp.float32)
+        block_ref[...] = (middle + part(GATE_MLP) * output).astype(jnp.bfloat16)
+        normal, root = norm_parts(middle)
+        grad_middle = grad + norm_back(grad_hidden, normal, root, part(SCALE_MLP))
+        grad_middle_ref[...] = grad_middle
+        sums_ref[0, 0:1] = column_sum(grad_middle * branch_ref[...])
+        sums_ref[0, 1:2] = column_sum(grad_hidden)
+        sums_ref[0, 2:3] = column_sum(grad_hidden * normal)
+        sums_ref[0, 3:4] = column_sum(grad * output)
+        grad_branch = (part(GATE_ATTN) * grad_middle).astype(jnp.bfloat16)
+        grad_attended_ref[...] = dot_nt(proj_ref[...], grad_branch).astype(jnp.bfloat16)
+        added = dot_nn(attended_ref[...], grad_branch)
+
+        @pl.when(region == 0)
+        def _():
+            total_ref[...] = added
+
+        @pl.when(region > 0)
+        def _():
+            total_ref[...] += added
+
+        @pl.when(region == regions - 1)
+        def _():
+            grad_proj_ref[...] = total_ref[...].astype(jnp.bfloat16)
+
+
+def mlp_both(hidden, hidden_t, gated, gated_t, up, down_t, middle, branch, grad, attended_t, proj, mod):
+    count, width = hidden.shape
+    wide = up.shape[1]
+    tile = 512
+    tiles = wide // tile
     regions = count // REGION
-    rows = pl.BlockSpec((REGION, width), lambda r: (r, 0))
-    columns = pl.BlockSpec((width, REGION), lambda r: (0, r))
+    region = lambda s: jnp.maximum(s - tiles, 0)
+    rows = pl.BlockSpec((REGION, width), lambda s: (region(s), 0))
+    columns = pl.BlockSpec((width, REGION), lambda s: (0, region(s)))
+    part = pl.BlockSpec((width, tile), lambda s: (0, jnp.minimum(s, tiles - 1)))
     shape = jax.ShapeDtypeStruct
-    return local_call(
-        after_kernel,
-        (regions,),
-        [rows, rows, rows, rows, rows, columns, fixed(width, width), fixed(*mod.shape)],
-        [
+    bf16, f32 = jnp.bfloat16, jnp.float32
+    return pl.pallas_call(
+        mlp_kernel,
+        grid=(tiles + regions,),
+        in_specs=[
+            once(count, width),
+            once(width, count),
+            once(count, width),
+            once(width, count),
+            part,
+            part,
             rows,
             rows,
-            fixed(width, width),
+            rows,
             columns,
-            pl.BlockSpec((1, 4, width), lambda r: (r, 0, 0)),
+            once(width, width),
+            once(*mod.shape),
         ],
-        [
-            shape((count, width), jnp.bfloat16),
-            shape((count, width), jnp.float32),
-            shape((width, width), jnp.bfloat16),
-            shape((width, count), jnp.bfloat16),
-            shape((regions, 4, width), jnp.float32),
+        out_specs=[
+            part,
+            part,
+            rows,
+            rows,
+            once(width, width),
+            columns,
+            pl.BlockSpec((1, 4, width), lambda s: (region(s), 0, 0)),
         ],
-        [pltpu.VMEM((width, width), jnp.float32)],
-        "after_mlp",
-        output,
-        grad_hidden,
-        middle,
-        branch,
-        grad,
-        attended_t,
-        proj,
-        mod,
-    )
+        out_shape=[
+            shape((width, wide), bf16),
+            shape((width, wide), bf16),
+            shape((count, width), bf16),
+            shape((count, width), f32),
+            shape((width, width), bf16),
+            shape((width, count), bf16),
+            shape((regions, 4, width), f32),
+        ],
+        scratch_shapes=[
+            pltpu.VMEM((count, width), f32),
+            pltpu.VMEM((count, width), f32),
+            pltpu.VMEM((width, width), f32),
+        ],
+        compiler_params=pltpu.CompilerParams(vmem_limit_bytes=VMEM_LIMIT),
+        name="mlp_both",
+    )(hidden, hidden_t, gated, gated_t, up, down_t, middle, branch, grad, attended_t, proj, mod)
 
 
 def swap_columns(shard):
@@ -1984,11 +2005,19 @@
         1,
     )
     grad_out = grad_out.reshape(tokens_count, D)
-    output, grad_hidden_mlp, grad_fc1, grad_fc2 = mlp_both(
-        hidden_mlp, hidden_mlp_t, grad_output, grad_output_t, fc1_full, fc2_full, 512
-    )
-    block_slot, grad_middle, grad_proj, grad_attended, sums_mlp = after_mlp(
-        output, grad_hidden_mlp, middle, branch, grad_out, attended_t, proj_full, mod
+    grad_fc1, grad_fc2, block_slot, grad_middle, grad_proj, grad_attended, sums_mlp = mlp_both(
+        hidden_mlp,
+        hidden_mlp_t,
+        grad_output,
+        grad_output_t,
+        fc1_full,
+        fc2_full,
+        middle,
+        branch,
+        grad_out,
+        attended_t,
+        proj_full,
+        mod,
     )
     grad_joined, sum_fc1, sum_fc2, grad_hidden, block_out = backward(
         kind,
@@ -2018,27 +2047,25 @@
         bands,
         3,
     )
-    kept_grad = grad_kept.astype(jnp.float32)
-    grad_mask = grad_mask[0]
-    norm_value = jnp.sqrt(squares[0, 0] + jnp.sum(grad_mask * grad_mask))
-    factor = clip_level / jnp.maximum(norm_value, clip_level)
-    mask_new = adamw(mask_token, mask_first, mask_second, grad_mask * factor)
     odd = (lax.axis_index("dp") % 2).astype(jnp.int32)
-    new = adam_all(
+    new, norm_value, kept_grad, block_out = finish_all(
         odd[None],
-        factor[None],
+        squares,
+        grad_mask,
+        grad_kept,
+        block_out,
         [sum_joined, other_joined, sum_fc1, other_fc1, sum_fc2, red_ada],
         [
-            w_qkv, w_proj, w_fc1, w_fc2, w_ada,
-            first_qkv, first_proj, first_fc1, first_fc2, first_ada,
-            second_qkv, second_proj, second_fc1, second_fc2, second_ada,
+            w_qkv, w_proj, w_fc1, w_fc2, w_ada, mask_token[None],
+            first_qkv, first_proj, first_fc1, first_fc2, first_ada, mask_first[None],
+            second_qkv, second_proj, second_fc1, second_fc2, second_ada, mask_second[None],
         ],
     )
     return (
-        (block_out, kept_grad, norm_value)
-        + (mask_new[0], *new[:5])
-        + (mask_new[1], *new[5:10])
-        + (mask_new[2], *new[10:])
+        (block_out, kept_grad, norm_value[0, 0])
+        + (new[5][0], *new[:5])
+        + (new[11][0], *new[6:11])
+        + (new[17][0], *new[12:17])
     )
 
 

time: 533 us -> 524 us (0.983)
    pallas_call x3 -> x2, Pallas kernels: 110 us -> 110 us  [the longest x1 97 us: mlp_both(): pl.pallas_call(mlp_kernel, grid=(tiles + regions,), in_specs=[once(count,...]
  transfers between devices with their start and end apart: 1 -> 1, of which waited for: 0 -> 0; matrix products, arithmetic and copies ran while one was open for 1% -> 2% of each run, Pallas kernels for 0% -> 0%
where the time goes in v6:
time: 524 us; the launch traced here: 520 us
  Pallas kernels  493 us (94%)
  other arithmetic  12 us (2%)
  local copies, waits for them, and re-layouts  6.99 us (1%)
    pallas_call x1, Pallas kernels, backward(): pl.pallas_call(backward_kernel, grid=(PAIRS + groups,), in_specs=[pl.Bloc...  119 us
    pallas_call x1, Pallas kernels, forward(): pl.pallas_call(forward_kernel, grid=(groups + PAIRS + regions,), in_specs...  113 us
    pallas_call x1, Pallas kernels, mlp_both(): pl.pallas_call(mlp_kernel, grid=(tiles + regions,), in_specs=[once(count,...  97 us
    pallas_call x1, Pallas kernels, tail(): pl.pallas_call(tail_kernel, in_specs=[hbm, pl.BlockSpec(memory_space=pltp...  80.5 us
    pallas_call x1, Pallas kernels, head(): pl.pallas_call(head_kernel, in_specs=[vmem, vmem, vmem, hbm, hbm], out_sp...  69.7 us
    pallas_call x1, Pallas kernels, finish_all(): pl.pallas_call(finish_kernel, in_specs=[pl.BlockSpec(memory_space=pltpu.S...  13.4 us
  transfers between devices with their start and end apart: 1, of which 0 were waited for; matrix products, arithmetic and copies ran while one was open for 2% of the time, Pallas kernels for 0%

profile of v6, /device:TPU:0, one launch (start us, length us, event | category | flops | bytes accessed | tf_op | source)
XLA Modules:
  0.0 519.5 jit_solution(2072462604363399385)
XLA Ops:
  0.7 1.2 convert.14
  1.9 1.1 convert.12
  3.0 1.0 convert.13
  4.7 3.0 collective-permute-start
  8.5 2.4 multiply_convert_fusion
  10.9 0.8 convert_element_type.36.ada_ref
  11.7 0.6 broadcast_in_dim.40.mask_ref.refs_5_
  12.3 0.8 convert_bitcast_fusion.fc2_ref
  13.7 0.6 broadcast_in_dim.45.refs_17_
  15.5 0.6 pad_convert_fusion.cond_ref
  16.2 0.7 pad_maximum_fusion.1.table_ref
  18.2 0.8 pad_maximum_fusion.block_ref
  19.0 69.7 %head.1 = (bf16[1152,4608]{1,0:T(8,128)(2,1)}, f32[8,4,864]{2,1,0:T(4,128)}, f32[8,4,8,288]{3,2,1,0:T(8,128)}, bf16[4,128,1152]{2,1,0:T(8,128)(2,1)}, s32[4,1,128]{2,1,0:T(1,128)}) custom-call(bf16[144,1152]{1,0:T(8,128)(2,1)} %pad_maximum_fusion.block_ref, f32[4,8,288]{2,1,0:T(8,128)} %pad_convert_fusion.cond_ref, ...), custom_call_target="tpu_custom_call" | custom-call | tf_op jit(solution)/shard_map/head/pallas_call | solution.py:775
  88.7 0.9 copy.59
  90.1 1.0 reshape.108.fc1_ref
  91.1 0.7 broadcast_select_fusion.mod_ref.scales_ref
  91.8 113.4 %forward.1 = (bf16[3456,1024]{1,0:T(8,128)(2,1)}, bf16[1152,1024]{1,0:T(8,128)(2,1)}, f32[16,1,1024]{2,1,0:T(1,128)}, f32[1024,1152]{1,0:T(8,128)}, f32[1024,115...) custom-call(s32[1]{0:T(128)} %dynamic_slice.12.kind_ref, ...), custom_call_target="tpu_custom_call" | custom-call | tf_op jit(solution)/shard_map/forward/pallas_call | solution.py:1514
  205.2 97.0 %mlp_both.1 = (bf16[1152,4608]{1,0:T(8,128)(2,1)}, bf16[1152,4608]{1,0:T(8,128)(2,1)}, bf16[1024,1152]{1,0:T(8,128)(2,1)}, f32[1024,1152]{1,0:T(8,128)}, bf16[11...) custom-call(bf16[1024,1152]{1,0:T(8,128)(2,1)} %get-tuple-element.87.h_ref, ...), custom_call_target="tpu_custom_call" | custom-call | tf_op jit(solution)/shard_map/mlp_both/pallas_call | solution.py:1825
  302.2 119.1 %backward.1 = (bf16[1152,4608]{1,0:T(8,128)(2,1)}, bf16[144,1152]{1,0:T(8,128)(2,1)}, bf16[144,1152]{1,0:T(8,128)(2,1)}, f32[1024,1152]{1,0:T(8,128)}, bf16[4,256,1152]{2,1,0:T(8,128)(2,1)}) custom-call(s32[1]{0:T(128)} %dynamic_slice.12.kind_ref, bf16[3456,1024]{1,0:T(8,128)(2,1)} %get-tuple-element.85.q_ref.k_ref.v_ref, ...), custom_call_target="tpu_custom_call" | custom-call | tf_op jit(solution)/shard_map/backward/pallas_call | solution.py:1690
  421.3 80.5 %tail.1 = (bf16[144,1152]{1,0:T(8,128)(2,1)}, bf16[144,1152]{1,0:T(8,128)(2,1)}, bf16[144,1152]{1,0:T(8,128)(2,1)}, f32[288,864]{1,0:T(8,128)}, f32[8,1152]{1,0:...) custom-call(bf16[1152,4608]{1,0:T(8,128)(2,1)} %get-tuple-element.104.grad_ref, s32[1]{0:T(128)} %dynamic_slice.12.kind_ref, ...), custom_call_target="tpu_custom_call" | custom-call | tf_op jit(solution)/shard_map/tail/pallas_call | solution.py:1133
  501.8 13.4 %finish_all.1 = (f32[288,432]{1,0:T(8,128)}, f32[144,288]{1,0:T(8,128)}, f32[288,576]{1,0:T(8,128)}, f32[144,1152]{1,0:T(8,128)}, f32[288,864]{1,0:T(8,128)}, /*...) custom-call(s32[1]{0:T(128)} %bitcast.odd_ref, ...), custom_call_target="tpu_custom_call" | custom-call | tf_op jit(solution)/shard_map/finish_all/pallas_call | solution.py:1244
  515.2 1.3 reduce
  516.5 1.3 reduce.1
  517.8 1.3 reduce.2
  (46 shorter events, 4.3 us)
Async XLA Ops:
  1.8 6.4 %copy-start.6 = (s32[4,4]{1,0:T(4,128)S(1)}, s32[4,4]{1,0:T(4,128)}, u32[]{:S(2)}) copy-start(s32[4,4]{1,0:T(4,128)} %param.29) | copy-start | bytes 196
  1.9 6.5 %copy-start.5 = (s32[4,4]{1,0:T(4,128)S(1)}, s32[4,4]{1,0:T(4,128)}, u32[]{:S(2)}) copy-start(s32[4,4]{1,0:T(4,128)} %param.28) | copy-start | bytes 196
  4.1 6.8 %copy-start = (f32[288,864]{1,0:T(8,128)S(1)}, f32[288,864]{1,0:T(8,128)}, u32[]{:S(2)}) copy-start(f32[288,864]{1,0:T(8,128)} %refs_4_.1) | copy-start | bytes 2985988
  4.6 7.1 %copy-start.2 = (f32[1152]{0:T(1024)S(1)}, f32[1152]{0:T(1024)}, u32[]{:S(2)}) copy-start(f32[1152]{0:T(1024)} %param.32) | copy-start | bytes 13828
  4.6 7.7 %copy-start.1 = (f32[1152,144]{0,1:T(8,128)S(1)}, f32[1152,144]{0,1:T(8,128)}, u32[]{:S(2)}) copy-start(f32[1152,144]{0,1:T(8,128)} %param.36) | copy-start | bytes 1990660
  4.7 12.2 %collective-permute-start = (bf16[144,1152]{1,0:T(8,128)(2,1)S(1)}, bf16[144,1152]{1,0:T(8,128)(2,1)S(1)}, u32[]{:S(2)}, u32[]{:S(2)}) collective-permute-start(bf16[144,1152]{1,0:T(8,128)(2,1)S(1)} %get-tuple-element.142), channel_id=1, source_target_pairs={{0,4},{4,0},{8,12},{12,8},{16,20},{20,16},{24,28},{28,24},{1,5},{5... | collective-permute-start | bytes 995336 | tf_op jit(solution)/shard_map/ppermute | solution.py:1876
  8.0 5.1 copy-start.3
  8.0 5.7 %copy-start.4 = (f32[1152]{0:T(1024)S(1)}, f32[1152]{0:T(1024)}, u32[]{:S(2)}) copy-start(f32[1152]{0:T(1024)} %param.44) | copy-start | bytes 13828
  8.0 6.3 %copy-start.7 = (s32[4]{0:T(128)S(1)}, s32[4]{0:T(128)}, u32[]{:S(2)}) copy-start(s32[4]{0:T(128)} %param.27) | copy-start | bytes 52

commit v7 on v6

--- a/solution.py
+++ b/solution.py
@@ -964,10 +964,10 @@
     *rest,
 ):
     place = Place()
-    plans = ((False, (0,)),)
+    plans = ((False, (2,)),)
     order = [
-        (3, 1, 1), (0, 1, 1), (3, 0, 1), (1, 0, 0), (1, 1, 0), (2, 1, 1), (3, 1, 0), (3, 0, 0),
-        (1, 1, 1), (2, 0, 1), (1, 0, 1), (2, 1, 0), (0, 0, 1), (0, 0, 0), (0, 1, 0), (2, 0, 0),
+        (2, 1, 1), (3, 1, 1), (3, 1, 0), (1, 0, 0), (1, 1, 0), (2, 0, 1), (3, 0, 1), (1, 1, 1),
+        (3, 0, 0), (2, 0, 0), (1, 0, 1), (2, 1, 0), (0, 1, 0), (0, 1, 1), (0, 0, 0), (0, 0, 1),
     ]
     begin, fold, combine, finish = scatter_actions(
         place, plans, [(0,) + piece for piece in order], [grad_ref], [own_ref], *rest[:7]
@@ -1002,7 +1002,7 @@
     begin()
     fc1_copy = across(0, fc1_ref, fc1_other_ref)
     fc1_copy.start()
-    folds(4)
+    folds(6)
     for copy in loads:
         copy.wait()
 
@@ -1010,10 +1010,9 @@
     regions = count // REGION
     for region in range(regions):
         if region == 2:
+            folds(1)
+        if region == 3:
             combine(0, 3, 0, 1)
-        folds((0, 2, 2, 2)[region])
-        if region == 3:
-            combine(0, 2, 0, 1)
         spot = slice(region * REGION, (region + 1) * REGION)
         grad = grad_hidden[spot]
         normal, root = norm_parts(tokens[spot])
@@ -1053,23 +1052,26 @@
     early += [to_band(0, n, mask_own, mask_band.at[n]) for n in range(3)]
     for copy in early:
         copy.start()
+    mods_dp[own] = mods_own[own]
+    folds(2)
     kept_start()
-    mods_dp[own] = mods_own[own]
     combine(0, 3, 0, 0)
-    folds(5)
-    combine(0, 1, 0, 1)
-    folds(1)
     for copy in early:
         copy.wait()
+    folds(4)
+    combine(0, 2, 1, 0)
+    folds(1)
     mask_sum[...] = mask_own[...] + mask_band[0] + mask_band[1] + mask_band[2]
     second = [to_band(1, n, mods_dp, mods_all.at[place.band()]) for n in range(3)]
     second += [to_dp(1, n, mask_sum, mask_dp.at[n]) for n in range(7)]
     for copy in second:
         copy.start()
     mods_all[place.band()] = mods_dp[...]
+    combine(0, 0, 1, 0)
+    combine(0, 1, 0, 1)
+    combine(0, 2, 0, 0)
+    folds(2)
     fc1_copy.wait()
-    combine(0, 2, 0, 0)
-    combine(0, 0, 1, 0)
     combine(0, 0, 0, 1)
     for copy in second:
         copy.wait()

time: 524 us -> 520 us (level)
  no operation moved by 1% of the time
where the time goes in v7:
time: 520 us; the launch traced here: 516 us
  Pallas kernels  489 us (94%)
  other arithmetic  12 us (2%)
  local copies, waits for them, and re-layouts  6.99 us (1%)
    pallas_call x1, Pallas kernels, backward(): pl.pallas_call(backward_kernel, grid=(PAIRS + groups,), in_specs=[pl.Bloc...  119 us
    pallas_call x1, Pallas kernels, forward(): pl.pallas_call(forward_kernel, grid=(groups + PAIRS + regions,), in_specs...  113 us
    pallas_call x1, Pallas kernels, mlp_both(): pl.pallas_call(mlp_kernel, grid=(tiles + regions,), in_specs=[once(count,...  97 us
    pallas_call x1, Pallas kernels, tail(): pl.pallas_call(tail_kernel, in_specs=[hbm, pl.BlockSpec(memory_space=pltp...  76.5 us
    pallas_call x1, Pallas kernels, head(): pl.pallas_call(head_kernel, in_specs=[vmem, vmem, vmem, hbm, hbm], out_sp...  69.7 us
    pallas_call x1, Pallas kernels, finish_all(): pl.pallas_call(finish_kernel, in_specs=[pl.BlockSpec(memory_space=pltpu.S...  13.4 us
  transfers between devices with their start and end apart: 1, of which 0 were waited for; matrix products, arithmetic and copies ran while one was open for 2% of the time, Pallas kernels for 0%

profile of v7, /device:TPU:0, one launch (start us, length us, event | category | flops | bytes accessed | tf_op | source)
XLA Modules:
  0.0 515.5 jit_solution(18413949671588321664)
XLA Ops:
  0.7 1.2 convert.14
  1.9 1.1 convert.12
  3.0 1.0 convert.13
  4.7 3.0 collective-permute-start
  8.5 2.4 multiply_convert_fusion
  10.9 0.8 convert_element_type.36.ada_ref
  11.7 0.6 broadcast_in_dim.40.mask_ref.refs_5_
  12.3 0.8 convert_bitcast_fusion.fc2_ref
  13.1 0.6 broadcast_in_dim.44.refs_11_
  15.5 0.6 pad_convert_fusion.cond_ref
  16.2 0.7 pad_maximum_fusion.1.table_ref
  18.2 0.8 pad_maximum_fusion.block_ref
  19.0 69.7 %head.1 = (bf16[1152,4608]{1,0:T(8,128)(2,1)}, f32[8,4,864]{2,1,0:T(4,128)}, f32[8,4,8,288]{3,2,1,0:T(8,128)}, bf16[4,128,1152]{2,1,0:T(8,128)(2,1)}, s32[4,1,128]{2,1,0:T(1,128)}) custom-call(bf16[144,1152]{1,0:T(8,128)(2,1)} %pad_maximum_fusion.block_ref, f32[4,8,288]{2,1,0:T(8,128)} %pad_convert_fusion.cond_ref, ...), custom_call_target="tpu_custom_call" | custom-call | tf_op jit(solution)/shard_map/head/pallas_call | solution.py:775
  88.7 0.9 copy.59
  90.1 1.0 reshape.108.fc1_ref
  91.1 0.7 broadcast_select_fusion.mod_ref.scales_ref
  91.8 113.4 %forward.1 = (bf16[3456,1024]{1,0:T(8,128)(2,1)}, bf16[1152,1024]{1,0:T(8,128)(2,1)}, f32[16,1,1024]{2,1,0:T(1,128)}, f32[1024,1152]{1,0:T(8,128)}, f32[1024,115...) custom-call(s32[1]{0:T(128)} %dynamic_slice.12.kind_ref, ...), custom_call_target="tpu_custom_call" | custom-call | tf_op jit(solution)/shard_map/forward/pallas_call | solution.py:1516
  205.2 97.0 %mlp_both.1 = (bf16[1152,4608]{1,0:T(8,128)(2,1)}, bf16[1152,4608]{1,0:T(8,128)(2,1)}, bf16[1024,1152]{1,0:T(8,128)(2,1)}, f32[1024,1152]{1,0:T(8,128)}, bf16[11...) custom-call(bf16[1024,1152]{1,0:T(8,128)(2,1)} %get-tuple-element.87.h_ref, ...), custom_call_target="tpu_custom_call" | custom-call | tf_op jit(solution)/shard_map/mlp_both/pallas_call | solution.py:1827
  302.2 119.1 %backward.1 = (bf16[1152,4608]{1,0:T(8,128)(2,1)}, bf16[144,1152]{1,0:T(8,128)(2,1)}, bf16[144,1152]{1,0:T(8,128)(2,1)}, f32[1024,1152]{1,0:T(8,128)}, bf16[4,256,1152]{2,1,0:T(8,128)(2,1)}) custom-call(s32[1]{0:T(128)} %dynamic_slice.12.kind_ref, bf16[3456,1024]{1,0:T(8,128)(2,1)} %get-tuple-element.85.q_ref.k_ref.v_ref, ...), custom_call_target="tpu_custom_call" | custom-call | tf_op jit(solution)/shard_map/backward/pallas_call | solution.py:1692
  421.3 76.5 %tail.1 = (bf16[144,1152]{1,0:T(8,128)(2,1)}, bf16[144,1152]{1,0:T(8,128)(2,1)}, bf16[144,1152]{1,0:T(8,128)(2,1)}, f32[288,864]{1,0:T(8,128)}, f32[8,1152]{1,0:...) custom-call(bf16[1152,4608]{1,0:T(8,128)(2,1)} %get-tuple-element.104.grad_ref, s32[1]{0:T(128)} %dynamic_slice.12.kind_ref, ...), custom_call_target="tpu_custom_call" | custom-call | tf_op jit(solution)/shard_map/tail/pallas_call | solution.py:1135
  497.8 13.4 %finish_all.1 = (f32[288,432]{1,0:T(8,128)}, f32[144,288]{1,0:T(8,128)}, f32[288,576]{1,0:T(8,128)}, f32[144,1152]{1,0:T(8,128)}, f32[288,864]{1,0:T(8,128)}, /*...) custom-call(s32[1]{0:T(128)} %bitcast.odd_ref, ...), custom_call_target="tpu_custom_call" | custom-call | tf_op jit(solution)/shard_map/finish_all/pallas_call | solution.py:1246
  511.2 1.3 reduce
  512.5 1.3 reduce.1
  513.8 1.3 reduce.2
  (46 shorter events, 4.3 us)
Async XLA Ops:
  1.8 6.4 %copy-start.6 = (s32[4,4]{1,0:T(4,128)S(1)}, s32[4,4]{1,0:T(4,128)}, u32[]{:S(2)}) copy-start(s32[4,4]{1,0:T(4,128)} %param.29) | copy-start | bytes 196
  1.9 6.5 %copy-start.5 = (s32[4,4]{1,0:T(4,128)S(1)}, s32[4,4]{1,0:T(4,128)}, u32[]{:S(2)}) copy-start(s32[4,4]{1,0:T(4,128)} %param.28) | copy-start | bytes 196
  4.1 6.8 %copy-start = (f32[288,864]{1,0:T(8,128)S(1)}, f32[288,864]{1,0:T(8,128)}, u32[]{:S(2)}) copy-start(f32[288,864]{1,0:T(8,128)} %refs_4_.1) | copy-start | bytes 2985988
  4.6 7.1 %copy-start.2 = (f32[1152]{0:T(1024)S(1)}, f32[1152]{0:T(1024)}, u32[]{:S(2)}) copy-start(f32[1152]{0:T(1024)} %param.32) | copy-start | bytes 13828
  4.6 7.7 %copy-start.1 = (f32[1152,144]{0,1:T(8,128)S(1)}, f32[1152,144]{0,1:T(8,128)}, u32[]{:S(2)}) copy-start(f32[1152,144]{0,1:T(8,128)} %param.36) | copy-start | bytes 1990660
  4.7 12.2 %collective-permute-start = (bf16[144,1152]{1,0:T(8,128)(2,1)S(1)}, bf16[144,1152]{1,0:T(8,128)(2,1)S(1)}, u32[]{:S(2)}, u32[]{:S(2)}) collective-permute-start(bf16[144,1152]{1,0:T(8,128)(2,1)S(1)} %get-tuple-element.142), channel_id=1, source_target_pairs={{0,4},{4,0},{8,12},{12,8},{16,20},{20,16},{24,28},{28,24},{1,5},{5... | collective-permute-start | bytes 995336 | tf_op jit(solution)/shard_map/ppermute | solution.py:1878
  8.0 5.1 copy-start.3
  8.0 5.7 %copy-start.4 = (f32[1152]{0:T(1024)S(1)}, f32[1152]{0:T(1024)}, u32[]{:S(2)}) copy-start(f32[1152]{0:T(1024)} %param.44) | copy-start | bytes 13828
  8.0 6.3 %copy-start.7 = (s32[4]{0:T(128)S(1)}, s32[4]{0:T(128)}, u32[]{:S(2)}) copy-start(s32[4]{0:T(128)} %param.27) | copy-start | bytes 52
